TPU v7x, 256 devices: a whole 4x4x8 slice. The times are simulated.
256 devices in a mesh: dp: 32 (over z, x), head: 8 (over y, core).
Axes of the slice: x: 4, y: 4, z: 8, core: 2. Of those that a mesh axis runs over, the one named last changes fastest.
Arguments:
- query_in: bfloat16 [32, 1024, 4096], P(None, 'dp', 'head'), may hold values from -36 to 36
- key_in: bfloat16 [32, 1024, 1024], P(None, 'dp', 'head'), may hold values from -36 to 36
- value_input: bfloat16 [32, 1024, 1024], P(None, 'dp', 'head'), may hold values from -6 to 6
- grad_out: bfloat16 [32, 1024, 4096], P(None, 'dp', 'head'), may hold values from -16 to 16
- q_gain: float32 [128], replicated, may hold values from 0.5 to 7
- k_gain: float32 [128], replicated, may hold values from 0.5 to 7
- lengths: int32 [32], replicated, may hold values from 512 to 1024
- owners: int32 [32], replicated, may hold values from 0 to 31, as said below
- doc_ids: int32 [32, 1024], replicated, may hold values from 0 to 7, never falling along the last dimension, each value on 1 to 512 neighbouring positions
Outputs:
- attention: bfloat16 [32, 1024, 4096], P('dp', 'head')
- query_gradient_packed: bfloat16 [32, 1024, 4096], P('dp', 'head')
- key_gradient_packed: bfloat16 [32, 1024, 1024], P('dp', 'head')
- value_grad: bfloat16 [32, 1024, 1024], P('dp', 'head')
- q_gain_grad: float32 [128], replicated
- key_gain_gradient: float32 [128], replicated
Inputs may be any that keep to these rules, and one draw needn't show every extreme that they name: `owners`: each of the 32 data shards owns exactly 1 sequence.
All inputs are finite; a program needn't handle non-finite values.
Results may differ from a plain program's by a relative error of at most 0.0075.
The roundings to bfloat16 on the way count: a program that leaves them out, or rounds other values in their place, can miss the bound.
Values may be sent and summed in bfloat16 or wider, within the bound.
No kernel may reach another device: no remote copies, remote signals or barrier semaphores. Data moves between devices by JAX's collectives and lax.ppermute only.
A program may use at most 64 MiB of HBM per device.

v0:
```python
import math

import jax
import jax.numpy as jnp
from jax import lax
from jax.sharding import PartitionSpec as P

HEAD_WIDTH = 128


EPSILON = 1e-06
NEG_FILL = -1e30


def apply_rms_norm(values):
    inverse = lax.rsqrt(jnp.mean(values * values, axis=-1, keepdims=True) + EPSILON)
    return (values * inverse, inverse)


def unnormalize(grad_normed, gain_vec, normed, inverse):
    grad_hat = grad_normed * gain_vec
    inner_mean = jnp.mean(grad_hat * normed, axis=-1, keepdims=True)
    return inverse * (grad_hat - normed * inner_mean)


def allowed_pairs(doc_row, live_len):
    positions = jnp.arange(doc_row.shape[0], dtype=jnp.int32)
    same_doc = doc_row[:, None] == doc_row[None, :]
    causal = positions[None, :] <= positions[:, None]
    alive_pos = positions < live_len
    return same_doc & causal & alive_pos[:, None] & alive_pos[None, :]


def probabilities(query_head, key_head, allowed):
    score_scale = 1.0 / math.sqrt(query_head.shape[-1])
    scores = jnp.dot(query_head, key_head.T, preferred_element_type=jnp.float32) * score_scale
    scores = jnp.where(allowed, scores, NEG_FILL)
    largest = jnp.max(scores, axis=1, keepdims=True)
    weights = jnp.where(allowed, jnp.exp(scores - largest), 0.0)
    row_total = jnp.maximum(jnp.sum(weights, axis=1, keepdims=True), 1.0)
    return weights / row_total


def backward_from(
    query_head, key_head, value_head, grad_head, weights_norm, weights_low, attention_output
):
    score_scale = 1.0 / math.sqrt(query_head.shape[-1])
    grad_probs = jnp.dot(grad_head, value_head.T, preferred_element_type=jnp.float32)
    row_delta = jnp.sum(grad_head.astype(jnp.float32) * attention_output, axis=1, keepdims=True)
    grad_scores = (weights_norm * (grad_probs - row_delta)).astype(jnp.bfloat16)
    grad_query = jnp.dot(grad_scores, key_head, preferred_element_type=jnp.float32) * score_scale
    grad_key = jnp.dot(grad_scores.T, query_head, preferred_element_type=jnp.float32) * score_scale
    grad_value = jnp.dot(weights_low.T, grad_head, preferred_element_type=jnp.float32)
    return (grad_query, grad_key, grad_value)


def heads_to_rows(stacked, seq_dev, heads):
    grouped = stacked.reshape(seq_dev, heads, stacked.shape[1], stacked.shape[2])
    return jnp.transpose(grouped, (0, 2, 1, 3))


def group_sum(stacked, seq_dev, kv_heads, group_width):
    grouped = stacked.reshape(seq_dev, kv_heads, group_width, stacked.shape[1], stacked.shape[2])
    return jnp.transpose(jnp.sum(grouped, axis=2), (0, 2, 1, 3))


def per_device(query_in, key_in, value_input, grad_out, q_gain, k_gain, lengths, owners, doc_ids):
    dp_count = lax.axis_size("dp")
    head_count = lax.axis_size("head")
    total_seqs = owners.shape[0]
    seq_dev = total_seqs // dp_count
    packed_order = jnp.argsort(owners, stable=True)
    my_rows = lax.dynamic_slice_in_dim(packed_order, lax.axis_index("dp") * seq_dev, seq_dev)
    live_lens = jnp.take(lengths, my_rows)
    doc_rows = jnp.take(doc_ids, my_rows, axis=0)
    sorted_query = jnp.take(query_in, packed_order, axis=0)
    sorted_key = jnp.take(key_in, packed_order, axis=0)
    sorted_value = jnp.take(value_input, packed_order, axis=0)
    sorted_grad = jnp.take(grad_out, packed_order, axis=0)
    query_mine, key_mine, value_mine, grad_mine = (
        lax.all_to_all(sorted_query, "dp", split_axis=0, concat_axis=1, tiled=True),
        lax.all_to_all(sorted_key, "dp", split_axis=0, concat_axis=1, tiled=True),
        lax.all_to_all(sorted_value, "dp", split_axis=0, concat_axis=1, tiled=True),
        lax.all_to_all(sorted_grad, "dp", split_axis=0, concat_axis=1, tiled=True),
    )
    slot_width = query_mine.shape[1]
    q_heads = query_mine.shape[2] // HEAD_WIDTH
    kv_heads = key_mine.shape[2] // HEAD_WIDTH
    group_width = q_heads // kv_heads
    q_hat, q_inv = apply_rms_norm(
        query_mine.astype(jnp.float32).reshape(seq_dev, slot_width, q_heads, HEAD_WIDTH)
    )
    key_unit_rows, key_inverse_norm = apply_rms_norm(
        key_mine.astype(jnp.float32).reshape(seq_dev, slot_width, kv_heads, HEAD_WIDTH)
    )
    q_normed = (q_hat * q_gain).astype(jnp.bfloat16)
    k_normed = (key_unit_rows * k_gain).astype(jnp.bfloat16)
    value_head_rows = value_mine.reshape(seq_dev, slot_width, kv_heads, HEAD_WIDTH)
    item_ids = jnp.arange(seq_dev * q_heads, dtype=jnp.int32)

    def pieces(item_idx):
        seq_idx = item_idx // q_heads
        head_idx = item_idx % q_heads
        kv_idx = head_idx // group_width
        allowed = allowed_pairs(doc_rows[seq_idx], live_lens[seq_idx])
        return (
            seq_idx,
            head_idx,
            q_normed[seq_idx, :, head_idx],
            k_normed[seq_idx, :, kv_idx],
            value_head_rows[seq_idx, :, kv_idx],
            allowed,
        )

    grad_heads = grad_mine.reshape(seq_dev, slot_width, q_heads, HEAD_WIDTH)

    def joined_item(item_idx):
        seq_idx, head_idx, query_head, key_head, value_head, allowed = pieces(item_idx)
        weights_norm = probabilities(query_head, key_head, allowed)
        weights_low = weights_norm.astype(jnp.bfloat16)
        attention_output = jnp.dot(weights_low, value_head, preferred_element_type=jnp.float32)
        grads = backward_from(
            query_head,
            key_head,
            value_head,
            grad_heads[seq_idx, :, head_idx],
            weights_norm,
            weights_low,
            attention_output,
        )
        return (attention_output,) + grads

    output_items, grad_qn_items, grad_kn_items, grad_v_items = lax.map(joined_item, item_ids)
    attention_local = (
        heads_to_rows(output_items, seq_dev, q_heads)
        .reshape(seq_dev, slot_width, q_heads * HEAD_WIDTH)
        .astype(jnp.bfloat16)
    )
    grad_qn = heads_to_rows(grad_qn_items, seq_dev, q_heads)
    normed_key_gradient = group_sum(grad_kn_items, seq_dev, kv_heads, group_width)
    value_head_gradient = group_sum(grad_v_items, seq_dev, kv_heads, group_width)
    query_gradient_packed = unnormalize(grad_qn, q_gain, q_hat, q_inv).astype(jnp.bfloat16)
    key_gradient_packed = unnormalize(
        normed_key_gradient, k_gain, key_unit_rows, key_inverse_norm
    ).astype(jnp.bfloat16)
    value_grad = value_head_gradient.astype(jnp.bfloat16)
    query_correction = jnp.sum(grad_qn * q_hat, axis=(0, 1, 2))
    key_correction = jnp.sum(normed_key_gradient * key_unit_rows, axis=(0, 1, 2))
    query_local, key_local, value_local, query_correction, key_correction = (
        query_gradient_packed.reshape(seq_dev, slot_width, q_heads * HEAD_WIDTH),
        key_gradient_packed.reshape(seq_dev, slot_width, kv_heads * HEAD_WIDTH),
        value_grad.reshape(seq_dev, slot_width, kv_heads * HEAD_WIDTH),
        query_correction,
        key_correction,
    )
    attention, query_gradient_packed, key_gradient_packed, value_grad = (
        lax.all_to_all(attention_local, "head", split_axis=1, concat_axis=2, tiled=True),
        lax.all_to_all(query_local, "head", split_axis=1, concat_axis=2, tiled=True),
        lax.all_to_all(key_local, "head", split_axis=1, concat_axis=2, tiled=True),
        lax.all_to_all(value_local, "head", split_axis=1, concat_axis=2, tiled=True),
    )
    q_sum, k_sum = lax.psum((query_correction, key_correction), ("dp", "head"))
    tokens_all = total_seqs * slot_width
    q_gain_grad = q_sum / math.sqrt(tokens_all * q_heads * head_count)
    key_gain_gradient = k_sum / math.sqrt(tokens_all * kv_heads * head_count)
    return (
        attention,
        query_gradient_packed,
        key_gradient_packed,
        value_grad,
        q_gain_grad,
        key_gain_gradient,
    )


def solution(mesh):
    in_specs = (
        P(None, "dp", "head"),
        P(None, "dp", "head"),
        P(None, "dp", "head"),
        P(None, "dp", "head"),
        P(),
        P(),
        P(),
        P(),
        P(),
    )
    out_specs = (
        P("dp", "head", None),
        P("dp", "head", None),
        P("dp", "head", None),
        P("dp", "head", None),
        P(),
        P(),
    )
    return jax.shard_map(
        per_device, mesh=mesh, in_specs=in_specs, out_specs=out_specs, check_vma=False
    )
```

profile of v0, /device:TPU:1, one launch (start us, length us, event | category | flops | bytes accessed | tf_op | source)
XLA Modules:
  0.0 460.4 jit_solution(9139691111928165976)
XLA Ops:
  0.7 2.3 sort.17
  7.0 11.9 %all-to-all-start.1 = ((bf16[32,32,128]{2,1,0:T(8,128)(2,1)}), bf16[32,32,128]{2,1,0:T(8,128)(2,1)S(1)}, u32[]{:S(2)}, u32[]{:S(2)}) async-start(bf16[32,32,128]{2,1,0:T(8,128)(2,1)} %get-tuple-element.304), calls=%async_computation.1 | async-start | bytes 524288 | tf_op jit(solution)/shard_map/all_to_all | solution.py:82
  19.6 1.8 gather_fusion.3
  23.0 7.1 %all-to-all-done.1 = bf16[32,32,128]{2,1,0:T(8,128)(2,1)S(1)} async-done(((bf16[32,32,128]{2,1,0:T(8,128)(2,1)}), bf16[32,32,128]{2,1,0:T(8,128)(2,1)S(1)}, u32[]{:S(2)}, u32[]{:S(2)}) %all-to-all-start.1) | async-done | bytes 262176 | tf_op jit(solution)/shard_map/all_to_all | solution.py:82
  30.1 29.8 %all_to_all.108 = bf16[32,32,512]{2,1,0:T(8,128)(2,1)} all-to-all(bf16[32,32,512]{2,1,0:T(8,128)(2,1)} %get-tuple-element.302), channel_id=1, replica_groups=mesh['dp'=32,'head'=8] {'dp'}, dimensions={0} | all-to-all | bytes 2097152 | tf_op jit(solution)/shard_map/all_to_all | solution.py:81
  59.9 7.3 %all-to-all-start.3 = ((bf16[32,32,512]{2,1,0:T(8,128)(2,1)}), bf16[32,32,512]{2,1,0:T(8,128)(2,1)}, u32[]{:S(2)}, u32[]{:S(2)}) async-start(bf16[32,32,512]{2,1,0:T(8,128)(2,1)} %get-tuple-element.301), calls=%async_computation.3 | async-start | bytes 2097152 | tf_op jit(solution)/shard_map/all_to_all | solution.py:84
  73.7 1.7 reshape.542
  75.4 2.0 multiply_reduce_fusion.2
  77.4 14.2 %all-to-all-done.3 = bf16[32,32,512]{2,1,0:T(8,128)(2,1)} async-done(((bf16[32,32,512]{2,1,0:T(8,128)(2,1)}), bf16[32,32,512]{2,1,0:T(8,128)(2,1)}, u32[]{:S(2)}, u32[]{:S(2)}) %all-to-all-start.3) | async-done | bytes 1048608 | tf_op jit(solution)/shard_map/all_to_all | solution.py:84
  91.6 7.8 %all-to-all-start.2 = ((bf16[32,32,128]{2,1,0:T(8,128)(2,1)}), bf16[32,32,128]{2,1,0:T(8,128)(2,1)}, u32[]{:S(2)}, u32[]{:S(2)}) async-start(bf16[32,32,128]{2,1,0:T(8,128)(2,1)} %get-tuple-element.303), calls=%async_computation.2 | async-start | bytes 524288 | tf_op jit(solution)/shard_map/all_to_all | solution.py:83
  101.3 2.4 multiply_convert_fusion.2
  104.8 2.1 reshape.500
  107.0 2.4 copy.72
  109.9 147.8 %while.20 = (s32[]{:T(128)}, bf16[4,1024,128]{1,2,0:T(8,128)(2,1)}, f32[4,1024,128]{2,0,1:T(4,128)}, f32[4,1024,128]{2,1,0:T(8,128)}, f32[4,1024,128]{2,1,0:T(8,...) while((s32[]{:T(128)}, bf16[4,1024,128]{1,2,0:T(8,128)(2,1)}, ...), condition=%wide.region_7.10_spmd, body=%wide.region_3.0_spmd.sunk | while | flops 1666841600 | bytes 42306952 | solution.py:133
  112.4 1.9 fusion.55
  114.4 2.3 fusion.56
  116.7 4.5 fusion.58
  121.3 2.4 bitcast_dynamic-update-slice_fusion.2
  125.7 2.7 multiply_convert_fusion.6
  129.9 14.4 %dynamic_update_slice.35 = f32[4,1024,128]{2,0,1:T(4,128)} dynamic-update-slice(f32[4,1024,128]{2,0,1:T(4,128)} %get-tuple-element.406, f32[1,1024,128]{2,0,1:T(1,128)} %bitcast.136, s32[]{:T(128)} %get-tuple-element.404, s32[]{:T(128)} %constant.146.clone.1..sunk, s32[]{:T(128)} %constant.146.clone.1..sunk) | dynamic-update-slice | bytes 1048580 | tf_op jit(solution)/shard_map/while/body/jit(dynamic_update_index_in_dim)/dynamic_update_slice | solution.py:133
  144.4 2.4 fusion.57
  149.4 1.9 fusion.55
  151.3 2.3 fusion.56
  153.7 4.6 fusion.58
  158.2 2.4 bitcast_dynamic-update-slice_fusion.2
  162.6 2.7 multiply_convert_fusion.6
  166.9 14.4 %dynamic_update_slice.35 = f32[4,1024,128]{2,0,1:T(4,128)} dynamic-update-slice(f32[4,1024,128]{2,0,1:T(4,128)} %get-tuple-element.406, f32[1,1024,128]{2,0,1:T(1,128)} %bitcast.136, s32[]{:T(128)} %get-tuple-element.404, s32[]{:T(128)} %constant.146.clone.1..sunk, s32[]{:T(128)} %constant.146.clone.1..sunk) | dynamic-update-slice | bytes 1048580 | tf_op jit(solution)/shard_map/while/body/jit(dynamic_update_index_in_dim)/dynamic_update_slice | solution.py:133
  181.3 2.5 fusion.57
  186.3 1.9 fusion.55
  188.3 2.3 fusion.56
  190.6 4.5 fusion.58
  195.2 2.4 bitcast_dynamic-update-slice_fusion.2
  199.6 2.7 multiply_convert_fusion.6
  203.8 14.4 %dynamic_update_slice.35 = f32[4,1024,128]{2,0,1:T(4,128)} dynamic-update-slice(f32[4,1024,128]{2,0,1:T(4,128)} %get-tuple-element.406, f32[1,1024,128]{2,0,1:T(1,128)} %bitcast.136, s32[]{:T(128)} %get-tuple-element.404, s32[]{:T(128)} %constant.146.clone.1..sunk, s32[]{:T(128)} %constant.146.clone.1..sunk) | dynamic-update-slice | bytes 1048580 | tf_op jit(solution)/shard_map/while/body/jit(dynamic_update_index_in_dim)/dynamic_update_slice | solution.py:133
  218.3 2.5 fusion.57
  223.3 1.9 fusion.55
  225.2 2.3 fusion.56
  227.6 4.6 fusion.58
  232.1 2.4 bitcast_dynamic-update-slice_fusion.2
  236.5 2.7 multiply_convert_fusion.6
  240.8 14.4 %dynamic_update_slice.35 = f32[4,1024,128]{2,0,1:T(4,128)} dynamic-update-slice(f32[4,1024,128]{2,0,1:T(4,128)} %get-tuple-element.406, f32[1,1024,128]{2,0,1:T(1,128)} %bitcast.136, s32[]{:T(128)} %get-tuple-element.404, s32[]{:T(128)} %constant.146.clone.1..sunk, s32[]{:T(128)} %constant.146.clone.1..sunk) | dynamic-update-slice | bytes 1048580 | tf_op jit(solution)/shard_map/while/body/jit(dynamic_update_index_in_dim)/dynamic_update_slice | solution.py:133
  255.2 2.5 fusion.57
  257.7 17.1 %fusion.31 = (f32[128]{0:T(128)S(1)}, f32[1024,4]{1,0:T(8,128)}) fusion(f32[4,1024,128]{2,0,1:T(4,128)} %get-tuple-element.164, f32[1,1024,4,128]{3,2,1,0:T(4,128)} %copy-done.1, f32[1024,4]{1,0:T(8,128)} %copy-done.3, f32[128]{0:T(128)S(1)} %copy-done.17), kind=kLoop, calls=%fused_computation.46 | loop fusion | flops 3141504 | bytes 4228096 | tf_op jit(solution)/shard_map/reduce_sum | solution.py:147
  274.8 1.8 reduce_sum.103
  277.1 4.7 %fusion.32 = bf16[1024,1,128]{2,1,0:T(2,128)(2,1)} fusion(f32[1024]{0:T(1024)S(1)} %div.48, f32[1,1024,128]{2,0,1:T(1,128)S(1)} %bitcast.144, f32[1,1024,128]{2,0,1:T(1,128)S(1)} %bitcast.142, f32[128]{0:T(128)S(1)} %copy-done.15, f32[1024]{0:T(1024)S(1)} %copy-done.13), kind=kLoop, calls=%fused_computation.72 | loop fusion | flops 786432 | bytes 1319424
  282.3 3.3 reduce.17
  286.3 8.4 %all-to-all-start.6 = ((bf16[8,2,8192]{2,1,0:T(2,128)(2,1)}), bf16[8,2,8192]{2,1,0:T(2,128)(2,1)}, u32[]{:S(2)}, u32[]{:S(2)}) async-start(bf16[8,2,8192]{2,1,0:T(2,128)(2,1)} %reshape.601), calls=%async_computation.6 | async-start | bytes 524288 | tf_op jit(solution)/shard_map/all_to_all | solution.py:159
  294.7 1.7 reduce_sum.107
  297.6 3.1 reduce.18
  301.5 1.9 broadcast_multiply_fusion
  303.4 5.0 %all-to-all-start.7 = ((bf16[8,2,8192]{2,1,0:T(2,128)(2,1)}), bf16[8,2,8192]{2,1,0:T(2,128)(2,1)S(1)}, u32[]{:S(2)}, u32[]{:S(2)}) async-start(bf16[8,2,8192]{2,1,0:T(2,128)(2,1)} %reshape.603), calls=%async_computation.7 | async-start | bytes 524288 | tf_op jit(solution)/shard_map/all_to_all | solution.py:160
  308.4 6.0 %multiply_convert_fusion.1 = bf16[1,1024,4,128]{3,2,1,0:T(4,128)(2,1)} fusion(f32[4,1024,128]{2,0,1:T(4,128)} %get-tuple-element.164, f32[1,1024,4,128]{3,2,1,0:T(4,128)S(1)} %copy-done.2, f32[1024,4]{1,0:T(8,128)} %broadcast_multiply_fusion, f32[128]{0:T(128)S(1)} %copy-done.17, f32[1024,4]{1,0:T(8,128)} %copy-done.3), kind=kLoop, calls=%fused_computation.47 | loop fusion | flops 3145728 | bytes 5276160 | tf_op jit(solution)/shard_map/convert_element_type | solution.py:142
  314.4 2.4 copy.76
  316.9 4.6 %copy.77 = bf16[1,1024,512]{2,0,1:T(2,128)(2,1)S(1)} copy(bf16[1,1024,512]{1,2,0:T(8,128)(2,1)} %bitcast.145) | data formatting | bytes 2097152 | tf_op jit(solution)/shard_map/reshape | solution.py:150
  321.5 8.0 %reduce.16 = bf16[1024,512]{1,0:T(8,128)(2,1)} reduce(bf16[1024,1,512]{2,1,0:T(2,128)(2,1)S(1)} %bitcast.140, bf16[]{:T(256)} %broadcast.355), dimensions={1}, to_apply=%bitcast.83.reduce_sub_computation | reduce | bytes 2097154
  329.5 2.6 reshape.599
  332.1 5.1 %all-to-all-start.5 = ((bf16[8,2,32768]{2,1,0:T(2,128)(2,1)}), bf16[8,2,32768]{2,1,0:T(2,128)(2,1)}, u32[]{:S(2)}, u32[]{:S(2)}) async-start(bf16[8,2,32768]{2,1,0:T(2,128)(2,1)} %reshape.599), calls=%async_computation.5 | async-start | bytes 2097152 | tf_op jit(solution)/shard_map/all_to_all | solution.py:158
  337.2 4.6 %copy.73 = bf16[1,1024,512]{2,0,1:T(2,128)(2,1)S(1)} copy(bf16[1,1024,512]{1,2,0:T(8,128)(2,1)} %bitcast.153) | data formatting | bytes 2097152 | tf_op jit(solution)/shard_map/convert_element_type | solution.py:137
  341.9 8.0 %reduce.15 = bf16[1024,512]{1,0:T(8,128)(2,1)} reduce(bf16[1024,1,512]{2,1,0:T(2,128)(2,1)S(1)} %bitcast.139, bf16[]{:T(256)} %broadcast.355), dimensions={1}, to_apply=%bitcast.81.reduce_sub_computation | reduce | bytes 2097154
  349.9 2.6 reshape.597
  352.5 4.9 %all-to-all-start.4 = ((bf16[8,2,32768]{2,1,0:T(2,128)(2,1)}), bf16[8,2,32768]{2,1,0:T(2,128)(2,1)}, u32[]{:S(2)}, u32[]{:S(2)}) async-start(bf16[8,2,32768]{2,1,0:T(2,128)(2,1)} %reshape.597), calls=%async_computation.4 | async-start | bytes 2097152 | tf_op jit(solution)/shard_map/all_to_all | solution.py:157
  357.4 81.7 %all-reduce = (f32[128]{0:T(128)S(1)}, f32[128]{0:T(128)S(1)}) all-reduce(f32[128]{0:T(128)S(1)} %get-tuple-element.267, f32[128]{0:T(128)S(1)} %get-tuple-element.269), channel_id=1, replica_groups=mesh['dp'=32,'head'=8] {'dp','head'}, use_global_device_ids=true, to_apply=%region_13.16 | all-reduce | flops 256 | bytes 2048 | tf_op jit(solution)/shard_map/psum | solution.py:162
  443.2 4.3 reshape.600
  451.7 4.3 reshape.598
  (121 shorter events, 46.2 us)
Async XLA Ops:
  0.6 18.3 %copy-start = (bf16[32,32,512]{2,1,0:T(8,128)(2,1)S(1)}, bf16[32,32,512]{2,1,0:T(8,128)(2,1)}, u32[]{:S(2)}) copy-start(bf16[32,32,512]{2,1,0:T(8,128)(2,1)} %param.15) | copy-start | bytes 3145732
  7.0 23.1 %all-to-all-start.1 = ((bf16[32,32,128]{2,1,0:T(8,128)(2,1)}), bf16[32,32,128]{2,1,0:T(8,128)(2,1)S(1)}, u32[]{:S(2)}, u32[]{:S(2)}) async-start(bf16[32,32,128]{2,1,0:T(8,128)(2,1)} %get-tuple-element.304), calls=%async_computation.1 | async-start | bytes 524288 | tf_op jit(solution)/shard_map/all_to_all | solution.py:82
  21.4 48.4 %copy-start.18 = (s32[32]{0:T(128)S(1)}, s32[32]{0:T(128)}, u32[]{:S(2)}) copy-start(s32[32]{0:T(128)} %param.21) | copy-start | bytes 388
  21.4 52.0 %copy-start.14 = (f32[128]{0:T(128)S(1)}, f32[128]{0:T(128)}, u32[]{:S(2)}) copy-start(f32[128]{0:T(128)} %param.20) | copy-start | bytes 1540
  30.1 42.5 %copy-start.6 = (bf16[32,32,128]{2,1,0:T(8,128)(2,1)}, bf16[32,32,128]{2,1,0:T(8,128)(2,1)S(1)}, u32[]{:S(2)}) copy-start(bf16[32,32,128]{2,1,0:T(8,128)(2,1)S(1)} %all-to-all-done.1) | copy-start | bytes 786436
  59.9 31.7 %all-to-all-start.3 = ((bf16[32,32,512]{2,1,0:T(8,128)(2,1)}), bf16[32,32,512]{2,1,0:T(8,128)(2,1)}, u32[]{:S(2)}, u32[]{:S(2)}) async-start(bf16[32,32,512]{2,1,0:T(8,128)(2,1)} %get-tuple-element.301), calls=%async_computation.3 | async-start | bytes 2097152 | tf_op jit(solution)/shard_map/all_to_all | solution.py:84
  72.0 0.6 copy-start.10
  72.1 0.6 copy-start.12
  72.6 0.8 copy-start.4
  72.6 28.7 %copy-start.16 = (f32[128]{0:T(128)S(1)}, f32[128]{0:T(128)}, u32[]{:S(2)}) copy-start(f32[128]{0:T(128)} %param.19) | copy-start | bytes 1540
  75.4 29.4 %copy-start.1 = (f32[1,1024,4,128]{3,2,1,0:T(4,128)}, f32[1,1024,4,128]{3,2,1,0:T(4,128)S(1)}, u32[]{:S(2)}) copy-start(f32[1,1024,4,128]{3,2,1,0:T(4,128)S(1)} %reshape.542) | copy-start | bytes 6291460
  91.6 18.3 %all-to-all-start.2 = ((bf16[32,32,128]{2,1,0:T(8,128)(2,1)}), bf16[32,32,128]{2,1,0:T(8,128)(2,1)}, u32[]{:S(2)}, u32[]{:S(2)}) async-start(bf16[32,32,128]{2,1,0:T(8,128)(2,1)} %get-tuple-element.303), calls=%async_computation.2 | async-start | bytes 524288 | tf_op jit(solution)/shard_map/all_to_all | solution.py:83
  100.5 0.8 copy-start.3
  109.9 147.8 %copy-start.17 = (f32[128]{0:T(128)S(1)}, f32[128]{0:T(128)}, u32[]{:S(2)}) copy-start(f32[128]{0:T(128)} %param.19) | copy-start | bytes 1540
  116.7 4.6 copy-start.8
  123.7 1.0 copy-start.9
  153.7 4.6 copy-start.8
  160.6 1.0 copy-start.9
  190.6 4.5 copy-start.8
  197.6 1.0 copy-start.9
  227.6 4.6 copy-start.8
  234.5 1.0 copy-start.9
  257.7 18.9 %copy-start.7 = (bf16[32,32,128]{2,1,0:T(8,128)(2,1)S(1)}, bf16[32,32,128]{2,1,0:T(8,128)(2,1)}, u32[]{:S(2)}) copy-start(bf16[32,32,128]{2,1,0:T(8,128)(2,1)} %copy-done.6) | copy-start | bytes 786436
  257.7 18.9 %copy-start.11 = (f32[32,32]{1,0:T(8,128)S(1)}, f32[32,32]{1,0:T(8,128)}, u32[]{:S(2)}) copy-start(f32[32,32]{1,0:T(8,128)} %copy-done.10) | copy-start | bytes 12292
  257.7 18.9 %copy-start.15 = (f32[128]{0:T(128)S(1)}, f32[128]{0:T(128)}, u32[]{:S(2)}) copy-start(f32[128]{0:T(128)} %param.20) | copy-start | bytes 1540
  257.7 19.4 %copy-start.5 = (f32[32,32,128]{2,1,0:T(8,128)S(1)}, f32[32,32,128]{2,1,0:T(8,128)}, u32[]{:S(2)}) copy-start(f32[32,32,128]{2,1,0:T(8,128)} %copy-done.4) | copy-start | bytes 1572868
  257.7 19.4 %copy-start.13 = (f32[1024]{0:T(1024)S(1)}, f32[1024]{0:T(1024)}, u32[]{:S(2)}) copy-start(f32[1024]{0:T(1024)} %copy-done.12) | copy-start | bytes 12292
  281.8 26.7 %copy-start.2 = (f32[1,1024,4,128]{3,2,1,0:T(4,128)S(1)}, f32[1,1024,4,128]{3,2,1,0:T(4,128)}, u32[]{:S(2)}) copy-start(f32[1,1024,4,128]{3,2,1,0:T(4,128)} %copy-done.1) | copy-start | bytes 6291460
  286.3 17.1 %all-to-all-start.6 = ((bf16[8,2,8192]{2,1,0:T(2,128)(2,1)}), bf16[8,2,8192]{2,1,0:T(2,128)(2,1)}, u32[]{:S(2)}, u32[]{:S(2)}) async-start(bf16[8,2,8192]{2,1,0:T(2,128)(2,1)} %reshape.601), calls=%async_computation.6 | async-start | bytes 524288 | tf_op jit(solution)/shard_map/all_to_all | solution.py:159
  303.4 28.7 %all-to-all-start.7 = ((bf16[8,2,8192]{2,1,0:T(2,128)(2,1)}), bf16[8,2,8192]{2,1,0:T(2,128)(2,1)S(1)}, u32[]{:S(2)}, u32[]{:S(2)}) async-start(bf16[8,2,8192]{2,1,0:T(2,128)(2,1)} %reshape.603), calls=%async_computation.7 | async-start | bytes 524288 | tf_op jit(solution)/shard_map/all_to_all | solution.py:160
  332.1 20.4 %all-to-all-start.5 = ((bf16[8,2,32768]{2,1,0:T(2,128)(2,1)}), bf16[8,2,32768]{2,1,0:T(2,128)(2,1)}, u32[]{:S(2)}, u32[]{:S(2)}) async-start(bf16[8,2,32768]{2,1,0:T(2,128)(2,1)} %reshape.599), calls=%async_computation.5 | async-start | bytes 2097152 | tf_op jit(solution)/shard_map/all_to_all | solution.py:158
  352.5 99.2 %all-to-all-start.4 = ((bf16[8,2,32768]{2,1,0:T(2,128)(2,1)}), bf16[8,2,32768]{2,1,0:T(2,128)(2,1)}, u32[]{:S(2)}, u32[]{:S(2)}) async-start(bf16[8,2,32768]{2,1,0:T(2,128)(2,1)} %reshape.597), calls=%async_computation.4 | async-start | bytes 2097152 | tf_op jit(solution)/shard_map/all_to_all | solution.py:157
where the time goes:
time: 468 us; the launch traced here: 460 us
  local copies, waits for them, and re-layouts  121 us (26%)
  blocking collectives  112 us (24%)
  other arithmetic  81.5 us (17%)
  matrix products  62.2 us (13%)
  starting transfers between devices  50.3 us (11%)
  waiting for transfers between devices  21.7 us (5%)
  loops' own time  8.08 us (2%)
    psum x1, blocking collectives, per_device(): q_sum, k_sum = lax.psum((query_correction, key_correction), ('dp', 'head'))  81.7 us
    dynamic_update_slice x4, local copies, waits for them, and re-layouts, per_device(): lax.map(joined_item, item_ids)  57.8 us
    all_to_all x1, blocking collectives, per_device(): lax.all_to_all(sorted_query, 'dp', split_axis=0, concat_axis=1, tiled=True)  29.8 us
    unnamed x5, other arithmetic  27.1 us
    unnamed x51, local copies, waits for them, and re-layouts  26.4 us
    dot_general x4, matrix products, backward_from(): jnp.dot(weights_low.T, grad_head, preferred_element_type=jnp.float32)  18.2 us
    reduce_sum x1, other arithmetic, per_device(): query_correction = jnp.sum(grad_qn * q_hat, axis=(0, 1, 2))  17.1 us
    all_to_all x1, waiting for transfers between devices, per_device(): lax.all_to_all(sorted_grad, 'dp', split_axis=0, concat_axis=1, tiled=True)  14.2 us
  transfers between devices with their start and end apart: 7, of which 3 were waited for; matrix products, arithmetic and copies ran while one was open for 17% of the time, Pallas kernels for 0%

commit v1 on v0

v1 whole, which is shorter than its diff:
```python
import functools
import math

import jax
import jax.numpy as jnp
from jax import lax
from jax.experimental import pallas as pl
from jax.experimental.pallas import tpu as pltpu
from jax.sharding import PartitionSpec as P

WIDTH = 128
SLOT = 1024
TILE = 256
REACH = 512
EPSILON = 1e-06
NEG_FILL = -1e30
SCALE = 1.0 / math.sqrt(WIDTH)
BF = jnp.bfloat16
F32 = jnp.float32


def rms(rows):
    values = rows.astype(F32)
    inverse = lax.rsqrt(jnp.mean(values * values, axis=-1, keepdims=True) + EPSILON)
    return values * inverse, inverse


def unnormalize(grad_normed, gain, normed, inverse):
    grad_hat = grad_normed * gain
    inner = jnp.mean(grad_hat * normed, axis=-1, keepdims=True)
    return inverse * (grad_hat - normed * inner)


def pack_first(owners, key, value, query, grad, out):
    for s in range(key.shape[0]):
        o = owners[s]
        out[o, 0] = key[s]
        out[o, 1] = value[s]
        out[o, 2] = query[s]
        out[o, 3] = grad[s]


def pack_rest(owners, query, grad, *outs):
    for s in range(query.shape[0]):
        o = owners[s]
        for h, out in enumerate(outs):
            cols = pl.ds(h * WIDTH, WIDTH)
            out[o, 0] = query[s, :, cols]
            out[o, 1] = grad[s, :, cols]


def dot(a, b):
    return jnp.dot(a, b, preferred_element_type=F32)


def dot_t(a, b):
    return lax.dot_general(a, b, (((1,), (1,)), ((), ())), preferred_element_type=F32)


def attend(head, last, *refs):
    refs = list(refs)
    live, doc, q_gain, k_gain, kv = refs[:5]
    del refs[:5]
    if head == 0:
        own, q_slot, g_slot = kv, 2, 3
    else:
        own, q_slot, g_slot = refs.pop(0), 0, 1
        dk_in, dv_in, qs_in = refs[:3]
        del refs[:3]
    send = refs.pop(0)
    if last:
        kv_send, sums = refs[:2]
    else:
        dk, dv, qs = refs[:3]
    del refs[: 2 if last else 3]
    if last:
        kn, knt, vt, dk, dv = refs
    else:
        kn, knt, vt = refs

    def rows(ref, slot, at, size):
        return ref[at // 32 : (at + size) // 32, slot].reshape(size, WIDTH)

    doc_row = doc[...]
    start = jnp.zeros_like(doc_row)
    for d in range(8):
        count = jnp.sum((doc_row == d).astype(jnp.int32), axis=1, keepdims=True)
        start = start + jnp.where(doc_row > d, count, 0)
    length = live[0]
    if head == 0:
        dk[...] = jnp.zeros_like(dk)
        dv[...] = jnp.zeros_like(dv)
        q_sum = jnp.zeros((1, WIDTH), F32)
    else:
        dk[...] = dk_in[...]
        dv[...] = dv_in[...]
        q_sum = qs_in[...]
    for at in range(0, SLOT, TILE):
        part = pl.ds(at, TILE)
        k_hat, _ = rms(rows(kv, 0, at, TILE))
        normed = k_hat * k_gain[...]
        kn[part] = normed.astype(BF)
        knt[:, part] = normed.T.astype(BF)
        vt[:, part] = rows(kv, 1, at, TILE).astype(F32).T.astype(BF)
    u_rel = lax.broadcasted_iota(jnp.int32, (TILE, TILE), 0)
    t_rel = lax.broadcasted_iota(jnp.int32, (1, TILE), 1)
    for t0 in range(0, SLOT, TILE):
        u_list = [u for u in range(0, t0 + 1, TILE) if t0 - (u + TILE - 1) < REACH]
        q_hat, q_inv = rms(rows(own, q_slot, t0, TILE))
        q_n = (q_hat * q_gain[...]).astype(BF)
        g = rows(own, g_slot, t0, TILE)
        g_t = g.astype(F32).T
        g_tb = g_t.astype(BF)
        first = start[:, t0 : t0 + TILE]
        scores = []
        for u0 in u_list:
            s = dot_t(kn[pl.ds(u0, TILE)], q_n) * (SCALE * math.log2(math.e))
            allowed = u_rel >= first - u0
            if u0 == t0:
                allowed = allowed & (u_rel <= t_rel)
            scores.append(jnp.where(allowed, s, NEG_FILL))
        largest = functools.reduce(
            jnp.maximum, [jnp.max(s, axis=0, keepdims=True) for s in scores]
        )
        weights = [jnp.exp2(s - largest) for s in scores]
        total = sum(jnp.sum(w, axis=0, keepdims=True) for w in weights)
        factor = jnp.where(t_rel + t0 < length, 1.0 / jnp.maximum(total, 1.0), 0.0)
        probs = [w * factor for w in weights]
        low = [p.astype(BF) for p in probs]
        o_t = sum(dot(vt[:, pl.ds(u0, TILE)], p) for u0, p in zip(u_list, low))
        delta = jnp.sum(g_t * o_t, axis=0, keepdims=True)
        dq_t = 0.0
        for u0, p, pb in zip(u_list, probs, low):
            part = pl.ds(u0, TILE)
            dv[part] += dot(pb, g)
            dp = dot(rows(kv, 1, u0, TILE), g_tb)
            ds = (p * (dp - delta)).astype(BF)
            dk[part] += dot(ds, q_n)
            dq_t += dot(knt[:, part], ds)
        dq = dq_t.T * SCALE
        q_sum += jnp.sum(dq * q_hat, axis=0, keepdims=True)
        dq = unnormalize(dq, q_gain[...], q_hat, q_inv).astype(BF)
        o = o_t.T.astype(BF)
        for n in range(TILE // WIDTH):
            block = t0 // WIDTH + n
            send[block, 0] = o[n * WIDTH : (n + 1) * WIDTH]
            send[block, 1] = dq[n * WIDTH : (n + 1) * WIDTH]
    if not last:
        qs[...] = q_sum
        return
    k_sum = jnp.zeros((1, WIDTH), F32)
    for at in range(0, SLOT, WIDTH):
        part = pl.ds(at, WIDTH)
        k_hat, k_inv = rms(rows(kv, 0, at, WIDTH))
        gk = dk[part] * SCALE
        k_sum += jnp.sum(gk * k_hat, axis=0, keepdims=True)
        kv_send[at // WIDTH, 0] = unnormalize(gk, k_gain[...], k_hat, k_inv).astype(BF)
        kv_send[at // WIDTH, 1] = dv[part].astype(BF)
    sums[0:1] = q_sum
    sums[1:2] = k_sum


def place(*refs):
    heads = len(refs) - 5
    received, kv, outs = refs[:heads], refs[heads], refs[heads + 1 :]
    for src in range(kv.shape[0]):
        for h, ref in enumerate(received):
            cols = pl.ds((src * heads + h) * WIDTH, WIDTH)
            outs[0][0, :, cols] = ref[src, 0]
            outs[1][0, :, cols] = ref[src, 1]
        cols = pl.ds(src * WIDTH, WIDTH)
        outs[2][0, :, cols] = kv[src, 0]
        outs[3][0, :, cols] = kv[src, 1]


def params():
    return pltpu.CompilerParams(vmem_limit_bytes=32 * 1024 * 1024)


def shape(dims, dtype=BF):
    return jax.ShapeDtypeStruct(dims, dtype)


def attend_head(head, last, live, doc, q_gain, k_gain, kv, own, carry):
    args = [live, doc, q_gain, k_gain, kv]
    if head > 0:
        args += [own, *carry]
    blocks = SLOT // WIDTH
    outs = [shape((blocks, 2, WIDTH, WIDTH))]
    if last:
        outs += [shape((blocks, 2, WIDTH, WIDTH)), shape((2, WIDTH), F32)]
    else:
        outs += [shape((SLOT, WIDTH), F32), shape((SLOT, WIDTH), F32), shape((1, WIDTH), F32)]
    scratch = [
        pltpu.VMEM((SLOT, WIDTH), BF),
        pltpu.VMEM((WIDTH, SLOT), BF),
        pltpu.VMEM((WIDTH, SLOT), BF),
    ]
    if last:
        scratch += [pltpu.VMEM((SLOT, WIDTH), F32), pltpu.VMEM((SLOT, WIDTH), F32)]
    return pl.pallas_call(
        functools.partial(attend, head, last),
        out_shape=outs,
        in_specs=[pl.BlockSpec(memory_space=pltpu.SMEM)]
        + [pl.BlockSpec(memory_space=pltpu.VMEM)] * (len(args) - 1),
        out_specs=[pl.BlockSpec(memory_space=pltpu.VMEM)] * len(outs),
        scratch_shapes=scratch,
        compiler_params=params(),
        cost_estimate=pl.CostEstimate(
            flops=12 * 9 * TILE * TILE * WIDTH, bytes_accessed=4 << 20, transcendentals=9 * TILE * TILE
        ),
        name="attend",
    )(*args)


def per_device(query, key, value, grad, q_gain, k_gain, lengths, owners, doc_ids):
    seqs, per_src, features = query.shape
    heads = features // WIDTH
    head_devs = lax.axis_size("head")
    vmem = pl.BlockSpec(memory_space=pltpu.VMEM)
    smem = pl.BlockSpec(memory_space=pltpu.SMEM)
    one = pl.BlockSpec((seqs, per_src, WIDTH), lambda n: (0, 0, 0))
    first = pl.pallas_call(
        pack_first,
        grid=(1,),
        out_shape=shape((seqs, 4, per_src, WIDTH)),
        in_specs=[smem, one, one, one, one],
        out_specs=pl.BlockSpec((seqs, 4, per_src, WIDTH), lambda n: (0, 0, 0, 0)),
        compiler_params=params(),
        name="pack_first",
    )(owners, key, value, query, grad)
    rest = pl.pallas_call(
        pack_rest,
        out_shape=[shape((seqs, 2, per_src, WIDTH))] * (heads - 1),
        in_specs=[smem, vmem, vmem],
        out_specs=[vmem] * (heads - 1),
        compiler_params=params(),
        name="pack_rest",
    )(owners, query[:, :, WIDTH:], grad[:, :, WIDTH:])

    mine = jnp.argmax(owners == lax.axis_index("dp")).astype(jnp.int32)
    live = lax.dynamic_slice_in_dim(lengths, mine, 1)
    doc = lax.dynamic_slice_in_dim(doc_ids, mine, 1, axis=0)
    q_gain = q_gain.reshape(1, WIDTH)
    k_gain = k_gain.reshape(1, WIDTH)

    kv = lax.all_to_all(first, "dp", 0, 0, tiled=True)
    own = [None] + [lax.all_to_all(r, "dp", 0, 0, tiled=True) for r in rest]
    received, carry = [], None
    for h in range(heads):
        last = h == heads - 1
        out, *carry = attend_head(h, last, live, doc, q_gain, k_gain, kv, own[h], carry)
        received.append(lax.all_to_all(out, "head", 0, 0, tiled=True))
    kv_send, sums = carry
    received.append(lax.all_to_all(kv_send, "head", 0, 0, tiled=True))
    sums = lax.psum(sums, ("dp", "head"))
    wide, narrow = shape((1, WIDTH, heads * head_devs * WIDTH)), shape((1, WIDTH, head_devs * WIDTH))
    outs = pl.pallas_call(
        place,
        out_shape=[wide, wide, narrow, narrow],
        in_specs=[vmem] * len(received),
        out_specs=[vmem] * 4,
        compiler_params=params(),
        name="place",
    )(*received)
    tokens = seqs * SLOT
    return (
        *outs,
        sums[0] / math.sqrt(tokens * heads * head_devs),
        sums[1] / math.sqrt(tokens * head_devs),
    )


def solution(mesh):
    spread = P(None, "dp", "head")
    packed = P("dp", "head", None)
    return jax.shard_map(
        per_device,
        mesh=mesh,
        in_specs=(spread,) * 4 + (P(),) * 5,
        out_specs=(packed,) * 4 + (P(),) * 2,
        check_vma=False,
    )
```

time: 468 us -> 253 us (0.54); the launches traced: 460 us -> 252 us
  local copies, waits for them, and re-layouts: 121 us -> 10.7 us
  other arithmetic: 81.5 us -> 1.17 us
  matrix products: 62.2 us -> 0 us
  blocking collectives: 112 us -> 162 us
  Pallas kernels: 0 us -> 27.8 us
  starting transfers between devices: 50.3 us -> 30 us
  loops' own time: 8.08 us -> 0 us
    dot_general x24 -> x0, matrix products: 62.2 us -> none  [the longest x4 18.2 us: backward_from(): jnp.dot(weights_low.T, grad_head, preferred_element_type=jnp.float32)]
    dynamic_update_slice x4 -> x0, local copies, waits for them, and re-layouts: 57.8 us -> none  [per_device(): lax.map(joined_item, item_ids)]
    all_to_all x1 -> x4, blocking collectives: 29.8 us -> 86.7 us  [the longest x1 31.6 us: per_device(): kv = lax.all_to_all(first, 'dp', 0, 0, tiled=True)]
    reduce_sum x14 -> x0, other arithmetic: 36.6 us -> none  [the longest x1 17.1 us: per_device(): query_correction = jnp.sum(grad_qn * q_hat, axis=(0, 1, 2))]
    pallas_call x0 -> x7, Pallas kernels: none -> 27.8 us  [the longest x4 23.2 us: attend_head(): pl.pallas_call(functools.partial(attend, head, last), out_shape=outs, in_...]
    unnamed x5 -> x0, other arithmetic: 27.1 us -> none
    all_to_all x7 -> x5, starting transfers between devices: 50.3 us -> 30 us  [the longest x3 17.7 us: per_device(): received.append(lax.all_to_all(out, 'head', 0, 0, tiled=True))]
    unnamed x51 -> x34, local copies, waits for them, and re-layouts: 26.4 us -> 8.7 us
  transfers between devices with their start and end apart: 7 -> 5, of which waited for: 3 -> 3; matrix products, arithmetic and copies ran while one was open for 17% -> 1% of each run, Pallas kernels for 0% -> 9%
where the time goes in v1:
time: 253 us; the launch traced here: 252 us
  blocking collectives  162 us (64%)
  starting transfers between devices  30 us (12%)
  Pallas kernels  27.8 us (11%)
  waiting for transfers between devices  17.5 us (7%)
  local copies, waits for them, and re-layouts  10.7 us (4%)
  between operations  2.74 us (1%)
    psum x1, blocking collectives, per_device(): sums = lax.psum(sums, ('dp', 'head'))  75 us
    all_to_all x1, blocking collectives, per_device(): kv = lax.all_to_all(first, 'dp', 0, 0, tiled=True)  31.6 us
    all_to_all x1, blocking collectives, per_device(): own = [None] + [lax.all_to_all(r, 'dp', 0, 0, tiled=True) for r in rest]  28.2 us
    pallas_call x4, Pallas kernels, attend_head(): pl.pallas_call(functools.partial(attend, head, last), out_shape=outs, in_...  23.2 us
    all_to_all x3, starting transfers between devices, per_device(): received.append(lax.all_to_all(out, 'head', 0, 0, tiled=True))  17.7 us
    all_to_all x2, waiting for transfers between devices, per_device(): own = [None] + [lax.all_to_all(r, 'dp', 0, 0, tiled=True) for r in rest]  16.7 us
    all_to_all x1, blocking collectives, per_device(): received.append(lax.all_to_all(out, 'head', 0, 0, tiled=True))  14.2 us
    all_to_all x1, blocking collectives, per_device(): received.append(lax.all_to_all(kv_send, 'head', 0, 0, tiled=True))  12.8 us
  transfers between devices with their start and end apart: 5, of which 3 were waited for; matrix products, arithmetic and copies ran while one was open for 1% of the time, Pallas kernels for 9%

profile of v1, /device:TPU:1, one launch (start us, length us, event | category | flops | bytes accessed | tf_op | source)
XLA Modules:
  0.0 251.6 jit_solution(17600856142131931101)
XLA Ops:
  0.6 0.0 copy-start
  0.6 0.0 copy-start.2
  0.7 1.3 slice.12.query
  2.0 0.2 copy-done.2
  2.1 0.0 copy-start.7
  2.1 0.1 slice.13.grad
  2.2 0.6 copy-done.7
  2.8 1.8 pack_rest.1
  4.6 0.0 copy-start.1
  4.6 28.2 %all_to_all.45.refs_5_ = bf16[32,2,32,128]{3,2,1,0:T(8,128)(2,1)} all-to-all(bf16[32,2,32,128]{3,2,1,0:T(8,128)(2,1)S(1)} %get-tuple-element.31), channel_id=1, replica_groups=mesh['dp'=32,'head'=8] {'dp'}, dimensions={0} | all-to-all | bytes 1048576 | tf_op jit(solution)/shard_map/all_to_all | solution.py:248
  32.7 0.0 copy-start.5
  32.7 5.5 %all-to-all-start.4 = ((bf16[32,2,32,128]{3,2,1,0:T(8,128)(2,1)}), bf16[32,2,32,128]{3,2,1,0:T(8,128)(2,1)}, u32[]{:S(2)}, u32[]{:S(2)}) async-start(bf16[32,2,32,128]{3,2,1,0:T(8,128)(2,1)} %get-tuple-element.36), calls=%async_computation.4 | async-start | bytes 1048576 | tf_op jit(solution)/shard_map/all_to_all | solution.py:248
  38.2 0.0 copy-done.1
  38.2 0.0 copy-done.5
  38.2 0.0 copy-start.6
  38.3 0.9 copy-done.6
  39.2 0.6 pack_first.1
  39.8 13.4 %all-to-all-done.4.refs_5_ = bf16[32,2,32,128]{3,2,1,0:T(8,128)(2,1)} async-done(((bf16[32,2,32,128]{3,2,1,0:T(8,128)(2,1)}), bf16[32,2,32,128]{3,2,1,0:T(8,128)(2,1)}, u32[]{:S(2)}, u32[]{:S(2)}) %all-to-all-start.4) | async-done | bytes 524320 | tf_op jit(solution)/shard_map/all_to_all | solution.py:248
  53.3 31.6 %all_to_all.46.refs_4_ = bf16[32,4,32,128]{3,2,1,0:T(8,128)(2,1)S(1)} all-to-all(bf16[32,4,32,128]{3,2,1,0:T(8,128)(2,1)S(1)} %pack_first.1), channel_id=1, replica_groups=mesh['dp'=32,'head'=8] {'dp'}, dimensions={0} | all-to-all | bytes 2097152 | tf_op jit(solution)/shard_map/all_to_all | solution.py:247
  84.8 6.8 %all-to-all-start.6 = ((bf16[32,2,32,128]{3,2,1,0:T(8,128)(2,1)}), bf16[32,2,32,128]{3,2,1,0:T(8,128)(2,1)S(1)}, u32[]{:S(2)}, u32[]{:S(2)}) async-start(bf16[32,2,32,128]{3,2,1,0:T(8,128)(2,1)} %get-tuple-element.41), calls=%async_computation.6 | async-start | bytes 1048576 | tf_op jit(solution)/shard_map/all_to_all | solution.py:248
  91.6 0.7 compare_reduce_fusion
  93.6 0.0 copy-start.16
  94.2 0.0 copy-done.16
  94.3 0.6 dynamic_slice.6.refs_0_
  94.8 0.0 copy-done
  94.9 0.0 copy-start.8
  94.9 0.0 copy-start.9
  94.9 0.6 copy-done.8
  95.5 0.0 copy-done.9
  95.5 5.8 %attend.4 = (bf16[8,2,128,128]{3,2,1,0:T(8,128)(2,1)}, f32[1024,128]{1,0:T(8,128)S(1)}, f32[1024,128]{1,0:T(8,128)S(1)}, f32[1,128]{1,0:T(1,128)S(1)}) custom-call(s32[1]{0:T(128)} %dynamic_slice.6.refs_0_, s32[1,1024]{1,0:T(1,128)S(1)} %constant_dynamic-slice_fusion.refs_1_, f32[1,128]{1,0:T(1,128)S(1)} %bitcast.6, f32[1,128]{1,0:T(1,128)S(1)} %bitcast.10, ...), custom_call_target="tpu_custom_call" | custom-call | flops 905969664 | bytes 4194304 | tf_op jit(solution)/shard_map/attend/pallas_call | solution.py:201
  101.3 0.0 copy-start.12
  101.3 0.8 copy-done.12
  102.1 0.0 copy-start.14
  102.1 0.8 copy-done.14
  102.9 3.2 %all-to-all-done.6.refs_5_ = bf16[32,2,32,128]{3,2,1,0:T(8,128)(2,1)S(1)} async-done(((bf16[32,2,32,128]{3,2,1,0:T(8,128)(2,1)}), bf16[32,2,32,128]{3,2,1,0:T(8,128)(2,1)S(1)}, u32[]{:S(2)}, u32[]{:S(2)}) %all-to-all-start.6) | async-done | bytes 524320 | tf_op jit(solution)/shard_map/all_to_all | solution.py:248
  106.2 0.0 copy-start.3
  106.2 9.0 %all-to-all-start.1 = ((bf16[8,2,128,128]{3,2,1,0:T(8,128)(2,1)}), bf16[8,2,128,128]{3,2,1,0:T(8,128)(2,1)S(1)}, u32[]{:S(2)}, u32[]{:S(2)}) async-start(bf16[8,2,128,128]{3,2,1,0:T(8,128)(2,1)} %get-tuple-element.30), calls=%async_computation.1 | async-start | bytes 1048576 | tf_op jit(solution)/shard_map/all_to_all | solution.py:253
  115.1 0.0 copy-done.3
  115.1 0.0 copy-start.13
  115.1 1.0 copy-done.13
  116.2 0.0 copy-start.15
  116.2 1.0 copy-done.15
  117.2 5.8 %attend.5 = (bf16[8,2,128,128]{3,2,1,0:T(8,128)(2,1)}, f32[1024,128]{1,0:T(8,128)S(1)}, f32[1024,128]{1,0:T(8,128)S(1)}, f32[1,128]{1,0:T(1,128)S(1)}) custom-call(s32[1]{0:T(128)} %dynamic_slice.6.refs_0_, s32[1,1024]{1,0:T(1,128)S(1)} %constant_dynamic-slice_fusion.refs_1_, f32[1,128]{1,0:T(1,128)S(1)} %bitcast.7, f32[1,128]{1,0:T(1,128)S(1)} %bitcast.11, ...), custom_call_target="tpu_custom_call" | custom-call | flops 905969664 | bytes 4194304 | tf_op jit(solution)/shard_map/attend/pallas_call | solution.py:201
  123.0 0.0 copy-start.10
  123.0 0.8 copy-done.10
  123.8 0.8 all-to-all-done.1.refs_0_
  124.6 4.3 %all-to-all-start.3 = ((bf16[8,2,128,128]{3,2,1,0:T(8,128)(2,1)}), bf16[8,2,128,128]{3,2,1,0:T(8,128)(2,1)S(1)}, u32[]{:S(2)}, u32[]{:S(2)}) async-start(bf16[8,2,128,128]{3,2,1,0:T(8,128)(2,1)} %get-tuple-element.35), calls=%async_computation.3 | async-start | bytes 1048576 | tf_op jit(solution)/shard_map/all_to_all | solution.py:253
  128.9 0.0 copy-start.11
  128.9 1.0 copy-done.11
  129.9 6.8 %attend.6 = (bf16[8,2,128,128]{3,2,1,0:T(8,128)(2,1)}, f32[1024,128]{1,0:T(8,128)S(1)}, f32[1024,128]{1,0:T(8,128)S(1)}, f32[1,128]{1,0:T(1,128)S(1)}) custom-call(s32[1]{0:T(128)} %dynamic_slice.6.refs_0_, s32[1,1024]{1,0:T(1,128)S(1)} %constant_dynamic-slice_fusion.refs_1_, f32[1,128]{1,0:T(1,128)S(1)} %bitcast.8, f32[1,128]{1,0:T(1,128)S(1)} %bitcast.12, ...), custom_call_target="tpu_custom_call" | custom-call | flops 905969664 | bytes 4194304 | tf_op jit(solution)/shard_map/attend/pallas_call | solution.py:201
  136.7 5.0 %attend.7 = (bf16[8,2,128,128]{3,2,1,0:T(8,128)(2,1)S(1)}, bf16[8,2,128,128]{3,2,1,0:T(8,128)(2,1)S(1)}, f32[2,128]{1,0:T(2,128)S(1)}) custom-call(s32[1]{0:T(128)} %dynamic_slice.6.refs_0_, s32[1,1024]{1,0:T(1,128)S(1)} %constant_dynamic-slice_fusion.refs_1_, f32[1,128]{1,0:T(1,128)S(1)} %bitcast.9, f32[1,128]{1,0:T(1,128)S(1)} %bitcast.13, ...), custom_call_target="tpu_custom_call" | custom-call | flops 905969664 | bytes 4194304 | tf_op jit(solution)/shard_map/attend/pallas_call | solution.py:201
  141.7 0.0 copy-start.4
  141.7 0.8 copy-done.4
  142.5 0.0 all-to-all-done.3.refs_1_
  142.5 14.2 %all_to_all.47.refs_3_ = bf16[8,2,128,128]{3,2,1,0:T(8,128)(2,1)S(1)} all-to-all(bf16[8,2,128,128]{3,2,1,0:T(8,128)(2,1)} %copy-done.4), channel_id=1, replica_groups=mesh['dp'=32,'head'=8] {'head'}, dimensions={0} | all-to-all | bytes 1048576 | tf_op jit(solution)/shard_map/all_to_all | solution.py:253
  156.7 12.8 %all_to_all.48.refs_4_ = bf16[8,2,128,128]{3,2,1,0:T(8,128)(2,1)S(1)} all-to-all(bf16[8,2,128,128]{3,2,1,0:T(8,128)(2,1)S(1)} %get-tuple-element.46), channel_id=1, replica_groups=mesh['dp'=32,'head'=8] {'head'}, dimensions={0} | all-to-all | bytes 1048576 | tf_op jit(solution)/shard_map/all_to_all | solution.py:255
  169.4 4.4 %all-to-all-start.5 = ((bf16[8,2,128,128]{3,2,1,0:T(8,128)(2,1)}), bf16[8,2,128,128]{3,2,1,0:T(8,128)(2,1)S(1)}, u32[]{:S(2)}, u32[]{:S(2)}) async-start(bf16[8,2,128,128]{3,2,1,0:T(8,128)(2,1)} %get-tuple-element.40), calls=%async_computation.5 | async-start | bytes 1048576 | tf_op jit(solution)/shard_map/all_to_all | solution.py:253
  173.9 75.0 %psum.7 = f32[2,128]{1,0:T(2,128)S(1)} all-reduce(f32[2,128]{1,0:T(2,128)S(1)} %get-tuple-element.51), channel_id=1, replica_groups=mesh['dp'=32,'head'=8] {'dp','head'}, use_global_device_ids=true, to_apply=%region_1.2 | all-reduce | flops 256 | bytes 2048 | tf_op jit(solution)/shard_map/psum | solution.py:256
  248.9 0.5 multiply_bitcast_fusion
  249.4 0.0 all-to-all-done.5.refs_2_
  249.4 2.2 place.1
  (1 shorter events, 0.0 us)
Async XLA Ops:
  0.6 94.2 %copy-start = (s32[32,1024]{1,0:T(8,128)S(1)}, s32[32,1024]{1,0:T(8,128)}, u32[]{:S(2)}) copy-start(s32[32,1024]{1,0:T(8,128)} %param.17) | copy-start | bytes 393220
  0.6 1.5 copy-start.2
  2.1 0.7 copy-start.7
  4.6 33.6 %copy-start.1 = (bf16[32,32,512]{2,1,0:T(8,128)(2,1)S(1)}, bf16[32,32,512]{2,1,0:T(8,128)(2,1)}, u32[]{:S(2)}) copy-start(bf16[32,32,512]{2,1,0:T(8,128)(2,1)} %query.1) | copy-start | bytes 3145732
  32.7 5.5 %copy-start.5 = (bf16[32,32,128]{2,1,0:T(8,128)(2,1)S(1)}, bf16[32,32,128]{2,1,0:T(8,128)(2,1)}, u32[]{:S(2)}) copy-start(bf16[32,32,128]{2,1,0:T(8,128)(2,1)} %key.1) | copy-start | bytes 786436
  32.7 20.5 %all-to-all-start.4 = ((bf16[32,2,32,128]{3,2,1,0:T(8,128)(2,1)}), bf16[32,2,32,128]{3,2,1,0:T(8,128)(2,1)}, u32[]{:S(2)}, u32[]{:S(2)}) async-start(bf16[32,2,32,128]{3,2,1,0:T(8,128)(2,1)} %get-tuple-element.36), calls=%async_computation.4 | async-start | bytes 1048576 | tf_op jit(solution)/shard_map/all_to_all | solution.py:248
  38.2 1.0 copy-start.6
  84.8 21.3 %all-to-all-start.6 = ((bf16[32,2,32,128]{3,2,1,0:T(8,128)(2,1)}), bf16[32,2,32,128]{3,2,1,0:T(8,128)(2,1)S(1)}, u32[]{:S(2)}, u32[]{:S(2)}) async-start(bf16[32,2,32,128]{3,2,1,0:T(8,128)(2,1)} %get-tuple-element.41), calls=%async_computation.6 | async-start | bytes 1048576 | tf_op jit(solution)/shard_map/all_to_all | solution.py:248
  93.6 0.7 copy-start.16
  94.9 0.7 copy-start.8
  94.9 0.7 copy-start.9
  101.3 0.8 copy-start.12
  102.1 0.8 copy-start.14
  106.2 9.0 %copy-start.3 = (bf16[32,2,32,128]{3,2,1,0:T(8,128)(2,1)S(1)}, bf16[32,2,32,128]{3,2,1,0:T(8,128)(2,1)}, u32[]{:S(2)}) copy-start(bf16[32,2,32,128]{3,2,1,0:T(8,128)(2,1)} %all_to_all.45.refs_5_) | copy-start | bytes 1572868
  106.2 18.5 %all-to-all-start.1 = ((bf16[8,2,128,128]{3,2,1,0:T(8,128)(2,1)}), bf16[8,2,128,128]{3,2,1,0:T(8,128)(2,1)S(1)}, u32[]{:S(2)}, u32[]{:S(2)}) async-start(bf16[8,2,128,128]{3,2,1,0:T(8,128)(2,1)} %get-tuple-element.30), calls=%async_computation.1 | async-start | bytes 1048576 | tf_op jit(solution)/shard_map/all_to_all | solution.py:253
  115.1 1.0 copy-start.13
  116.2 1.0 copy-start.15
  123.0 0.8 copy-start.10
  124.6 17.9 %all-to-all-start.3 = ((bf16[8,2,128,128]{3,2,1,0:T(8,128)(2,1)}), bf16[8,2,128,128]{3,2,1,0:T(8,128)(2,1)S(1)}, u32[]{:S(2)}, u32[]{:S(2)}) async-start(bf16[8,2,128,128]{3,2,1,0:T(8,128)(2,1)} %get-tuple-element.35), calls=%async_computation.3 | async-start | bytes 1048576 | tf_op jit(solution)/shard_map/all_to_all | solution.py:253
  128.9 1.0 copy-start.11
  141.7 0.8 copy-start.4
  169.4 80.0 %all-to-all-start.5 = ((bf16[8,2,128,128]{3,2,1,0:T(8,128)(2,1)}), bf16[8,2,128,128]{3,2,1,0:T(8,128)(2,1)S(1)}, u32[]{:S(2)}, u32[]{:S(2)}) async-start(bf16[8,2,128,128]{3,2,1,0:T(8,128)(2,1)} %get-tuple-element.40), calls=%async_computation.5 | async-start | bytes 1048576 | tf_op jit(solution)/shard_map/all_to_all | solution.py:253

commit v2 on v1

v2 whole, which is shorter than its diff:
```python
import functools
import math

import jax
import jax.numpy as jnp
from jax import lax
from jax.experimental import pallas as pl
from jax.experimental.pallas import tpu as pltpu
from jax.sharding import PartitionSpec as P

WIDTH = 128
SLOT = 1024
TILE = 256
REACH = 512
CHUNKS = (3, 1)
EPSILON = 1e-06
NEG_FILL = -1e30
SCALE = 1.0 / math.sqrt(WIDTH)
BF = jnp.bfloat16
F32 = jnp.float32


def rms(rows):
    values = rows.astype(F32)
    inverse = lax.rsqrt(jnp.mean(values * values, axis=-1, keepdims=True) + EPSILON)
    return values * inverse, inverse


def unnormalize(grad_normed, gain, normed, inverse):
    grad_hat = grad_normed * gain
    inner = jnp.mean(grad_hat * normed, axis=-1, keepdims=True)
    return inverse * (grad_hat - normed * inner)


def dot(a, b):
    return jnp.dot(a, b, preferred_element_type=F32)


def dot_t(a, b):
    return lax.dot_general(a, b, (((1,), (1,)), ((), ())), preferred_element_type=F32)


def identity(size):
    row = lax.broadcasted_iota(jnp.int32, (size, size), 0)
    col = lax.broadcasted_iota(jnp.int32, (size, size), 1)
    return (row == col).astype(F32).astype(BF)


def start_all(copies):
    for copy in copies:
        copy.start()


def wait_all(copies):
    for copy in copies:
        copy.wait()


def pack(pieces, owners, *refs):
    *arrays, out, stage, in_sems, out_sems = refs
    seqs = stage.shape[0]
    groups = in_sems.shape[0]
    span = seqs // groups
    loads = [
        [
            pltpu.make_async_copy(
                ref.at[pl.ds(g * span, span), :, pl.ds(at, size)],
                stage.at[pl.ds(g * span, span), :, pl.ds(to, size)],
                in_sems.at[g, n],
            )
            for n, (ref, (at, to, size)) in enumerate(zip(arrays, pieces))
        ]
        for g in range(groups)
    ]
    for group in loads:
        start_all(group)
    stores = []
    for g, group in enumerate(loads):
        wait_all(group)
        for s in range(g * span, (g + 1) * span):
            stores.append(pltpu.make_async_copy(stage.at[s], out.at[owners[s]], out_sems.at[s]))
            stores[-1].start()
    wait_all(stores)


def my_place():
    head = lax.axis_index("head")
    return head // 2, lax.rem(head, 2)


def attend(heads, first, last, *refs):
    refs = list(refs)
    owners, lengths, docs, q_gain, k_gain, kv_hbm = refs[:6]
    del refs[:6]
    own_hbm = kv_hbm if first else refs.pop(0)
    if not first:
        carry_in = refs[:6]
        del refs[:6]
    outs = refs[:8]
    del refs[:8]
    if last:
        sums = refs.pop(0)
    else:
        carry_out = refs[:6]
        del refs[:6]
    kv, own, send, kn, knt, vt, dk, dv, q_acc, in_sems, carry_sems, out_sem = refs
    kept = (kn, knt, vt, dk, dv, q_acc)

    def column(n):
        return pl.ds(n * WIDTH, WIDTH)

    base = kv_hbm.shape[2] // WIDTH - 2
    kv_in = [
        pltpu.make_async_copy(kv_hbm.at[:, :, column(base + n)], kv.at[n], in_sems.at[n])
        for n in range(2)
    ]
    own_in = [
        pltpu.make_async_copy(own_hbm.at[:, :, column(n)], own.at[n], in_sems.at[n + 2])
        for n in (m for h in range(heads) for m in (h, heads + h))
    ]
    start_all(kv_in + own_in)
    if not first:
        carry = [
            pltpu.make_async_copy(a, b, carry_sems.at[n])
            for n, (a, b) in enumerate(zip(carry_in, kept))
        ]
        start_all(carry)

    eye = identity(WIDTH)
    eye_tile = identity(TILE)

    def rows(ref, slot, at, size):
        return ref[slot, at // 32 : (at + size) // 32].reshape(size, WIDTH)

    mine = jnp.int32(0)
    for s in range(owners.shape[0]):
        mine = jnp.where(owners[s] == lax.axis_index("dp"), s, mine)
    length = lengths[mine]
    doc_row = docs[pl.ds(mine, 1)]
    start = jnp.zeros_like(doc_row)
    for d in range(8):
        count = jnp.sum((doc_row == d).astype(jnp.int32), axis=1, keepdims=True)
        start = start + jnp.where(doc_row > d, count, 0)
    gain = jnp.broadcast_to(q_gain[...], (TILE, WIDTH)).T
    y, c = my_place()
    if first:
        dk[...] = jnp.zeros_like(dk)
        dv[...] = jnp.zeros_like(dv)
        q_acc[...] = jnp.zeros_like(q_acc)
        wait_all(kv_in)
        for at in range(0, SLOT, TILE):
            part = pl.ds(at, TILE)
            normed = (rms(rows(kv, 0, at, TILE))[0] * k_gain[...]).astype(BF)
            kn[part] = normed
            knt[:, part] = dot_t(eye, normed).astype(BF)
            vt[:, part] = dot_t(eye, rows(kv, 1, at, TILE)).astype(BF)
    else:
        wait_all(kv_in + carry)
    wait_all(own_in)
    u_rel = lax.broadcasted_iota(jnp.int32, (TILE, TILE), 0)
    t_rel = lax.broadcasted_iota(jnp.int32, (1, TILE), 1)

    def copies_out(n):
        cols = pl.ds(pl.multiple_of(n * WIDTH, WIDTH), WIDTH)
        return [
            pltpu.make_async_copy(
                send.at[lax.rem(y + r // 2, 4), c ^ (r % 2), :, cols], out.at[:, cols], out_sem.at[r]
            )
            for r, out in enumerate(outs)
        ]

    def one_head(h):
        for t0 in range(0, SLOT, TILE):
            u_list = [u for u in range(0, t0 + 1, TILE) if t0 - (u + TILE - 1) < REACH]
            q_t = dot_t(eye, rows(own, h, t0, TILE))
            g_t = dot_t(eye, rows(own, heads + h, t0, TILE))
            g_b = g_t.astype(BF)
            q_inv = lax.rsqrt(jnp.mean(q_t * q_t, axis=0, keepdims=True) + EPSILON)
            q_hat = q_t * q_inv
            q_n = (q_hat * gain).astype(BF)
            starts = start[:, t0 : t0 + TILE]
            scores = [dot(kn[pl.ds(u0, TILE)], q_n) for u0 in u_list]
            grads = [dot(rows(kv, 1, u0, TILE), g_b) for u0 in u_list]
            masked = []
            for u0, s in zip(u_list, scores):
                allowed = u_rel >= starts - u0
                if u0 == t0:
                    allowed = allowed & (u_rel <= t_rel)
                masked.append(jnp.where(allowed, s * (SCALE * math.log2(math.e)), NEG_FILL))
            largest = functools.reduce(
                jnp.maximum, [jnp.max(s, axis=0, keepdims=True) for s in masked]
            )
            weights = [jnp.exp2(s - largest) for s in masked]
            total = sum(jnp.sum(w, axis=0, keepdims=True) for w in weights)
            factor = jnp.where(t_rel + t0 < length, 1.0 / jnp.maximum(total, 1.0), 0.0)
            probs = [w * factor for w in weights]
            low = [p.astype(BF) for p in probs]
            o_t = sum(dot(vt[:, pl.ds(u0, TILE)], p) for u0, p in zip(u_list, low))
            delta = jnp.sum(g_t * o_t, axis=0, keepdims=True)
            dq_t = 0.0
            for u0, p, pb, dp in zip(u_list, probs, low, grads):
                part = pl.ds(u0, TILE)
                dv[part] += dot_t(pb, g_b)
                ds = (p * (dp - delta)).astype(BF)
                dk[part] += dot_t(ds, q_n)
                dq_t += dot(knt[:, part], ds)
            dq_t = dq_t * SCALE
            q_acc[...] += dq_t * q_hat
            grad_hat = dq_t * gain
            inner = jnp.mean(grad_hat * q_hat, axis=0, keepdims=True)
            dq = (q_inv * (grad_hat - q_hat * inner)).astype(BF)
            o = dot_t(eye_tile, o_t.astype(BF)).astype(BF)
            dq = dot_t(eye_tile, dq).astype(BF)
            for n in range(TILE // WIDTH):
                for to, block in ((h, o), (heads + h, dq)):
                    cols = pl.ds(pl.multiple_of(to * WIDTH, WIDTH), WIDTH)
                    send[t0 // TILE, n, :, cols] = block[n * WIDTH : (n + 1) * WIDTH]
        start_all(copies_out(h) + copies_out(heads + h))

    def finish():
        k_sum = jnp.zeros((1, WIDTH), F32)
        for at in range(0, SLOT, WIDTH):
            part = pl.ds(at, WIDTH)
            k_hat, k_inv = rms(rows(kv, 0, at, WIDTH))
            gk = dk[part] * SCALE
            k_sum += jnp.sum(gk * k_hat, axis=0, keepdims=True)
            block = at // TILE, at // WIDTH % 2, slice(None)
            grad_k = unnormalize(gk, k_gain[...], k_hat, k_inv).astype(BF)
            send[(*block, column(2 * heads))] = grad_k
            send[(*block, column(2 * heads + 1))] = dv[part].astype(BF)
        start_all(copies_out(2 * heads) + copies_out(2 * heads + 1))
        q_sum = jnp.sum(q_acc[...], axis=1, keepdims=True)
        sums[0:1] = jnp.broadcast_to(q_sum, (WIDTH, WIDTH)).T[0:1]
        sums[1:2] = k_sum

    if heads == 1:
        one_head(0)
    else:
        pl.loop(0, heads)(one_head)
    if last:
        finish()
    else:
        carry = [
            pltpu.make_async_copy(b, a, carry_sems.at[n])
            for n, (a, b) in enumerate(zip(carry_out, kept))
        ]
        start_all(carry)
        wait_all(carry)
    for r, out in enumerate(outs):
        pltpu.make_async_copy(out, out, out_sem.at[r]).wait()


def place(at, *refs):
    refs = list(refs)
    stage, in_sems, out_sems = refs[-3:]
    received, outs = refs[:8], refs[-7:-3]
    y, c = my_place()
    columns = outs[0].shape[2] // (8 * WIDTH) * WIDTH
    count = 2 if at == 0 else 4
    per = received[0].shape[1] // count
    loads = [
        pltpu.make_async_copy(ref, stage.at[r], in_sems.at[r]) for r, ref in enumerate(received)
    ]
    start_all(loads)
    stores = []
    for r, load in enumerate(loads):
        load.wait()
        src = lax.rem(y + 4 - r // 2, 4) * 2 + (c ^ (r % 2))
        for n in range(count):
            start = src * columns + at if n < 2 else src * WIDTH
            stores.append(
                pltpu.make_async_copy(
                    stage.at[r, :, pl.ds(n * per, per)],
                    outs[n].at[0, :, pl.ds(pl.multiple_of(start, WIDTH), per)],
                    out_sems.at[r, n],
                )
            )
            stores[-1].start()
    wait_all(stores)


HBM = pl.BlockSpec(memory_space=pltpu.HBM)
VMEM = pl.BlockSpec(memory_space=pltpu.VMEM)
SMEM = pl.BlockSpec(memory_space=pltpu.SMEM)


def call(kernel, args, in_specs, outs, out_specs, scratch=(), name=None, flops=0, aliases=None):
    moved = sum(math.prod(a.shape) * a.dtype.itemsize for a in (*args, *outs))
    return pl.pallas_call(
        kernel,
        out_shape=outs,
        in_specs=in_specs,
        out_specs=out_specs,
        scratch_shapes=scratch,
        input_output_aliases=aliases or {},
        compiler_params=pltpu.CompilerParams(vmem_limit_bytes=60 * 1024 * 1024),
        cost_estimate=pl.CostEstimate(flops=flops, bytes_accessed=moved, transcendentals=0),
        name=name,
    )(*args)


def shape(dims, dtype=BF):
    return jax.ShapeDtypeStruct(dims, dtype)


def attend_chunk(heads, first, last, owners, lengths, docs, q_gain, k_gain, kv, own, carry):
    args = [owners, lengths, docs, q_gain, k_gain, kv]
    if not first:
        args += [own, *carry]
    width = (2 * heads + (2 if last else 0)) * WIDTH
    outs = [shape((WIDTH, width))] * 8
    kept = [
        ((SLOT, WIDTH), BF),
        ((WIDTH, SLOT), BF),
        ((WIDTH, SLOT), BF),
        ((SLOT, WIDTH), F32),
        ((SLOT, WIDTH), F32),
        ((WIDTH, TILE), F32),
    ]
    per_src = kv.shape[1]
    scratch = [
        pltpu.VMEM((2, SLOT // per_src, per_src, WIDTH), BF),
        pltpu.VMEM((2 * heads, SLOT // per_src, per_src, WIDTH), BF),
        pltpu.VMEM((4, 2, WIDTH, width), BF),
        *(pltpu.VMEM(*a) for a in kept),
        pltpu.SemaphoreType.DMA((2 + 2 * heads,)),
        pltpu.SemaphoreType.DMA((len(kept),)),
        pltpu.SemaphoreType.DMA((8,)),
    ]
    outs += [shape((2, WIDTH), F32)] if last else [shape(*a) for a in kept]
    result = call(
        functools.partial(attend, heads, first, last),
        args,
        [SMEM, SMEM, VMEM, VMEM, VMEM] + [HBM] * (len(args) - 5),
        outs,
        [HBM] * 8 + ([VMEM] if last else [HBM] * len(kept)),
        scratch,
        "attend",
        heads * 12 * 9 * TILE * TILE * WIDTH,
    )
    return result[:8], result[8:]


def across(r):
    return [(i, ((i // 2 + r // 2) % 4) * 2 + ((i % 2) ^ (r % 2))) for i in range(8)]


def packed_chunk(owners, arrays, pieces, name):
    seqs, per_src, _ = arrays[0].shape
    width = sum(p[2] for p in pieces)
    return call(
        functools.partial(pack, pieces),
        [owners, *arrays],
        [SMEM] + [HBM] * len(arrays),
        [shape((seqs, per_src, width))],
        [HBM],
        [
            pltpu.VMEM((seqs, per_src, width), BF),
            pltpu.SemaphoreType.DMA((4, len(pieces))),
            pltpu.SemaphoreType.DMA((seqs,)),
        ],
        name,
    )[0]


def total(sums, axis):
    spread = jnp.broadcast_to(sums, (lax.axis_size(axis), *sums.shape))
    return jnp.sum(lax.all_to_all(spread, axis, 0, 0, tiled=True), axis=0)


def per_device(query, key, value, grad, q_gain, k_gain, lengths, owners, doc_ids):
    seqs, _, features = query.shape
    heads = features // WIDTH
    head_devs = lax.axis_size("head")
    cut, rest = CHUNKS[0] * WIDTH, CHUNKS[1] * WIDTH
    front = packed_chunk(
        owners,
        [query, grad, key, value],
        [(0, 0, cut), (0, cut, cut), (0, 2 * cut, WIDTH), (0, 2 * cut + WIDTH, WIDTH)],
        "pack_front",
    )
    back = packed_chunk(owners, [query, grad], [(cut, 0, rest), (cut, rest, rest)], "pack_back")
    front = lax.all_to_all(front, "dp", 0, 0, tiled=True)
    front, back = lax.optimization_barrier((front, back))
    back = lax.all_to_all(back, "dp", 0, 0, tiled=True)

    small = (owners, lengths, doc_ids, q_gain.reshape(1, WIDTH), k_gain.reshape(1, WIDTH))
    out, carry = attend_chunk(CHUNKS[0], True, False, *small, front, None, None)
    early = [out[0]] + [lax.ppermute(out[r], "head", across(r)) for r in range(1, 8)]
    out, (sums,) = attend_chunk(CHUNKS[1], False, True, *small, front, back, carry)
    late = [out[0]] + [lax.ppermute(out[r], "head", across(r)) for r in range(1, 8)]
    sums, late = lax.optimization_barrier((total(sums, "dp"), late))
    sums = total(sums, "head")
    wide, narrow = shape((1, WIDTH, heads * head_devs * WIDTH)), shape((1, WIDTH, head_devs * WIDTH))
    outs = None
    for at, got in ((0, early), (cut, late)):
        outs = call(
            functools.partial(place, at),
            [*got, *(outs or [])],
            [HBM] * (8 + len(outs or [])),
            [wide, wide, narrow, narrow],
            [HBM] * 4,
            [
                pltpu.VMEM((8, *got[0].shape), BF),
                pltpu.SemaphoreType.DMA((8,)),
                pltpu.SemaphoreType.DMA((8, 4)),
            ],
            "place",
            aliases={8 + n: n for n in range(4)} if outs else None,
        )
    tokens = seqs * SLOT
    return (
        *outs,
        sums[0] / math.sqrt(tokens * heads * head_devs),
        sums[1] / math.sqrt(tokens * head_devs),
    )


def solution(mesh):
    spread = P(None, "dp", "head")
    packed = P("dp", "head", None)
    return jax.shard_map(
        per_device,
        mesh=mesh,
        in_specs=(spread,) * 4 + (P(),) * 5,
        out_specs=(packed,) * 4 + (P(),) * 2,
        check_vma=False,
    )
```

time: 253 us -> 154 us (0.61)
  blocking collectives: 162 us -> 18.1 us
  waiting for transfers between devices: 17.5 us -> 52.6 us
  starting transfers between devices: 30 us -> 40.6 us
  Pallas kernels: 27.8 us -> 38.2 us
  local copies, waits for them, and re-layouts: 10.7 us -> 3.01 us
    psum x1 -> x0, blocking collectives: 75 us -> none  [per_device(): sums = lax.psum(sums, ('dp', 'head'))]
    all_to_all x4 -> x1, blocking collectives: 86.7 us -> 18.1 us  [total(): return jnp.sum(lax.all_to_all(spread, axis, 0, 0, tiled=True), axis=0)]
    all_to_all x5 -> x3, waiting for transfers between devices: 17.5 us -> 45.7 us  [the longest x1 45.7 us: per_device(): front = lax.all_to_all(front, 'dp', 0, 0, tiled=True)]
    ppermute x0 -> x14, starting transfers between devices: none -> 17.4 us  [per_device(): lax.ppermute(out[r], 'head', across(r))]
    pallas_call x7 -> x6, Pallas kernels: 27.8 us -> 38.2 us  [call(): pl.pallas_call(kernel, out_shape=outs, in_specs=in_specs, out_specs=out_s...]
    unnamed x34 -> x42, local copies, waits for them, and re-layouts: 8.7 us -> 1.74 us
    ppermute x0 -> x14, waiting for transfers between devices: none -> 6.84 us  [per_device(): lax.ppermute(out[r], 'head', across(r))]
    all_to_all x5 -> x3, starting transfers between devices: 30 us -> 23.1 us  [the longest x1 11.9 us: per_device(): front = lax.all_to_all(front, 'dp', 0, 0, tiled=True)]
  transfers between devices with their start and end apart: 5 -> 17, of which waited for: 3 -> 5; matrix products, arithmetic and copies ran while one was open for 1% -> 1% of each run, Pallas kernels for 9% -> 22%
where the time goes in v2:
time: 154 us
  waiting for transfers between devices  52.6 us (34%)
  starting transfers between devices  40.6 us (26%)
  Pallas kernels  38.2 us (25%)
  blocking collectives  18.1 us (12%)
  local copies, waits for them, and re-layouts  3.01 us (2%)
    all_to_all x1, waiting for transfers between devices, per_device(): front = lax.all_to_all(front, 'dp', 0, 0, tiled=True)  45.7 us
    pallas_call x6, Pallas kernels, call(): pl.pallas_call(kernel, out_shape=outs, in_specs=in_specs, out_specs=out_s...  38.2 us
    all_to_all x1, blocking collectives, total(): return jnp.sum(lax.all_to_all(spread, axis, 0, 0, tiled=True), axis=0)  18.1 us
    ppermute x14, starting transfers between devices, per_device(): lax.ppermute(out[r], 'head', across(r))  17.4 us
    all_to_all x1, starting transfers between devices, per_device(): front = lax.all_to_all(front, 'dp', 0, 0, tiled=True)  11.9 us
    ppermute x14, waiting for transfers between devices, per_device(): lax.ppermute(out[r], 'head', across(r))  6.84 us
    all_to_all x1, starting transfers between devices, per_device(): back = lax.all_to_all(back, 'dp', 0, 0, tiled=True)  6.61 us
    all_to_all x1, starting transfers between devices, total(): return jnp.sum(lax.all_to_all(spread, axis, 0, 0, tiled=True), axis=0)  4.65 us
  transfers between devices with their start and end apart: 17, of which 5 were waited for; matrix products, arithmetic and copies ran while one was open for 1% of the time, Pallas kernels for 22%

profile of v2, /device:TPU:1, one launch (start us, length us, event | category | flops | bytes accessed | tf_op | source)
XLA Modules:
  0.0 153.9 jit_solution(6205002180759356012)
XLA Ops:
  0.6 3.5 %pack_front.1 = bf16[32,32,1024]{2,1,0:T(8,128)(2,1)} custom-call(s32[32]{0:T(128)} %refs_0_.7, bf16[32,32,512]{2,1,0:T(8,128)(2,1)} %refs_0_.5, bf16[32,32,512]{2,1,0:T(8,128)(2,1)} %refs_1_.5, bf16[32,32,128]{2,1,0:T(8,128)(2,1)} %refs_2_.3, bf16[32,32,128]{2,1,0:T(8,128)(2,1)} %refs_3_.1), custom_call_target="tpu_custom_call" | custom-call | bytes 4718720 | tf_op jit(solution)/shard_map/pack_front/pallas_call | solution.py:289
  4.2 11.9 %all-to-all-start = ((bf16[32,32,1024]{2,1,0:T(8,128)(2,1)}), bf16[32,32,1024]{2,1,0:T(8,128)(2,1)S(1)}, u32[]{:S(2)}, u32[]{:S(2)}) async-start(bf16[32,32,1024]{2,1,0:T(8,128)(2,1)} %pack_front.1), calls=%async_computation | async-start | bytes 4194304 | tf_op jit(solution)/shard_map/all_to_all | solution.py:383
  16.1 2.7 %pack_back.1 = bf16[32,32,256]{2,1,0:T(8,128)(2,1)} custom-call(s32[32]{0:T(128)} %refs_0_.7, bf16[32,32,512]{2,1,0:T(8,128)(2,1)} %refs_0_.5, bf16[32,32,512]{2,1,0:T(8,128)(2,1)} %refs_1_.5), custom_call_target="tpu_custom_call" | custom-call | bytes 2621568 | tf_op jit(solution)/shard_map/pack_back/pallas_call | solution.py:289
  18.8 45.7 %all-to-all-done.refs_5_ = bf16[32,32,1024]{2,1,0:T(8,128)(2,1)S(1)} async-done(((bf16[32,32,1024]{2,1,0:T(8,128)(2,1)}), bf16[32,32,1024]{2,1,0:T(8,128)(2,1)S(1)}, u32[]{:S(2)}, u32[]{:S(2)}) %all-to-all-start) | async-done | bytes 2097184 | tf_op jit(solution)/shard_map/all_to_all | solution.py:383
  64.5 6.6 %all-to-all-start.1 = ((bf16[32,32,256]{2,1,0:T(8,128)(2,1)}), bf16[32,32,256]{2,1,0:T(8,128)(2,1)S(1)}, u32[]{:S(2)}, u32[]{:S(2)}) async-start(bf16[32,32,256]{2,1,0:T(8,128)(2,1)} %pack_back.1), calls=%async_computation.1 | async-start | bytes 1048576 | tf_op jit(solution)/shard_map/all_to_all | solution.py:385
  71.2 0.0 copy-done
  71.2 17.9 %attend.2 = (bf16[128,768]{1,0:T(8,128)(2,1)}, bf16[128,768]{1,0:T(8,128)(2,1)}, bf16[128,768]{1,0:T(8,128)(2,1)}, bf16[128,768]{1,0:T(8,128)(2,1)}, bf16[128,76...) custom-call(s32[32]{0:T(128)} %refs_0_.7, ...), custom_call_target="tpu_custom_call" | custom-call | flops 2717908992 | bytes 5768448 | tf_op jit(solution)/shard_map/attend/pallas_call | solution.py:289
  89.1 2.0 %collective-permute-start.7 = (bf16[128,768]{1,0:T(8,128)(2,1)}, bf16[128,768]{1,0:T(8,128)(2,1)S(1)}, u32[]{:S(2)}, u32[]{:S(2)}) collective-permute-start(bf16[128,768]{1,0:T(8,128)(2,1)} %get-tuple-element.74), channel_id=1, source_target_pairs={{0,1},{1,0},{2,3},{3,2},{4,5},{5,4},{6,7},{7,6},{8,9},{9,8},{10,11... | collective-permute-start | bytes 589832 | tf_op jit(solution)/shard_map/ppermute | solution.py:389
  91.1 1.3 collective-permute-start.8
  92.5 0.0 all-to-all-done.1.refs_6_
  92.5 0.8 copy-done.1
  93.3 0.0 copy-start.16
  93.3 9.2 %attend.3 = (bf16[128,512]{1,0:T(8,128)(2,1)}, bf16[128,512]{1,0:T(8,128)(2,1)}, bf16[128,512]{1,0:T(8,128)(2,1)}, bf16[128,512]{1,0:T(8,128)(2,1)}, bf16[128,51...) custom-call(s32[32]{0:T(128)} %refs_0_.7, ...), custom_call_target="tpu_custom_call" | custom-call | flops 905969664 | bytes 5769472 | tf_op jit(solution)/shard_map/attend/pallas_call | solution.py:289
  102.5 0.4 collective-permute-start
  102.9 1.3 collective-permute-start.1
  104.2 1.4 collective-permute-start.2
  105.6 0.0 collective-permute-done.7.refs_1_
  105.6 1.6 %collective-permute-start.3 = (bf16[128,512]{1,0:T(8,128)(2,1)}, bf16[128,512]{1,0:T(8,128)(2,1)S(1)}, u32[]{:S(2)}, u32[]{:S(2)}) collective-permute-start(bf16[128,512]{1,0:T(8,128)(2,1)} %get-tuple-element.61), channel_id=1, source_target_pairs={{0,4},{1,5},{2,6},{3,7},{4,0},{5,1},{6,2},{7,3},{8,12},{9,13},{10,... | collective-permute-start | bytes 393224 | tf_op jit(solution)/shard_map/ppermute | solution.py:391
  107.2 0.0 collective-permute-done.8.refs_2_
  107.2 1.5 collective-permute-start.4
  108.7 0.0 collective-permute-done.refs_1_
  108.7 1.7 %collective-permute-start.5 = (bf16[128,512]{1,0:T(8,128)(2,1)}, bf16[128,512]{1,0:T(8,128)(2,1)S(1)}, u32[]{:S(2)}, u32[]{:S(2)}) collective-permute-start(bf16[128,512]{1,0:T(8,128)(2,1)} %get-tuple-element.63), channel_id=1, source_target_pairs={{0,6},{1,7},{2,0},{3,1},{4,2},{5,3},{6,4},{7,5},{8,14},{9,15},{10,... | collective-permute-start | bytes 393224 | tf_op jit(solution)/shard_map/ppermute | solution.py:391
  110.4 0.0 collective-permute-done.1.refs_2_
  110.4 0.6 collective-permute-start.6
  111.0 2.2 %collective-permute-done.2.refs_3_ = bf16[128,512]{1,0:T(8,128)(2,1)S(1)} collective-permute-done((bf16[128,512]{1,0:T(8,128)(2,1)}, bf16[128,512]{1,0:T(8,128)(2,1)S(1)}, u32[]{:S(2)}, u32[]{:S(2)}) %collective-permute-start.2) | collective-permute-done | bytes 131104 | tf_op jit(solution)/shard_map/ppermute | solution.py:391
  113.3 0.0 copy-done.20
  113.3 0.0 collective-permute-start.9
  113.3 1.5 collective-permute-done.3.refs_4_
  114.8 0.0 copy-done.19
  114.8 1.6 %collective-permute-start.10 = (bf16[128,768]{1,0:T(8,128)(2,1)S(1)}, bf16[128,768]{1,0:T(8,128)(2,1)S(1)}, u32[]{:S(2)}, u32[]{:S(2)}) collective-permute-start(bf16[128,768]{1,0:T(8,128)(2,1)S(1)} %copy-done.19), channel_id=1, source_target_pairs={{0,4},{1,5},{2,6},{3,7},{4,0},{5,1},{6,2},{7,3},{8,12},{9,13},{10,... | collective-permute-start | bytes 589832 | tf_op jit(solution)/shard_map/ppermute | solution.py:389
  116.4 2.2 %collective-permute-done.4.refs_5_ = bf16[128,512]{1,0:T(8,128)(2,1)S(1)} collective-permute-done((bf16[128,512]{1,0:T(8,128)(2,1)}, bf16[128,512]{1,0:T(8,128)(2,1)S(1)}, u32[]{:S(2)}, u32[]{:S(2)}) %collective-permute-start.4) | collective-permute-done | bytes 131104 | tf_op jit(solution)/shard_map/ppermute | solution.py:391
  118.6 0.0 copy-done.18
  118.6 1.1 collective-permute-start.11
  119.7 0.0 collective-permute-done.5.refs_6_
  119.7 0.0 copy-done.17
  119.7 0.4 collective-permute-start.12
  120.1 0.9 collective-permute-done.6.refs_7_
  121.0 0.0 copy-done.16
  121.0 2.4 %collective-permute-start.13 = (bf16[128,768]{1,0:T(8,128)(2,1)S(1)}, bf16[128,768]{1,0:T(8,128)(2,1)S(1)}, u32[]{:S(2)}, u32[]{:S(2)}) collective-permute-start(bf16[128,768]{1,0:T(8,128)(2,1)S(1)} %copy-done.16), channel_id=1, source_target_pairs={{0,7},{1,6},{2,1},{3,0},{4,3},{5,2},{6,5},{7,4},{8,15},{9,14},{10,... | collective-permute-start | bytes 589832 | tf_op jit(solution)/shard_map/ppermute | solution.py:389
  123.4 0.7 broadcast_in_dim.6
  124.1 18.1 %all_to_all.20 = f32[32,2,128]{2,1,0:T(2,128)S(1)} all-to-all(f32[32,2,128]{2,1,0:T(2,128)S(1)} %broadcast_in_dim.6), channel_id=1, replica_groups=mesh['dp'=32,'head'=8] {'dp'}, dimensions={0} | all-to-all | bytes 65536 | tf_op jit(solution)/shard_map/all_to_all | solution.py:368
  142.2 0.6 broadcast_in_dim.7
  142.8 4.6 %all-to-all-start.3 = ((f32[8,2,128]{2,1,0:T(2,128)}), f32[8,2,128]{2,1,0:T(2,128)S(1)}, u32[]{:S(2)}, u32[]{:S(2)}) async-start(f32[8,2,128]{2,1,0:T(2,128)} %broadcast_in_dim.7), calls=%async_computation.3 | async-start | bytes 16384 | tf_op jit(solution)/shard_map/all_to_all | solution.py:368
  147.4 0.0 collective-permute-done.9.refs_3_
  147.4 0.0 collective-permute-done.10.refs_4_
  147.4 0.0 copy-start.5
  147.5 0.0 collective-permute-done.11.refs_5_
  147.5 0.0 copy-start.6
  147.5 0.0 collective-permute-done.12.refs_6_
  147.5 0.0 copy-start.7
  147.5 0.0 collective-permute-done.13.refs_7_
  147.5 0.0 copy-start.8
  147.5 0.0 copy-done.2
  147.5 0.0 copy-done.3
  147.5 0.6 copy-done.4
  148.1 0.1 copy-done.5
  148.2 0.1 copy-done.6
  148.3 0.1 copy-done.7
  148.4 0.1 copy-done.8
  148.4 2.5 %place.2 = (bf16[1,128,4096]{2,1,0:T(8,128)(2,1)}, bf16[1,128,4096]{2,1,0:T(8,128)(2,1)}, bf16[1,128,1024]{2,1,0:T(8,128)(2,1)}, bf16[1,128,1024]{2,1,0:T(8,128)(2,1)}) custom-call(bf16[128,768]{1,0:T(8,128)(2,1)} %get-tuple-element.73.refs_0_, bf16[128,768]{1,0:T(8,128)(2,1)} %copy-done.2, bf16[128,768]{1,0:T(8,128)(2,1)} %copy-done.3, ...), custom_call_target="tpu_custom_call" | custom-call | bytes 4194304 | tf_op jit(solution)/shard_map/place/pallas_call | solution.py:289
  150.9 0.0 copy-done.9
  151.0 2.3 %place.3 = (bf16[1,128,4096]{2,1,0:T(8,128)(2,1)}, bf16[1,128,4096]{2,1,0:T(8,128)(2,1)}, bf16[1,128,1024]{2,1,0:T(8,128)(2,1)}, bf16[1,128,1024]{2,1,0:T(8,128)(2,1)}) custom-call(bf16[128,512]{1,0:T(8,128)(2,1)} %get-tuple-element.65.refs_0_, ...), custom_call_target="tpu_custom_call", output_to_operand_aliasing={{0}: (8, {}), {1}: (9, {}), {2}: (10, {}), {3}: (11, {})} | custom-call | bytes 6291456 | tf_op jit(solution)/shard_map/place/pallas_call | solution.py:289
  153.3 0.0 all-to-all-done.3
  153.3 0.5 multiply_bitcast_fusion
  (24 shorter events, 0.1 us)
Async XLA Ops:
  4.2 60.4 %all-to-all-start = ((bf16[32,32,1024]{2,1,0:T(8,128)(2,1)}), bf16[32,32,1024]{2,1,0:T(8,128)(2,1)S(1)}, u32[]{:S(2)}, u32[]{:S(2)}) async-start(bf16[32,32,1024]{2,1,0:T(8,128)(2,1)} %pack_front.1), calls=%async_computation | async-start | bytes 4194304 | tf_op jit(solution)/shard_map/all_to_all | solution.py:383
  64.5 6.6 %copy-start = (bf16[32,32,1024]{2,1,0:T(8,128)(2,1)}, bf16[32,32,1024]{2,1,0:T(8,128)(2,1)S(1)}, u32[]{:S(2)}) copy-start(bf16[32,32,1024]{2,1,0:T(8,128)(2,1)S(1)} %all-to-all-done.refs_5_) | copy-start | bytes 6291460
  64.5 27.9 %all-to-all-start.1 = ((bf16[32,32,256]{2,1,0:T(8,128)(2,1)}), bf16[32,32,256]{2,1,0:T(8,128)(2,1)S(1)}, u32[]{:S(2)}, u32[]{:S(2)}) async-start(bf16[32,32,256]{2,1,0:T(8,128)(2,1)} %pack_back.1), calls=%async_computation.1 | async-start | bytes 1048576 | tf_op jit(solution)/shard_map/all_to_all | solution.py:385
  89.1 16.5 %collective-permute-start.7 = (bf16[128,768]{1,0:T(8,128)(2,1)}, bf16[128,768]{1,0:T(8,128)(2,1)S(1)}, u32[]{:S(2)}, u32[]{:S(2)}) collective-permute-start(bf16[128,768]{1,0:T(8,128)(2,1)} %get-tuple-element.74), channel_id=1, source_target_pairs={{0,1},{1,0},{2,3},{3,2},{4,5},{5,4},{6,7},{7,6},{8,9},{9,8},{10,11... | collective-permute-start | bytes 589832 | tf_op jit(solution)/shard_map/ppermute | solution.py:389
  91.1 16.1 %collective-permute-start.8 = (bf16[128,768]{1,0:T(8,128)(2,1)}, bf16[128,768]{1,0:T(8,128)(2,1)S(1)}, u32[]{:S(2)}, u32[]{:S(2)}) collective-permute-start(bf16[128,768]{1,0:T(8,128)(2,1)} %get-tuple-element.75), channel_id=1, source_target_pairs={{0,2},{1,3},{2,4},{3,5},{4,6},{5,7},{6,0},{7,1},{8,10},{9,11},{10,... | collective-permute-start | bytes 589832 | tf_op jit(solution)/shard_map/ppermute | solution.py:389
  92.5 0.8 copy-start.1
  93.3 20.0 %copy-start.20 = (bf16[128,768]{1,0:T(8,128)(2,1)S(1)}, bf16[128,768]{1,0:T(8,128)(2,1)}, u32[]{:S(2)}) copy-start(bf16[128,768]{1,0:T(8,128)(2,1)} %get-tuple-element.76) | copy-start | bytes 589828
  93.3 21.5 %copy-start.19 = (bf16[128,768]{1,0:T(8,128)(2,1)S(1)}, bf16[128,768]{1,0:T(8,128)(2,1)}, u32[]{:S(2)}) copy-start(bf16[128,768]{1,0:T(8,128)(2,1)} %get-tuple-element.77) | copy-start | bytes 589828
  93.3 25.3 %copy-start.18 = (bf16[128,768]{1,0:T(8,128)(2,1)S(1)}, bf16[128,768]{1,0:T(8,128)(2,1)}, u32[]{:S(2)}) copy-start(bf16[128,768]{1,0:T(8,128)(2,1)} %get-tuple-element.78) | copy-start | bytes 589828
  93.3 26.5 %copy-start.17 = (bf16[128,768]{1,0:T(8,128)(2,1)S(1)}, bf16[128,768]{1,0:T(8,128)(2,1)}, u32[]{:S(2)}) copy-start(bf16[128,768]{1,0:T(8,128)(2,1)} %get-tuple-element.79) | copy-start | bytes 589828
  93.3 27.7 %copy-start.16 = (bf16[128,768]{1,0:T(8,128)(2,1)S(1)}, bf16[128,768]{1,0:T(8,128)(2,1)}, u32[]{:S(2)}) copy-start(bf16[128,768]{1,0:T(8,128)(2,1)} %get-tuple-element.80) | copy-start | bytes 589828
  102.5 6.3 %collective-permute-start = (bf16[128,512]{1,0:T(8,128)(2,1)}, bf16[128,512]{1,0:T(8,128)(2,1)S(1)}, u32[]{:S(2)}, u32[]{:S(2)}) collective-permute-start(bf16[128,512]{1,0:T(8,128)(2,1)} %get-tuple-element.58), channel_id=1, source_target_pairs={{0,1},{1,0},{2,3},{3,2},{4,5},{5,4},{6,7},{7,6},{8,9},{9,8},{10,11... | collective-permute-start | bytes 393224 | tf_op jit(solution)/shard_map/ppermute | solution.py:391
  102.9 7.5 %collective-permute-start.1 = (bf16[128,512]{1,0:T(8,128)(2,1)}, bf16[128,512]{1,0:T(8,128)(2,1)S(1)}, u32[]{:S(2)}, u32[]{:S(2)}) collective-permute-start(bf16[128,512]{1,0:T(8,128)(2,1)} %get-tuple-element.59), channel_id=1, source_target_pairs={{0,2},{1,3},{2,4},{3,5},{4,6},{5,7},{6,0},{7,1},{8,10},{9,11},{10,... | collective-permute-start | bytes 393224 | tf_op jit(solution)/shard_map/ppermute | solution.py:391
  104.2 9.1 %collective-permute-start.2 = (bf16[128,512]{1,0:T(8,128)(2,1)}, bf16[128,512]{1,0:T(8,128)(2,1)S(1)}, u32[]{:S(2)}, u32[]{:S(2)}) collective-permute-start(bf16[128,512]{1,0:T(8,128)(2,1)} %get-tuple-element.60), channel_id=1, source_target_pairs={{0,3},{1,2},{2,5},{3,4},{4,7},{5,6},{6,1},{7,0},{8,11},{9,10},{10,... | collective-permute-start | bytes 393224 | tf_op jit(solution)/shard_map/ppermute | solution.py:391
  105.6 41.9 %copy-start.2 = (bf16[128,768]{1,0:T(8,128)(2,1)}, bf16[128,768]{1,0:T(8,128)(2,1)S(1)}, u32[]{:S(2)}) copy-start(bf16[128,768]{1,0:T(8,128)(2,1)S(1)} %collective-permute-done.7.refs_1_) | copy-start | bytes 589828
  105.6 9.1 %collective-permute-start.3 = (bf16[128,512]{1,0:T(8,128)(2,1)}, bf16[128,512]{1,0:T(8,128)(2,1)S(1)}, u32[]{:S(2)}, u32[]{:S(2)}) collective-permute-start(bf16[128,512]{1,0:T(8,128)(2,1)} %get-tuple-element.61), channel_id=1, source_target_pairs={{0,4},{1,5},{2,6},{3,7},{4,0},{5,1},{6,2},{7,3},{8,12},{9,13},{10,... | collective-permute-start | bytes 393224 | tf_op jit(solution)/shard_map/ppermute | solution.py:391
  107.2 40.3 %copy-start.3 = (bf16[128,768]{1,0:T(8,128)(2,1)}, bf16[128,768]{1,0:T(8,128)(2,1)S(1)}, u32[]{:S(2)}) copy-start(bf16[128,768]{1,0:T(8,128)(2,1)S(1)} %collective-permute-done.8.refs_2_) | copy-start | bytes 589828
  107.2 11.4 %collective-permute-start.4 = (bf16[128,512]{1,0:T(8,128)(2,1)}, bf16[128,512]{1,0:T(8,128)(2,1)S(1)}, u32[]{:S(2)}, u32[]{:S(2)}) collective-permute-start(bf16[128,512]{1,0:T(8,128)(2,1)} %get-tuple-element.62), channel_id=1, source_target_pairs={{0,5},{1,4},{2,7},{3,6},{4,1},{5,0},{6,3},{7,2},{8,13},{9,12},{10,... | collective-permute-start | bytes 393224 | tf_op jit(solution)/shard_map/ppermute | solution.py:391
  108.7 42.2 %copy-start.9 = (bf16[128,512]{1,0:T(8,128)(2,1)}, bf16[128,512]{1,0:T(8,128)(2,1)S(1)}, u32[]{:S(2)}) copy-start(bf16[128,512]{1,0:T(8,128)(2,1)S(1)} %collective-permute-done.refs_1_) | copy-start | bytes 393220
  108.7 11.0 %collective-permute-start.5 = (bf16[128,512]{1,0:T(8,128)(2,1)}, bf16[128,512]{1,0:T(8,128)(2,1)S(1)}, u32[]{:S(2)}, u32[]{:S(2)}) collective-permute-start(bf16[128,512]{1,0:T(8,128)(2,1)} %get-tuple-element.63), channel_id=1, source_target_pairs={{0,6},{1,7},{2,0},{3,1},{4,2},{5,3},{6,4},{7,5},{8,14},{9,15},{10,... | collective-permute-start | bytes 393224 | tf_op jit(solution)/shard_map/ppermute | solution.py:391
  110.4 40.5 %copy-start.10 = (bf16[128,512]{1,0:T(8,128)(2,1)}, bf16[128,512]{1,0:T(8,128)(2,1)S(1)}, u32[]{:S(2)}) copy-start(bf16[128,512]{1,0:T(8,128)(2,1)S(1)} %collective-permute-done.1.refs_2_) | copy-start | bytes 393220
  110.4 10.5 %collective-permute-start.6 = (bf16[128,512]{1,0:T(8,128)(2,1)}, bf16[128,512]{1,0:T(8,128)(2,1)S(1)}, u32[]{:S(2)}, u32[]{:S(2)}) collective-permute-start(bf16[128,512]{1,0:T(8,128)(2,1)} %get-tuple-element.64), channel_id=1, source_target_pairs={{0,7},{1,6},{2,1},{3,0},{4,3},{5,2},{6,5},{7,4},{8,15},{9,14},{10,... | collective-permute-start | bytes 393224 | tf_op jit(solution)/shard_map/ppermute | solution.py:391
  113.3 37.7 %copy-start.11 = (bf16[128,512]{1,0:T(8,128)(2,1)}, bf16[128,512]{1,0:T(8,128)(2,1)S(1)}, u32[]{:S(2)}) copy-start(bf16[128,512]{1,0:T(8,128)(2,1)S(1)} %collective-permute-done.2.refs_3_) | copy-start | bytes 393220
  113.3 34.1 %collective-permute-start.9 = (bf16[128,768]{1,0:T(8,128)(2,1)S(1)}, bf16[128,768]{1,0:T(8,128)(2,1)S(1)}, u32[]{:S(2)}, u32[]{:S(2)}) collective-permute-start(bf16[128,768]{1,0:T(8,128)(2,1)S(1)} %copy-done.20), channel_id=1, source_target_pairs={{0,3},{1,2},{2,5},{3,4},{4,7},{5,6},{6,1},{7,0},{8,11},{9,10},{10,... | collective-permute-start | bytes 589832 | tf_op jit(solution)/shard_map/ppermute | solution.py:389
  114.8 36.2 %copy-start.12 = (bf16[128,512]{1,0:T(8,128)(2,1)}, bf16[128,512]{1,0:T(8,128)(2,1)S(1)}, u32[]{:S(2)}) copy-start(bf16[128,512]{1,0:T(8,128)(2,1)S(1)} %collective-permute-done.3.refs_4_) | copy-start | bytes 393220
  114.8 32.7 %collective-permute-start.10 = (bf16[128,768]{1,0:T(8,128)(2,1)S(1)}, bf16[128,768]{1,0:T(8,128)(2,1)S(1)}, u32[]{:S(2)}, u32[]{:S(2)}) collective-permute-start(bf16[128,768]{1,0:T(8,128)(2,1)S(1)} %copy-done.19), channel_id=1, source_target_pairs={{0,4},{1,5},{2,6},{3,7},{4,0},{5,1},{6,2},{7,3},{8,12},{9,13},{10,... | collective-permute-start | bytes 589832 | tf_op jit(solution)/shard_map/ppermute | solution.py:389
  118.6 32.4 %copy-start.13 = (bf16[128,512]{1,0:T(8,128)(2,1)}, bf16[128,512]{1,0:T(8,128)(2,1)S(1)}, u32[]{:S(2)}) copy-start(bf16[128,512]{1,0:T(8,128)(2,1)S(1)} %collective-permute-done.4.refs_5_) | copy-start | bytes 393220
  118.6 28.9 %collective-permute-start.11 = (bf16[128,768]{1,0:T(8,128)(2,1)S(1)}, bf16[128,768]{1,0:T(8,128)(2,1)S(1)}, u32[]{:S(2)}, u32[]{:S(2)}) collective-permute-start(bf16[128,768]{1,0:T(8,128)(2,1)S(1)} %copy-done.18), channel_id=1, source_target_pairs={{0,5},{1,4},{2,7},{3,6},{4,1},{5,0},{6,3},{7,2},{8,13},{9,12},{10,... | collective-permute-start | bytes 589832 | tf_op jit(solution)/shard_map/ppermute | solution.py:389
  119.7 31.3 %copy-start.14 = (bf16[128,512]{1,0:T(8,128)(2,1)}, bf16[128,512]{1,0:T(8,128)(2,1)S(1)}, u32[]{:S(2)}) copy-start(bf16[128,512]{1,0:T(8,128)(2,1)S(1)} %collective-permute-done.5.refs_6_) | copy-start | bytes 393220
  119.7 27.8 %collective-permute-start.12 = (bf16[128,768]{1,0:T(8,128)(2,1)S(1)}, bf16[128,768]{1,0:T(8,128)(2,1)S(1)}, u32[]{:S(2)}, u32[]{:S(2)}) collective-permute-start(bf16[128,768]{1,0:T(8,128)(2,1)S(1)} %copy-done.17), channel_id=1, source_target_pairs={{0,6},{1,7},{2,0},{3,1},{4,2},{5,3},{6,4},{7,5},{8,14},{9,15},{10,... | collective-permute-start | bytes 589832 | tf_op jit(solution)/shard_map/ppermute | solution.py:389
  121.0 30.0 %copy-start.15 = (bf16[128,512]{1,0:T(8,128)(2,1)}, bf16[128,512]{1,0:T(8,128)(2,1)S(1)}, u32[]{:S(2)}) copy-start(bf16[128,512]{1,0:T(8,128)(2,1)S(1)} %collective-permute-done.6.refs_7_) | copy-start | bytes 393220
  121.0 26.5 %collective-permute-start.13 = (bf16[128,768]{1,0:T(8,128)(2,1)S(1)}, bf16[128,768]{1,0:T(8,128)(2,1)S(1)}, u32[]{:S(2)}, u32[]{:S(2)}) collective-permute-start(bf16[128,768]{1,0:T(8,128)(2,1)S(1)} %copy-done.16), channel_id=1, source_target_pairs={{0,7},{1,6},{2,1},{3,0},{4,3},{5,2},{6,5},{7,4},{8,15},{9,14},{10,... | collective-permute-start | bytes 589832 | tf_op jit(solution)/shard_map/ppermute | solution.py:389
  142.8 10.5 %all-to-all-start.3 = ((f32[8,2,128]{2,1,0:T(2,128)}), f32[8,2,128]{2,1,0:T(2,128)S(1)}, u32[]{:S(2)}, u32[]{:S(2)}) async-start(f32[8,2,128]{2,1,0:T(2,128)} %broadcast_in_dim.7), calls=%async_computation.3 | async-start | bytes 16384 | tf_op jit(solution)/shard_map/all_to_all | solution.py:368
  147.4 0.7 copy-start.4
  147.4 0.7 copy-start.5
  147.5 0.8 copy-start.6
  147.5 0.9 copy-start.7
  147.5 0.9 copy-start.8

commit v3 on v2

--- a/solution.py
+++ b/solution.py
@@ -6,13 +6,16 @@
 from jax import lax
 from jax.experimental import pallas as pl
 from jax.experimental.pallas import tpu as pltpu
-from jax.sharding import PartitionSpec as P
+from jax.sharding import Mesh, PartitionSpec as P
 
 WIDTH = 128
 SLOT = 1024
 TILE = 256
 REACH = 512
-CHUNKS = (3, 1)
+CHUNKS = (2, 2)
+SUM_ROWS = 16
+DP = ("z", "x")
+GROUPS = ((0, 256, 512, 768),)
 EPSILON = 1e-06
 NEG_FILL = -1e30
 SCALE = 1.0 / math.sqrt(WIDTH)
@@ -57,7 +60,8 @@
 
 
 def pack(pieces, owners, *refs):
-    *arrays, out, stage, in_sems, out_sems = refs
+    arrays, refs = refs[: len(pieces)], refs[len(pieces) :]
+    *outs, stage, holder, in_sems, out_sems = refs
     seqs = stage.shape[0]
     groups = in_sems.shape[0]
     span = seqs // groups
@@ -75,12 +79,40 @@
     for group in loads:
         start_all(group)
     stores = []
-    for g, group in enumerate(loads):
-        wait_all(group)
-        for s in range(g * span, (g + 1) * span):
-            stores.append(pltpu.make_async_copy(stage.at[s], out.at[owners[s]], out_sems.at[s]))
-            stores[-1].start()
+    if len(outs) == 1:
+        for g, group in enumerate(loads):
+            wait_all(group)
+            for s in range(g * span, (g + 1) * span):
+                copy = pltpu.make_async_copy(stage.at[s], outs[0].at[owners[s]], out_sems.at[s])
+                copy.start()
+                stores.append(copy)
+    else:
+        for s in range(seqs):
+            holder[owners[s]] = s
+        for group in loads:
+            wait_all(group)
+        for k, out in enumerate(outs):
+            x = lax.rem(lax.axis_index("x") + k, len(outs))
+            for z in range(out.shape[0]):
+                s = holder[z * len(outs) + x]
+                copy = pltpu.make_async_copy(stage.at[s], out.at[z], out_sems.at[k * out.shape[0] + z])
+                copy.start()
+                stores.append(copy)
     wait_all(stores)
+
+
+def regroup(*refs):
+    *arrays, out, stage, in_sems, out_sem = refs
+    count = len(arrays)
+    loads = []
+    for k, ref in enumerate(arrays):
+        src = lax.rem(lax.axis_index("x") + count - k, count)
+        loads.append(pltpu.make_async_copy(ref, stage.at[:, src], in_sems.at[k]))
+    start_all(loads)
+    wait_all(loads)
+    store = pltpu.make_async_copy(stage, out, out_sem.at[0])
+    store.start()
+    store.wait()
 
 
 def my_place():
@@ -119,6 +151,10 @@
         for n in (m for h in range(heads) for m in (h, heads + h))
     ]
     start_all(kv_in + own_in)
+
+    def own_wait(n):
+        return pltpu.make_async_copy(own.at[n], own.at[n], in_sems.at[n + 2])
+
     if not first:
         carry = [
             pltpu.make_async_copy(a, b, carry_sems.at[n])
@@ -133,8 +169,9 @@
         return ref[slot, at // 32 : (at + size) // 32].reshape(size, WIDTH)
 
     mine = jnp.int32(0)
+    here = lax.axis_index("z") * lax.axis_size("x") + lax.axis_index("x")
     for s in range(owners.shape[0]):
-        mine = jnp.where(owners[s] == lax.axis_index("dp"), s, mine)
+        mine = jnp.where(owners[s] == here, s, mine)
     length = lengths[mine]
     doc_row = docs[pl.ds(mine, 1)]
     start = jnp.zeros_like(doc_row)
@@ -156,7 +193,6 @@
             vt[:, part] = dot_t(eye, rows(kv, 1, at, TILE)).astype(BF)
     else:
         wait_all(kv_in + carry)
-    wait_all(own_in)
     u_rel = lax.broadcasted_iota(jnp.int32, (TILE, TILE), 0)
     t_rel = lax.broadcasted_iota(jnp.int32, (1, TILE), 1)
 
@@ -170,52 +206,68 @@
         ]
 
     def one_head(h):
-        for t0 in range(0, SLOT, TILE):
-            u_list = [u for u in range(0, t0 + 1, TILE) if t0 - (u + TILE - 1) < REACH]
-            q_t = dot_t(eye, rows(own, h, t0, TILE))
-            g_t = dot_t(eye, rows(own, heads + h, t0, TILE))
-            g_b = g_t.astype(BF)
-            q_inv = lax.rsqrt(jnp.mean(q_t * q_t, axis=0, keepdims=True) + EPSILON)
-            q_hat = q_t * q_inv
-            q_n = (q_hat * gain).astype(BF)
-            starts = start[:, t0 : t0 + TILE]
-            scores = [dot(kn[pl.ds(u0, TILE)], q_n) for u0 in u_list]
-            grads = [dot(rows(kv, 1, u0, TILE), g_b) for u0 in u_list]
-            masked = []
-            for u0, s in zip(u_list, scores):
-                allowed = u_rel >= starts - u0
-                if u0 == t0:
+        wait_all([own_wait(h), own_wait(heads + h)])
+        for group in GROUPS:
+            together(h, group)
+        start_all(copies_out(h) + copies_out(heads + h))
+
+    def together(h, tiles):
+        us = {t: [u for u in range(0, t + 1, TILE) if t - (u + TILE - 1) < REACH] for t in tiles}
+        q_inv, q_hat, q_n, g_t, g_b, scores, grads = ({} for _ in range(7))
+        for t in tiles:
+            q_t = dot_t(eye, rows(own, h, t, TILE))
+            g_t[t] = dot_t(eye, rows(own, heads + h, t, TILE))
+            g_b[t] = g_t[t].astype(BF)
+            q_inv[t] = lax.rsqrt(jnp.mean(q_t * q_t, axis=0, keepdims=True) + EPSILON)
+            q_hat[t] = q_t * q_inv[t]
+            q_n[t] = (q_hat[t] * gain).astype(BF)
+        for t in tiles:
+            scores[t] = [dot(kn[pl.ds(u, TILE)], q_n[t]) for u in us[t]]
+        for t in tiles:
+            grads[t] = [dot(rows(kv, 1, u, TILE), g_b[t]) for u in us[t]]
+        largest, weights, factor, probs, low, o_t, delta, dq_t = ({} for _ in range(8))
+        for t in tiles:
+            first_u = start[:, t : t + TILE]
+            for n, u in enumerate(us[t]):
+                allowed = u_rel >= first_u - u
+                if u == t:
                     allowed = allowed & (u_rel <= t_rel)
-                masked.append(jnp.where(allowed, s * (SCALE * math.log2(math.e)), NEG_FILL))
-            largest = functools.reduce(
-                jnp.maximum, [jnp.max(s, axis=0, keepdims=True) for s in masked]
+                scaled = scores[t][n] * (SCALE * math.log2(math.e))
+                scores[t][n] = jnp.where(allowed, scaled, NEG_FILL)
+            largest[t] = functools.reduce(
+                jnp.maximum, [jnp.max(s, axis=0, keepdims=True) for s in scores[t]]
             )
-            weights = [jnp.exp2(s - largest) for s in masked]
-            total = sum(jnp.sum(w, axis=0, keepdims=True) for w in weights)
-            factor = jnp.where(t_rel + t0 < length, 1.0 / jnp.maximum(total, 1.0), 0.0)
-            probs = [w * factor for w in weights]
-            low = [p.astype(BF) for p in probs]
-            o_t = sum(dot(vt[:, pl.ds(u0, TILE)], p) for u0, p in zip(u_list, low))
-            delta = jnp.sum(g_t * o_t, axis=0, keepdims=True)
-            dq_t = 0.0
-            for u0, p, pb, dp in zip(u_list, probs, low, grads):
-                part = pl.ds(u0, TILE)
-                dv[part] += dot_t(pb, g_b)
-                ds = (p * (dp - delta)).astype(BF)
-                dk[part] += dot_t(ds, q_n)
-                dq_t += dot(knt[:, part], ds)
-            dq_t = dq_t * SCALE
-            q_acc[...] += dq_t * q_hat
-            grad_hat = dq_t * gain
-            inner = jnp.mean(grad_hat * q_hat, axis=0, keepdims=True)
-            dq = (q_inv * (grad_hat - q_hat * inner)).astype(BF)
-            o = dot_t(eye_tile, o_t.astype(BF)).astype(BF)
+        for t in tiles:
+            weights[t] = [jnp.exp2(s - largest[t]) for s in scores[t]]
+            total = sum(jnp.sum(w, axis=0, keepdims=True) for w in weights[t])
+            factor[t] = jnp.where(t_rel + t < length, 1.0 / jnp.maximum(total, 1.0), 0.0)
+        for t in tiles:
+            probs[t] = [w * factor[t] for w in weights[t]]
+            low[t] = [p.astype(BF) for p in probs[t]]
+            o_t[t] = sum(dot(vt[:, pl.ds(u, TILE)], p) for u, p in zip(us[t], low[t]))
+        for t in tiles:
+            delta[t] = jnp.sum(g_t[t] * o_t[t], axis=0, keepdims=True)
+            for u, p in zip(us[t], low[t]):
+                dv[pl.ds(u, TILE)] += dot_t(p, g_b[t])
+        for t in tiles:
+            dq_t[t] = 0.0
+            for u, p, dp in zip(us[t], probs[t], grads[t]):
+                part = pl.ds(u, TILE)
+                ds = (p * (dp - delta[t])).astype(BF)
+                dk[part] += dot_t(ds, q_n[t])
+                dq_t[t] += dot(knt[:, part], ds)
+        for t in tiles:
+            dq = dq_t[t] * SCALE
+            q_acc[...] += dq * q_hat[t]
+            grad_hat = dq * gain
+            inner = jnp.mean(grad_hat * q_hat[t], axis=0, keepdims=True)
+            dq = (q_inv[t] * (grad_hat - q_hat[t] * inner)).astype(BF)
+            o = dot_t(eye_tile, o_t[t].astype(BF)).astype(BF)
             dq = dot_t(eye_tile, dq).astype(BF)
             for n in range(TILE // WIDTH):
                 for to, block in ((h, o), (heads + h, dq)):
                     cols = pl.ds(pl.multiple_of(to * WIDTH, WIDTH), WIDTH)
-                    send[t0 // TILE, n, :, cols] = block[n * WIDTH : (n + 1) * WIDTH]
-        start_all(copies_out(h) + copies_out(heads + h))
+                    send[t // TILE, n, :, cols] = block[n * WIDTH : (n + 1) * WIDTH]
 
     def finish():
         k_sum = jnp.zeros((1, WIDTH), F32)
@@ -230,8 +282,10 @@
             send[(*block, column(2 * heads + 1))] = dv[part].astype(BF)
         start_all(copies_out(2 * heads) + copies_out(2 * heads + 1))
         q_sum = jnp.sum(q_acc[...], axis=1, keepdims=True)
-        sums[0:1] = jnp.broadcast_to(q_sum, (WIDTH, WIDTH)).T[0:1]
-        sums[1:2] = k_sum
+        q_row = jnp.broadcast_to(q_sum, (WIDTH, WIDTH)).T[0:1]
+        row = lax.broadcasted_iota(jnp.int32, (SUM_ROWS, WIDTH), 0)
+        both = jnp.where(row == 0, q_row, jnp.where(row == 1, k_sum, 0.0))
+        sums[...] = jnp.broadcast_to(both, sums.shape)
 
     if heads == 1:
         one_head(0)
@@ -250,14 +304,15 @@
         pltpu.make_async_copy(out, out, out_sem.at[r]).wait()
 
 
-def place(at, *refs):
-    refs = list(refs)
+def place(first_head, heads, last, *refs):
     stage, in_sems, out_sems = refs[-3:]
     received, outs = refs[:8], refs[-7:-3]
     y, c = my_place()
-    columns = outs[0].shape[2] // (8 * WIDTH) * WIDTH
-    count = 2 if at == 0 else 4
-    per = received[0].shape[1] // count
+    columns = outs[0].shape[2] // 8
+    per = heads * WIDTH
+    pieces = [(0, per, 0), (per, per, 1)]
+    if last:
+        pieces += [(2 * per, WIDTH, 2), (2 * per + WIDTH, WIDTH, 3)]
     loads = [
         pltpu.make_async_copy(ref, stage.at[r], in_sems.at[r]) for r, ref in enumerate(received)
     ]
@@ -266,12 +321,12 @@
     for r, load in enumerate(loads):
         load.wait()
         src = lax.rem(y + 4 - r // 2, 4) * 2 + (c ^ (r % 2))
-        for n in range(count):
-            start = src * columns + at if n < 2 else src * WIDTH
+        for n, (at, size, out) in enumerate(pieces):
+            start = src * columns + first_head * WIDTH if out < 2 else src * WIDTH
             stores.append(
                 pltpu.make_async_copy(
-                    stage.at[r, :, pl.ds(n * per, per)],
-                    outs[n].at[0, :, pl.ds(pl.multiple_of(start, WIDTH), per)],
+                    stage.at[r, :, pl.ds(at, size)],
+                    outs[out].at[0, :, pl.ds(pl.multiple_of(start, WIDTH), size)],
                     out_sems.at[r, n],
                 )
             )
@@ -327,7 +382,7 @@
         pltpu.SemaphoreType.DMA((len(kept),)),
         pltpu.SemaphoreType.DMA((8,)),
     ]
-    outs += [shape((2, WIDTH), F32)] if last else [shape(*a) for a in kept]
+    outs += [shape((kv.shape[0], SUM_ROWS, WIDTH), F32)] if last else [shape(*a) for a in kept]
     result = call(
         functools.partial(attend, heads, first, last),
         args,
@@ -345,26 +400,42 @@
     return [(i, ((i // 2 + r // 2) % 4) * 2 + ((i % 2) ^ (r % 2))) for i in range(8)]
 
 
-def packed_chunk(owners, arrays, pieces, name):
+def packed_chunk(owners, arrays, pieces, by_x):
     seqs, per_src, _ = arrays[0].shape
     width = sum(p[2] for p in pieces)
-    return call(
+    count = lax.axis_size("x") if by_x else 1
+    block = (seqs // count, per_src, width)
+    parts = call(
         functools.partial(pack, pieces),
         [owners, *arrays],
         [SMEM] + [HBM] * len(arrays),
-        [shape((seqs, per_src, width))],
-        [HBM],
+        [shape(block)] * count,
+        [HBM] * count,
         [
             pltpu.VMEM((seqs, per_src, width), BF),
+            pltpu.SMEM((seqs,), jnp.int32),
             pltpu.SemaphoreType.DMA((4, len(pieces))),
             pltpu.SemaphoreType.DMA((seqs,)),
         ],
-        name,
+        "pack",
+    )
+    if not by_x:
+        return parts[0]
+    shift = [[(i, (i + k) % count) for i in range(count)] for k in range(count)]
+    parts = [parts[0]] + [lax.ppermute(parts[k], "x", shift[k]) for k in range(1, count)]
+    whole = (block[0], count, *block[1:])
+    return call(
+        regroup,
+        parts,
+        [HBM] * count,
+        [shape(whole)],
+        [HBM],
+        [pltpu.VMEM(whole, BF), pltpu.SemaphoreType.DMA((count,)), pltpu.SemaphoreType.DMA((1,))],
+        "regroup",
     )[0]
 
 
-def total(sums, axis):
-    spread = jnp.broadcast_to(sums, (lax.axis_size(axis), *sums.shape))
+def total(spread, axis):
     return jnp.sum(lax.all_to_all(spread, axis, 0, 0, tiled=True), axis=0)
 
 
@@ -372,32 +443,36 @@
     seqs, _, features = query.shape
     heads = features // WIDTH
     head_devs = lax.axis_size("head")
-    cut, rest = CHUNKS[0] * WIDTH, CHUNKS[1] * WIDTH
-    front = packed_chunk(
-        owners,
-        [query, grad, key, value],
-        [(0, 0, cut), (0, cut, cut), (0, 2 * cut, WIDTH), (0, 2 * cut + WIDTH, WIDTH)],
-        "pack_front",
-    )
-    back = packed_chunk(owners, [query, grad], [(cut, 0, rest), (cut, rest, rest)], "pack_back")
-    front = lax.all_to_all(front, "dp", 0, 0, tiled=True)
-    front, back = lax.optimization_barrier((front, back))
-    back = lax.all_to_all(back, "dp", 0, 0, tiled=True)
-
     small = (owners, lengths, doc_ids, q_gain.reshape(1, WIDTH), k_gain.reshape(1, WIDTH))
-    out, carry = attend_chunk(CHUNKS[0], True, False, *small, front, None, None)
-    early = [out[0]] + [lax.ppermute(out[r], "head", across(r)) for r in range(1, 8)]
-    out, (sums,) = attend_chunk(CHUNKS[1], False, True, *small, front, back, carry)
-    late = [out[0]] + [lax.ppermute(out[r], "head", across(r)) for r in range(1, 8)]
-    sums, late = lax.optimization_barrier((total(sums, "dp"), late))
-    sums = total(sums, "head")
+    chunks, at = [], 0
+    for count in CHUNKS:
+        width = count * WIDTH
+        arrays, pieces = [query, grad], [(at, 0, width), (at, width, width)]
+        if at == 0:
+            arrays += [key, value]
+            pieces += [(0, 2 * width, WIDTH), (0, 2 * width + WIDTH, WIDTH)]
+        chunks.append(packed_chunk(owners, arrays, pieces, at > 0))
+        at += width
+    owned = [lax.all_to_all(chunks[0], DP, 0, 0, tiled=True)]
+    received, carry = [], None
+    for n, count in enumerate(CHUNKS):
+        last = n == len(CHUNKS) - 1
+        if not last:
+            owned[n], chunk = lax.optimization_barrier((owned[n], chunks[n + 1]))
+            owned.append(lax.all_to_all(chunk, "z", 0, 0, tiled=True).reshape(seqs, *query.shape[1:2], -1))
+        if n > 0:
+            owned[n], received[-1] = lax.optimization_barrier((owned[n], received[-1]))
+        out, carry = attend_chunk(count, n == 0, last, *small, owned[0], owned[n], carry)
+        received.append([out[0]] + [lax.ppermute(out[r], "head", across(r)) for r in range(1, 8)])
+    sums, received[-1][1:4] = lax.optimization_barrier((total(carry[0], DP), received[-1][1:4]))
+    sums = total(jnp.broadcast_to(sums, (head_devs, *sums.shape)), "head")
     wide, narrow = shape((1, WIDTH, heads * head_devs * WIDTH)), shape((1, WIDTH, head_devs * WIDTH))
-    outs = None
-    for at, got in ((0, early), (cut, late)):
+    outs, at = [], 0
+    for n, (count, got) in enumerate(zip(CHUNKS, received)):
         outs = call(
-            functools.partial(place, at),
-            [*got, *(outs or [])],
-            [HBM] * (8 + len(outs or [])),
+            functools.partial(place, at, count, n == len(CHUNKS) - 1),
+            [*got, *outs],
+            [HBM] * (8 + len(outs)),
             [wide, wide, narrow, narrow],
             [HBM] * 4,
             [
@@ -408,6 +483,7 @@
             "place",
             aliases={8 + n: n for n in range(4)} if outs else None,
         )
+        at += count
     tokens = seqs * SLOT
     return (
         *outs,
@@ -417,11 +493,13 @@
 
 
 def solution(mesh):
-    spread = P(None, "dp", "head")
-    packed = P("dp", "head", None)
+    dp, head = mesh.devices.shape
+    grid = Mesh(mesh.devices.reshape(dp // 4, 4, head), (*DP, "head"))
+    spread = P(None, DP, "head")
+    packed = P(DP, "head", None)
     return jax.shard_map(
         per_device,
-        mesh=mesh,
+        mesh=grid,
         in_specs=(spread,) * 4 + (P(),) * 5,
         out_specs=(packed,) * 4 + (P(),) * 2,
         check_vma=False,

time: 154 us -> 138 us (0.90)
  blocking collectives: 18.1 us -> 0 us
  starting transfers between devices: 40.6 us -> 58.2 us
  waiting for transfers between devices: 52.6 us -> 40.4 us
  Pallas kernels: 38.2 us -> 33.9 us
    all_to_all x2, waiting for transfers between devices: 45.7 us -> 6.34 us  [the longest x1 6.34 us: per_device(): owned = [lax.all_to_all(chunks[0], DP, 0, 0, tiled=True)]]
    ppermute x0 -> x3, waiting for transfers between devices: none -> 20.5 us  [packed_chunk(): lax.ppermute(parts[k], 'x', shift[k])]
    all_to_all x1 -> x0, blocking collectives: 18.1 us -> none  [total(): return jnp.sum(lax.all_to_all(spread, axis, 0, 0, tiled=True), axis=0)]
    all_to_all x1 -> x2, starting transfers between devices: 4.65 us -> 14.7 us  [total(): return jnp.sum(lax.all_to_all(spread, axis, 0, 0, tiled=True), axis=0)]
    ppermute x14, waiting for transfers between devices: 6.84 us -> 13.1 us  [per_device(): lax.ppermute(out[r], 'head', across(r))]
    ppermute x14, starting transfers between devices: 17.4 us -> 23.2 us  [per_device(): lax.ppermute(out[r], 'head', across(r))]
    ppermute x0 -> x3, starting transfers between devices: none -> 4.88 us  [packed_chunk(): lax.ppermute(parts[k], 'x', shift[k])]
    pallas_call x6 -> x7, Pallas kernels: 38.2 us -> 33.9 us  [call(): pl.pallas_call(kernel, out_shape=outs, in_specs=in_specs, out_specs=out_s...]
  transfers between devices with their start and end apart: 17 -> 21, of which waited for: 5 -> 12; matrix products, arithmetic and copies ran while one was open for 1% -> 1% of each run, Pallas kernels for 22% -> 14%
where the time goes in v3:
time: 138 us; the launch traced here: 137 us
  starting transfers between devices  58.2 us (42%)
  waiting for transfers between devices  40.4 us (29%)
  Pallas kernels  33.9 us (25%)
  local copies, waits for them, and re-layouts  3.05 us (2%)
    pallas_call x7, Pallas kernels, call(): pl.pallas_call(kernel, out_shape=outs, in_specs=in_specs, out_specs=out_s...  33.9 us
    ppermute x14, starting transfers between devices, per_device(): lax.ppermute(out[r], 'head', across(r))  23.2 us
    ppermute x3, waiting for transfers between devices, packed_chunk(): lax.ppermute(parts[k], 'x', shift[k])  20.5 us
    all_to_all x2, starting transfers between devices, total(): return jnp.sum(lax.all_to_all(spread, axis, 0, 0, tiled=True), axis=0)  14.7 us
    ppermute x14, waiting for transfers between devices, per_device(): lax.ppermute(out[r], 'head', across(r))  13.1 us
    all_to_all x1, starting transfers between devices, per_device(): owned = [lax.all_to_all(chunks[0], DP, 0, 0, tiled=True)]  11.9 us
    all_to_all x1, waiting for transfers between devices, per_device(): owned = [lax.all_to_all(chunks[0], DP, 0, 0, tiled=True)]  6.34 us
    ppermute x3, starting transfers between devices, packed_chunk(): lax.ppermute(parts[k], 'x', shift[k])  4.88 us
  transfers between devices with their start and end apart: 21, of which 12 were waited for; matrix products, arithmetic and copies ran while one was open for 1% of the time, Pallas kernels for 14%

profile of v3, /device:TPU:1, one launch (start us, length us, event | category | flops | bytes accessed | tf_op | source)
XLA Modules:
  0.0 137.0 jit_solution(7672698675869807851)
XLA Ops:
  0.6 3.3 %pack.2 = bf16[32,32,768]{2,1,0:T(8,128)(2,1)} custom-call(s32[32]{0:T(128)} %refs_0_.7, bf16[32,32,512]{2,1,0:T(8,128)(2,1)} %refs_0_.5, bf16[32,32,512]{2,1,0:T(8,128)(2,1)} %refs_1_.5, bf16[32,32,128]{2,1,0:T(8,128)(2,1)} %refs_2_.3, bf16[32,32,128]{2,1,0:T(8,128)(2,1)} %refs_3_.1), custom_call_target="tpu_custom_call" | custom-call | bytes 4194432 | tf_op jit(solution)/shard_map/pack/pallas_call | solution.py:344
  4.0 11.9 %all-to-all-start = ((bf16[32,32,768]{2,1,0:T(8,128)(2,1)}), bf16[32,32,768]{2,1,0:T(8,128)(2,1)S(1)}, u32[]{:S(2)}, u32[]{:S(2)}) async-start(bf16[32,32,768]{2,1,0:T(8,128)(2,1)} %pack.2), calls=%async_computation | async-start | bytes 3145728 | tf_op jit(solution)/shard_map/all_to_all | solution.py:456
  15.8 3.3 %pack.3 = (bf16[8,32,512]{2,1,0:T(8,128)(2,1)}, bf16[8,32,512]{2,1,0:T(8,128)(2,1)}, bf16[8,32,512]{2,1,0:T(8,128)(2,1)}, bf16[8,32,512]{2,1,0:T(8,128)(2,1)}) custom-call(s32[32]{0:T(128)} %refs_0_.7, bf16[32,32,512]{2,1,0:T(8,128)(2,1)} %refs_0_.5, bf16[32,32,512]{2,1,0:T(8,128)(2,1)} %refs_1_.5), custom_call_target="tpu_custom_call" | custom-call | bytes 3145856 | tf_op jit(solution)/shard_map/pack/pallas_call | solution.py:344
  19.1 1.3 collective-permute-start
  20.4 2.4 %collective-permute-start.1 = (bf16[8,32,512]{2,1,0:T(8,128)(2,1)}, bf16[8,32,512]{2,1,0:T(8,128)(2,1)S(1)}, u32[]{:S(2)}, u32[]{:S(2)}) collective-permute-start(bf16[8,32,512]{2,1,0:T(8,128)(2,1)} %get-tuple-element.58), channel_id=1, source_target_pairs={{0,16},{8,24},{16,0},{24,8},{1,17},{9,25},{17,1},{25,9},{2,18},{10... | collective-permute-start | bytes 786440 | tf_op jit(solution)/shard_map/ppermute | solution.py:425
  22.8 1.2 collective-permute-start.2
  24.0 11.5 %collective-permute-done.refs_1_ = bf16[8,32,512]{2,1,0:T(8,128)(2,1)S(1)} collective-permute-done((bf16[8,32,512]{2,1,0:T(8,128)(2,1)}, bf16[8,32,512]{2,1,0:T(8,128)(2,1)S(1)}, u32[]{:S(2)}, u32[]{:S(2)}) %collective-permute-start) | collective-permute-done | bytes 262176 | tf_op jit(solution)/shard_map/ppermute | solution.py:425
  35.5 4.9 %collective-permute-done.1.refs_2_ = bf16[8,32,512]{2,1,0:T(8,128)(2,1)S(1)} collective-permute-done((bf16[8,32,512]{2,1,0:T(8,128)(2,1)}, bf16[8,32,512]{2,1,0:T(8,128)(2,1)S(1)}, u32[]{:S(2)}, u32[]{:S(2)}) %collective-permute-start.1) | collective-permute-done | bytes 262176 | tf_op jit(solution)/shard_map/ppermute | solution.py:425
  40.4 4.1 %collective-permute-done.2.refs_3_ = bf16[8,32,512]{2,1,0:T(8,128)(2,1)S(1)} collective-permute-done((bf16[8,32,512]{2,1,0:T(8,128)(2,1)}, bf16[8,32,512]{2,1,0:T(8,128)(2,1)S(1)}, u32[]{:S(2)}, u32[]{:S(2)}) %collective-permute-start.2) | collective-permute-done | bytes 262176 | tf_op jit(solution)/shard_map/ppermute | solution.py:425
  44.5 0.0 copy-done.2
  44.5 0.0 copy-done.3
  44.5 0.7 copy-done.4
  45.2 2.2 %regroup.1 = bf16[8,4,32,512]{3,2,1,0:T(8,128)(2,1)} custom-call(bf16[8,32,512]{2,1,0:T(8,128)(2,1)} %get-tuple-element.56.refs_0_, bf16[8,32,512]{2,1,0:T(8,128)(2,1)} %copy-done.2, bf16[8,32,512]{2,1,0:T(8,128)(2,1)} %copy-done.3, bf16[8,32,512]{2,1,0:T(8,128)(2,1)} %copy-done.4), custom_call_target="tpu_custom_call" | custom-call | bytes 2097152 | tf_op jit(solution)/shard_map/regroup/pallas_call | solution.py:344
  47.4 6.3 %all-to-all-done.refs_5_ = bf16[32,32,768]{2,1,0:T(8,128)(2,1)S(1)} async-done(((bf16[32,32,768]{2,1,0:T(8,128)(2,1)}), bf16[32,32,768]{2,1,0:T(8,128)(2,1)S(1)}, u32[]{:S(2)}, u32[]{:S(2)}) %all-to-all-start) | async-done | bytes 1572896 | tf_op jit(solution)/shard_map/all_to_all | solution.py:456
  53.7 3.6 %all-to-all-start.1 = ((bf16[8,4,32,512]{3,2,1,0:T(8,128)(2,1)}), bf16[8,4,32,512]{3,2,1,0:T(8,128)(2,1)S(1)}, u32[]{:S(2)}, u32[]{:S(2)}) async-start(bf16[8,4,32,512]{3,2,1,0:T(8,128)(2,1)} %regroup.1), calls=%async_computation.1 | async-start | bytes 2097152 | tf_op jit(solution)/shard_map/all_to_all | solution.py:462
  57.3 0.0 copy-done
  57.3 9.5 %attend.2 = (bf16[128,512]{1,0:T(8,128)(2,1)}, bf16[128,512]{1,0:T(8,128)(2,1)}, bf16[128,512]{1,0:T(8,128)(2,1)}, bf16[128,512]{1,0:T(8,128)(2,1)}, bf16[128,51...) custom-call(s32[32]{0:T(128)} %refs_0_.7, ...), custom_call_target="tpu_custom_call" | custom-call | flops 1811939328 | bytes 4719872 | tf_op jit(solution)/shard_map/attend/pallas_call | solution.py:344
  66.8 2.7 %collective-permute-start.3 = (bf16[128,512]{1,0:T(8,128)(2,1)}, bf16[128,512]{1,0:T(8,128)(2,1)S(1)}, u32[]{:S(2)}, u32[]{:S(2)}) collective-permute-start(bf16[128,512]{1,0:T(8,128)(2,1)} %get-tuple-element.63), channel_id=1, source_target_pairs={{0,1},{1,0},{2,3},{3,2},{4,5},{5,4},{6,7},{7,6},{8,9},{9,8},{10,11... | collective-permute-start | bytes 393224 | tf_op jit(solution)/shard_map/ppermute | solution.py:466
  69.5 1.3 collective-permute-start.4
  70.8 1.5 %collective-permute-start.5 = (bf16[128,512]{1,0:T(8,128)(2,1)}, bf16[128,512]{1,0:T(8,128)(2,1)S(1)}, u32[]{:S(2)}, u32[]{:S(2)}) collective-permute-start(bf16[128,512]{1,0:T(8,128)(2,1)} %get-tuple-element.65), channel_id=1, source_target_pairs={{0,3},{1,2},{2,5},{3,4},{4,7},{5,6},{6,1},{7,0},{8,11},{9,10},{10,... | collective-permute-start | bytes 393224 | tf_op jit(solution)/shard_map/ppermute | solution.py:466
  72.4 1.3 collective-permute-start.6
  73.6 2.0 %collective-permute-start.7 = (bf16[128,512]{1,0:T(8,128)(2,1)}, bf16[128,512]{1,0:T(8,128)(2,1)S(1)}, u32[]{:S(2)}, u32[]{:S(2)}) collective-permute-start(bf16[128,512]{1,0:T(8,128)(2,1)} %get-tuple-element.67), channel_id=1, source_target_pairs={{0,5},{1,4},{2,7},{3,6},{4,1},{5,0},{6,3},{7,2},{8,13},{9,12},{10,... | collective-permute-start | bytes 393224 | tf_op jit(solution)/shard_map/ppermute | solution.py:466
  75.7 0.0 collective-permute-done.3.refs_1_
  75.7 1.4 %collective-permute-start.8 = (bf16[128,512]{1,0:T(8,128)(2,1)}, bf16[128,512]{1,0:T(8,128)(2,1)S(1)}, u32[]{:S(2)}, u32[]{:S(2)}) collective-permute-start(bf16[128,512]{1,0:T(8,128)(2,1)} %get-tuple-element.68), channel_id=1, source_target_pairs={{0,6},{1,7},{2,0},{3,1},{4,2},{5,3},{6,4},{7,5},{8,14},{9,15},{10,... | collective-permute-start | bytes 393224 | tf_op jit(solution)/shard_map/ppermute | solution.py:466
  77.1 0.0 collective-permute-done.4.refs_2_
  77.1 1.7 %collective-permute-start.9 = (bf16[128,512]{1,0:T(8,128)(2,1)}, bf16[128,512]{1,0:T(8,128)(2,1)S(1)}, u32[]{:S(2)}, u32[]{:S(2)}) collective-permute-start(bf16[128,512]{1,0:T(8,128)(2,1)} %get-tuple-element.69), channel_id=1, source_target_pairs={{0,7},{1,6},{2,1},{3,0},{4,3},{5,2},{6,5},{7,4},{8,15},{9,14},{10,... | collective-permute-start | bytes 393224 | tf_op jit(solution)/shard_map/ppermute | solution.py:466
  78.8 0.6 collective-permute-done.5.refs_3_
  79.3 3.5 %collective-permute-done.6.refs_4_ = bf16[128,512]{1,0:T(8,128)(2,1)S(1)} collective-permute-done((bf16[128,512]{1,0:T(8,128)(2,1)}, bf16[128,512]{1,0:T(8,128)(2,1)S(1)}, u32[]{:S(2)}, u32[]{:S(2)}) %collective-permute-start.6) | collective-permute-done | bytes 131104 | tf_op jit(solution)/shard_map/ppermute | solution.py:466
  82.9 3.3 %collective-permute-done.7.refs_5_ = bf16[128,512]{1,0:T(8,128)(2,1)S(1)} collective-permute-done((bf16[128,512]{1,0:T(8,128)(2,1)}, bf16[128,512]{1,0:T(8,128)(2,1)S(1)}, u32[]{:S(2)}, u32[]{:S(2)}) %collective-permute-start.7) | collective-permute-done | bytes 131104 | tf_op jit(solution)/shard_map/ppermute | solution.py:466
  86.1 0.0 collective-permute-done.8.refs_6_
  86.2 0.6 collective-permute-done.9.refs_7_
  86.8 0.0 all-to-all-done.1
  86.8 1.0 copy-done.1
  87.8 10.8 %attend.3 = (bf16[128,768]{1,0:T(8,128)(2,1)}, bf16[128,768]{1,0:T(8,128)(2,1)}, bf16[128,768]{1,0:T(8,128)(2,1)}, bf16[128,768]{1,0:T(8,128)(2,1)}, bf16[128,76...) custom-call(s32[32]{0:T(128)} %refs_0_.7, ...), custom_call_target="tpu_custom_call" | custom-call | flops 1811939328 | bytes 6554880 | tf_op jit(solution)/shard_map/attend/pallas_call | solution.py:344
  98.6 9.7 %all-to-all-start.2 = ((f32[32,16,128]{2,1,0:T(8,128)}), f32[32,16,128]{2,1,0:T(8,128)S(1)}, u32[]{:S(2)}, u32[]{:S(2)}) async-start(f32[32,16,128]{2,1,0:T(8,128)} %get-tuple-element.78), calls=%async_computation.2 | async-start | bytes 524288 | tf_op jit(solution)/shard_map/all_to_all | solution.py:439
  108.4 0.6 collective-permute-start.10
  109.0 2.3 %collective-permute-start.11 = (bf16[128,768]{1,0:T(8,128)(2,1)}, bf16[128,768]{1,0:T(8,128)(2,1)S(1)}, u32[]{:S(2)}, u32[]{:S(2)}) collective-permute-start(bf16[128,768]{1,0:T(8,128)(2,1)} %get-tuple-element.80), channel_id=1, source_target_pairs={{0,2},{1,3},{2,4},{3,5},{4,6},{5,7},{6,0},{7,1},{8,10},{9,11},{10,... | collective-permute-start | bytes 589832 | tf_op jit(solution)/shard_map/ppermute | solution.py:466
  111.3 0.1 collective-permute-start.12
  111.5 1.7 %collective-permute-start.13 = (bf16[128,768]{1,0:T(8,128)(2,1)}, bf16[128,768]{1,0:T(8,128)(2,1)S(1)}, u32[]{:S(2)}, u32[]{:S(2)}) collective-permute-start(bf16[128,768]{1,0:T(8,128)(2,1)} %get-tuple-element.85), channel_id=1, source_target_pairs={{0,4},{1,5},{2,6},{3,7},{4,0},{5,1},{6,2},{7,3},{8,12},{9,13},{10,... | collective-permute-start | bytes 589832 | tf_op jit(solution)/shard_map/ppermute | solution.py:466
  113.1 1.8 %collective-permute-start.14 = (bf16[128,768]{1,0:T(8,128)(2,1)}, bf16[128,768]{1,0:T(8,128)(2,1)S(1)}, u32[]{:S(2)}, u32[]{:S(2)}) collective-permute-start(bf16[128,768]{1,0:T(8,128)(2,1)} %get-tuple-element.86), channel_id=1, source_target_pairs={{0,5},{1,4},{2,7},{3,6},{4,1},{5,0},{6,3},{7,2},{8,13},{9,12},{10,... | collective-permute-start | bytes 589832 | tf_op jit(solution)/shard_map/ppermute | solution.py:466
  114.9 0.0 collective-permute-done.10.refs_1_
  114.9 2.7 %collective-permute-start.15 = (bf16[128,768]{1,0:T(8,128)(2,1)}, bf16[128,768]{1,0:T(8,128)(2,1)S(1)}, u32[]{:S(2)}, u32[]{:S(2)}) collective-permute-start(bf16[128,768]{1,0:T(8,128)(2,1)} %get-tuple-element.87), channel_id=1, source_target_pairs={{0,6},{1,7},{2,0},{3,1},{4,2},{5,3},{6,4},{7,5},{8,14},{9,15},{10,... | collective-permute-start | bytes 589832 | tf_op jit(solution)/shard_map/ppermute | solution.py:466
  117.6 0.0 collective-permute-done.11.refs_2_
  117.6 2.0 %collective-permute-start.16 = (bf16[128,768]{1,0:T(8,128)(2,1)}, bf16[128,768]{1,0:T(8,128)(2,1)S(1)}, u32[]{:S(2)}, u32[]{:S(2)}) collective-permute-start(bf16[128,768]{1,0:T(8,128)(2,1)} %get-tuple-element.88), channel_id=1, source_target_pairs={{0,7},{1,6},{2,1},{3,0},{4,3},{5,2},{6,5},{7,4},{8,15},{9,14},{10,... | collective-permute-start | bytes 589832 | tf_op jit(solution)/shard_map/ppermute | solution.py:466
  119.6 0.4 all-to-all-done.2
  120.1 1.5 %collective-permute-done.12.refs_3_ = bf16[128,768]{1,0:T(8,128)(2,1)S(1)} collective-permute-done((bf16[128,768]{1,0:T(8,128)(2,1)}, bf16[128,768]{1,0:T(8,128)(2,1)S(1)}, u32[]{:S(2)}, u32[]{:S(2)}) %collective-permute-start.12) | collective-permute-done | bytes 196640 | tf_op jit(solution)/shard_map/ppermute | solution.py:466
  121.6 0.7 broadcast_in_dim.3
  122.3 5.0 %all-to-all-start.3 = ((f32[8,16,128]{2,1,0:T(8,128)}), f32[8,16,128]{2,1,0:T(8,128)S(1)}, u32[]{:S(2)}, u32[]{:S(2)}) async-start(f32[8,16,128]{2,1,0:T(8,128)} %broadcast_in_dim.3), calls=%async_computation.3 | async-start | bytes 131072 | tf_op jit(solution)/shard_map/all_to_all | solution.py:439
  127.3 0.0 copy-done.14
  127.3 0.0 copy-done.15
  127.3 0.0 copy-done.16
  127.3 0.0 copy-done.17
  127.3 0.0 copy-done.18
  127.3 2.3 %place.2 = (bf16[1,128,4096]{2,1,0:T(8,128)(2,1)}, bf16[1,128,4096]{2,1,0:T(8,128)(2,1)}, bf16[1,128,1024]{2,1,0:T(8,128)(2,1)}, bf16[1,128,1024]{2,1,0:T(8,128)(2,1)}) custom-call(bf16[128,512]{1,0:T(8,128)(2,1)} %get-tuple-element.89.refs_0_, bf16[128,512]{1,0:T(8,128)(2,1)} %copy-done.12, bf16[128,512]{1,0:T(8,128)(2,1)} %copy-done.13, ...), custom_call_target="tpu_custom_call" | custom-call | bytes 3670016 | tf_op jit(solution)/shard_map/place/pallas_call | solution.py:344
  129.6 0.0 collective-permute-done.13.refs_4_
  129.6 1.3 collective-permute-done.14.refs_5_
  130.9 0.0 collective-permute-done.15.refs_6_
  130.9 2.3 %collective-permute-done.16.refs_7_ = bf16[128,768]{1,0:T(8,128)(2,1)S(1)} collective-permute-done((bf16[128,768]{1,0:T(8,128)(2,1)}, bf16[128,768]{1,0:T(8,128)(2,1)S(1)}, u32[]{:S(2)}, u32[]{:S(2)}) %collective-permute-start.16) | collective-permute-done | bytes 196640 | tf_op jit(solution)/shard_map/ppermute | solution.py:466
  133.2 0.0 copy-done.5
  133.2 0.0 copy-done.7
  133.3 0.6 copy-done.11
  133.9 2.5 %place.3 = (bf16[1,128,4096]{2,1,0:T(8,128)(2,1)}, bf16[1,128,4096]{2,1,0:T(8,128)(2,1)}, bf16[1,128,1024]{2,1,0:T(8,128)(2,1)}, bf16[1,128,1024]{2,1,0:T(8,128)(2,1)}) custom-call(bf16[128,768]{1,0:T(8,128)(2,1)} %get-tuple-element.77.refs_0_, ...), custom_call_target="tpu_custom_call", output_to_operand_aliasing={{0}: (8, {}), {1}: (9, {}), {2}: (10, {}), {3}: (11, {})} | custom-call | bytes 6815744 | tf_op jit(solution)/shard_map/place/pallas_call | solution.py:344
  136.4 0.0 all-to-all-done.3
  136.4 0.5 fusion
  (27 shorter events, 0.1 us)
Async XLA Ops:
  4.0 49.7 %all-to-all-start = ((bf16[32,32,768]{2,1,0:T(8,128)(2,1)}), bf16[32,32,768]{2,1,0:T(8,128)(2,1)S(1)}, u32[]{:S(2)}, u32[]{:S(2)}) async-start(bf16[32,32,768]{2,1,0:T(8,128)(2,1)} %pack.2), calls=%async_computation | async-start | bytes 3145728 | tf_op jit(solution)/shard_map/all_to_all | solution.py:456
  19.1 16.4 %collective-permute-start = (bf16[8,32,512]{2,1,0:T(8,128)(2,1)}, bf16[8,32,512]{2,1,0:T(8,128)(2,1)S(1)}, u32[]{:S(2)}, u32[]{:S(2)}) collective-permute-start(bf16[8,32,512]{2,1,0:T(8,128)(2,1)} %get-tuple-element.57), channel_id=1, source_target_pairs={{0,8},{8,16},{16,24},{24,0},{1,9},{9,17},{17,25},{25,1},{2,10},{10... | collective-permute-start | bytes 786440 | tf_op jit(solution)/shard_map/ppermute | solution.py:425
  20.4 20.0 %collective-permute-start.1 = (bf16[8,32,512]{2,1,0:T(8,128)(2,1)}, bf16[8,32,512]{2,1,0:T(8,128)(2,1)S(1)}, u32[]{:S(2)}, u32[]{:S(2)}) collective-permute-start(bf16[8,32,512]{2,1,0:T(8,128)(2,1)} %get-tuple-element.58), channel_id=1, source_target_pairs={{0,16},{8,24},{16,0},{24,8},{1,17},{9,25},{17,1},{25,9},{2,18},{10... | collective-permute-start | bytes 786440 | tf_op jit(solution)/shard_map/ppermute | solution.py:425
  22.8 21.7 %collective-permute-start.2 = (bf16[8,32,512]{2,1,0:T(8,128)(2,1)}, bf16[8,32,512]{2,1,0:T(8,128)(2,1)S(1)}, u32[]{:S(2)}, u32[]{:S(2)}) collective-permute-start(bf16[8,32,512]{2,1,0:T(8,128)(2,1)} %get-tuple-element.59), channel_id=1, source_target_pairs={{0,24},{8,0},{16,8},{24,16},{1,25},{9,1},{17,9},{25,17},{2,26},{10... | collective-permute-start | bytes 786440 | tf_op jit(solution)/shard_map/ppermute | solution.py:425
  35.5 8.9 %copy-start.2 = (bf16[8,32,512]{2,1,0:T(8,128)(2,1)}, bf16[8,32,512]{2,1,0:T(8,128)(2,1)S(1)}, u32[]{:S(2)}) copy-start(bf16[8,32,512]{2,1,0:T(8,128)(2,1)S(1)} %collective-permute-done.refs_1_) | copy-start | bytes 786436
  40.4 4.1 %copy-start.3 = (bf16[8,32,512]{2,1,0:T(8,128)(2,1)}, bf16[8,32,512]{2,1,0:T(8,128)(2,1)S(1)}, u32[]{:S(2)}) copy-start(bf16[8,32,512]{2,1,0:T(8,128)(2,1)S(1)} %collective-permute-done.1.refs_2_) | copy-start | bytes 786436
  44.5 0.7 copy-start.4
  53.7 3.6 %copy-start = (bf16[32,32,768]{2,1,0:T(8,128)(2,1)}, bf16[32,32,768]{2,1,0:T(8,128)(2,1)S(1)}, u32[]{:S(2)}) copy-start(bf16[32,32,768]{2,1,0:T(8,128)(2,1)S(1)} %all-to-all-done.refs_5_) | copy-start | bytes 4718596
  53.7 33.1 %all-to-all-start.1 = ((bf16[8,4,32,512]{3,2,1,0:T(8,128)(2,1)}), bf16[8,4,32,512]{3,2,1,0:T(8,128)(2,1)S(1)}, u32[]{:S(2)}, u32[]{:S(2)}) async-start(bf16[8,4,32,512]{3,2,1,0:T(8,128)(2,1)} %regroup.1), calls=%async_computation.1 | async-start | bytes 2097152 | tf_op jit(solution)/shard_map/all_to_all | solution.py:462
  66.8 8.9 %collective-permute-start.3 = (bf16[128,512]{1,0:T(8,128)(2,1)}, bf16[128,512]{1,0:T(8,128)(2,1)S(1)}, u32[]{:S(2)}, u32[]{:S(2)}) collective-permute-start(bf16[128,512]{1,0:T(8,128)(2,1)} %get-tuple-element.63), channel_id=1, source_target_pairs={{0,1},{1,0},{2,3},{3,2},{4,5},{5,4},{6,7},{7,6},{8,9},{9,8},{10,11... | collective-permute-start | bytes 393224 | tf_op jit(solution)/shard_map/ppermute | solution.py:466
  69.5 7.5 %collective-permute-start.4 = (bf16[128,512]{1,0:T(8,128)(2,1)}, bf16[128,512]{1,0:T(8,128)(2,1)S(1)}, u32[]{:S(2)}, u32[]{:S(2)}) collective-permute-start(bf16[128,512]{1,0:T(8,128)(2,1)} %get-tuple-element.64), channel_id=1, source_target_pairs={{0,2},{1,3},{2,4},{3,5},{4,6},{5,7},{6,0},{7,1},{8,10},{9,11},{10,... | collective-permute-start | bytes 393224 | tf_op jit(solution)/shard_map/ppermute | solution.py:466
  70.8 8.5 %collective-permute-start.5 = (bf16[128,512]{1,0:T(8,128)(2,1)}, bf16[128,512]{1,0:T(8,128)(2,1)S(1)}, u32[]{:S(2)}, u32[]{:S(2)}) collective-permute-start(bf16[128,512]{1,0:T(8,128)(2,1)} %get-tuple-element.65), channel_id=1, source_target_pairs={{0,3},{1,2},{2,5},{3,4},{4,7},{5,6},{6,1},{7,0},{8,11},{9,10},{10,... | collective-permute-start | bytes 393224 | tf_op jit(solution)/shard_map/ppermute | solution.py:466
  72.4 10.5 %collective-permute-start.6 = (bf16[128,512]{1,0:T(8,128)(2,1)}, bf16[128,512]{1,0:T(8,128)(2,1)S(1)}, u32[]{:S(2)}, u32[]{:S(2)}) collective-permute-start(bf16[128,512]{1,0:T(8,128)(2,1)} %get-tuple-element.66), channel_id=1, source_target_pairs={{0,4},{1,5},{2,6},{3,7},{4,0},{5,1},{6,2},{7,3},{8,12},{9,13},{10,... | collective-permute-start | bytes 393224 | tf_op jit(solution)/shard_map/ppermute | solution.py:466
  73.6 12.5 %collective-permute-start.7 = (bf16[128,512]{1,0:T(8,128)(2,1)}, bf16[128,512]{1,0:T(8,128)(2,1)S(1)}, u32[]{:S(2)}, u32[]{:S(2)}) collective-permute-start(bf16[128,512]{1,0:T(8,128)(2,1)} %get-tuple-element.67), channel_id=1, source_target_pairs={{0,5},{1,4},{2,7},{3,6},{4,1},{5,0},{6,3},{7,2},{8,13},{9,12},{10,... | collective-permute-start | bytes 393224 | tf_op jit(solution)/shard_map/ppermute | solution.py:466
  75.7 51.6 %copy-start.12 = (bf16[128,512]{1,0:T(8,128)(2,1)}, bf16[128,512]{1,0:T(8,128)(2,1)S(1)}, u32[]{:S(2)}) copy-start(bf16[128,512]{1,0:T(8,128)(2,1)S(1)} %collective-permute-done.3.refs_1_) | copy-start | bytes 393220
  75.7 10.5 %collective-permute-start.8 = (bf16[128,512]{1,0:T(8,128)(2,1)}, bf16[128,512]{1,0:T(8,128)(2,1)S(1)}, u32[]{:S(2)}, u32[]{:S(2)}) collective-permute-start(bf16[128,512]{1,0:T(8,128)(2,1)} %get-tuple-element.68), channel_id=1, source_target_pairs={{0,6},{1,7},{2,0},{3,1},{4,2},{5,3},{6,4},{7,5},{8,14},{9,15},{10,... | collective-permute-start | bytes 393224 | tf_op jit(solution)/shard_map/ppermute | solution.py:466
  77.1 50.2 %copy-start.13 = (bf16[128,512]{1,0:T(8,128)(2,1)}, bf16[128,512]{1,0:T(8,128)(2,1)S(1)}, u32[]{:S(2)}) copy-start(bf16[128,512]{1,0:T(8,128)(2,1)S(1)} %collective-permute-done.4.refs_2_) | copy-start | bytes 393220
  77.1 9.7 %collective-permute-start.9 = (bf16[128,512]{1,0:T(8,128)(2,1)}, bf16[128,512]{1,0:T(8,128)(2,1)S(1)}, u32[]{:S(2)}, u32[]{:S(2)}) collective-permute-start(bf16[128,512]{1,0:T(8,128)(2,1)} %get-tuple-element.69), channel_id=1, source_target_pairs={{0,7},{1,6},{2,1},{3,0},{4,3},{5,2},{6,5},{7,4},{8,15},{9,14},{10,... | collective-permute-start | bytes 393224 | tf_op jit(solution)/shard_map/ppermute | solution.py:466
  79.3 47.9 %copy-start.14 = (bf16[128,512]{1,0:T(8,128)(2,1)}, bf16[128,512]{1,0:T(8,128)(2,1)S(1)}, u32[]{:S(2)}) copy-start(bf16[128,512]{1,0:T(8,128)(2,1)S(1)} %collective-permute-done.5.refs_3_) | copy-start | bytes 393220
  82.9 44.4 %copy-start.15 = (bf16[128,512]{1,0:T(8,128)(2,1)}, bf16[128,512]{1,0:T(8,128)(2,1)S(1)}, u32[]{:S(2)}) copy-start(bf16[128,512]{1,0:T(8,128)(2,1)S(1)} %collective-permute-done.6.refs_4_) | copy-start | bytes 393220
  86.1 41.1 %copy-start.16 = (bf16[128,512]{1,0:T(8,128)(2,1)}, bf16[128,512]{1,0:T(8,128)(2,1)S(1)}, u32[]{:S(2)}) copy-start(bf16[128,512]{1,0:T(8,128)(2,1)S(1)} %collective-permute-done.7.refs_5_) | copy-start | bytes 393220
  86.2 41.1 %copy-start.17 = (bf16[128,512]{1,0:T(8,128)(2,1)}, bf16[128,512]{1,0:T(8,128)(2,1)S(1)}, u32[]{:S(2)}) copy-start(bf16[128,512]{1,0:T(8,128)(2,1)S(1)} %collective-permute-done.8.refs_6_) | copy-start | bytes 393220
  86.8 40.5 %copy-start.18 = (bf16[128,512]{1,0:T(8,128)(2,1)}, bf16[128,512]{1,0:T(8,128)(2,1)S(1)}, u32[]{:S(2)}) copy-start(bf16[128,512]{1,0:T(8,128)(2,1)S(1)} %collective-permute-done.9.refs_7_) | copy-start | bytes 393220
  86.8 1.0 copy-start.1
  98.6 21.4 %all-to-all-start.2 = ((f32[32,16,128]{2,1,0:T(8,128)}), f32[32,16,128]{2,1,0:T(8,128)S(1)}, u32[]{:S(2)}, u32[]{:S(2)}) async-start(f32[32,16,128]{2,1,0:T(8,128)} %get-tuple-element.78), calls=%async_computation.2 | async-start | bytes 524288 | tf_op jit(solution)/shard_map/all_to_all | solution.py:439
  108.4 6.5 %collective-permute-start.10 = (bf16[128,768]{1,0:T(8,128)(2,1)}, bf16[128,768]{1,0:T(8,128)(2,1)S(1)}, u32[]{:S(2)}, u32[]{:S(2)}) collective-permute-start(bf16[128,768]{1,0:T(8,128)(2,1)} %get-tuple-element.79), channel_id=1, source_target_pairs={{0,1},{1,0},{2,3},{3,2},{4,5},{5,4},{6,7},{7,6},{8,9},{9,8},{10,11... | collective-permute-start | bytes 589832 | tf_op jit(solution)/shard_map/ppermute | solution.py:466
  109.0 8.6 %collective-permute-start.11 = (bf16[128,768]{1,0:T(8,128)(2,1)}, bf16[128,768]{1,0:T(8,128)(2,1)S(1)}, u32[]{:S(2)}, u32[]{:S(2)}) collective-permute-start(bf16[128,768]{1,0:T(8,128)(2,1)} %get-tuple-element.80), channel_id=1, source_target_pairs={{0,2},{1,3},{2,4},{3,5},{4,6},{5,7},{6,0},{7,1},{8,10},{9,11},{10,... | collective-permute-start | bytes 589832 | tf_op jit(solution)/shard_map/ppermute | solution.py:466
  111.3 10.3 %collective-permute-start.12 = (bf16[128,768]{1,0:T(8,128)(2,1)}, bf16[128,768]{1,0:T(8,128)(2,1)S(1)}, u32[]{:S(2)}, u32[]{:S(2)}) collective-permute-start(bf16[128,768]{1,0:T(8,128)(2,1)} %get-tuple-element.81), channel_id=1, source_target_pairs={{0,3},{1,2},{2,5},{3,4},{4,7},{5,6},{6,1},{7,0},{8,11},{9,10},{10,... | collective-permute-start | bytes 589832 | tf_op jit(solution)/shard_map/ppermute | solution.py:466
  111.5 18.2 %collective-permute-start.13 = (bf16[128,768]{1,0:T(8,128)(2,1)}, bf16[128,768]{1,0:T(8,128)(2,1)S(1)}, u32[]{:S(2)}, u32[]{:S(2)}) collective-permute-start(bf16[128,768]{1,0:T(8,128)(2,1)} %get-tuple-element.85), channel_id=1, source_target_pairs={{0,4},{1,5},{2,6},{3,7},{4,0},{5,1},{6,2},{7,3},{8,12},{9,13},{10,... | collective-permute-start | bytes 589832 | tf_op jit(solution)/shard_map/ppermute | solution.py:466
  113.1 17.8 %collective-permute-start.14 = (bf16[128,768]{1,0:T(8,128)(2,1)}, bf16[128,768]{1,0:T(8,128)(2,1)S(1)}, u32[]{:S(2)}, u32[]{:S(2)}) collective-permute-start(bf16[128,768]{1,0:T(8,128)(2,1)} %get-tuple-element.86), channel_id=1, source_target_pairs={{0,5},{1,4},{2,7},{3,6},{4,1},{5,0},{6,3},{7,2},{8,13},{9,12},{10,... | collective-permute-start | bytes 589832 | tf_op jit(solution)/shard_map/ppermute | solution.py:466
  114.9 18.4 %copy-start.5 = (bf16[128,768]{1,0:T(8,128)(2,1)}, bf16[128,768]{1,0:T(8,128)(2,1)S(1)}, u32[]{:S(2)}) copy-start(bf16[128,768]{1,0:T(8,128)(2,1)S(1)} %collective-permute-done.10.refs_1_) | copy-start | bytes 589828
  114.9 16.0 %collective-permute-start.15 = (bf16[128,768]{1,0:T(8,128)(2,1)}, bf16[128,768]{1,0:T(8,128)(2,1)S(1)}, u32[]{:S(2)}, u32[]{:S(2)}) collective-permute-start(bf16[128,768]{1,0:T(8,128)(2,1)} %get-tuple-element.87), channel_id=1, source_target_pairs={{0,6},{1,7},{2,0},{3,1},{4,2},{5,3},{6,4},{7,5},{8,14},{9,15},{10,... | collective-permute-start | bytes 589832 | tf_op jit(solution)/shard_map/ppermute | solution.py:466
  117.6 15.7 %copy-start.6 = (bf16[128,768]{1,0:T(8,128)(2,1)}, bf16[128,768]{1,0:T(8,128)(2,1)S(1)}, u32[]{:S(2)}) copy-start(bf16[128,768]{1,0:T(8,128)(2,1)S(1)} %collective-permute-done.11.refs_2_) | copy-start | bytes 589828
  117.6 15.7 %collective-permute-start.16 = (bf16[128,768]{1,0:T(8,128)(2,1)}, bf16[128,768]{1,0:T(8,128)(2,1)S(1)}, u32[]{:S(2)}, u32[]{:S(2)}) collective-permute-start(bf16[128,768]{1,0:T(8,128)(2,1)} %get-tuple-element.88), channel_id=1, source_target_pairs={{0,7},{1,6},{2,1},{3,0},{4,3},{5,2},{6,5},{7,4},{8,15},{9,14},{10,... | collective-permute-start | bytes 589832 | tf_op jit(solution)/shard_map/ppermute | solution.py:466
  121.6 11.6 %copy-start.7 = (bf16[128,768]{1,0:T(8,128)(2,1)}, bf16[128,768]{1,0:T(8,128)(2,1)S(1)}, u32[]{:S(2)}) copy-start(bf16[128,768]{1,0:T(8,128)(2,1)S(1)} %collective-permute-done.12.refs_3_) | copy-start | bytes 589828
  122.3 14.2 %all-to-all-start.3 = ((f32[8,16,128]{2,1,0:T(8,128)}), f32[8,16,128]{2,1,0:T(8,128)S(1)}, u32[]{:S(2)}, u32[]{:S(2)}) async-start(f32[8,16,128]{2,1,0:T(8,128)} %broadcast_in_dim.3), calls=%async_computation.3 | async-start | bytes 131072 | tf_op jit(solution)/shard_map/all_to_all | solution.py:439
  129.6 3.6 %copy-start.8 = (bf16[128,768]{1,0:T(8,128)(2,1)}, bf16[128,768]{1,0:T(8,128)(2,1)S(1)}, u32[]{:S(2)}) copy-start(bf16[128,768]{1,0:T(8,128)(2,1)S(1)} %collective-permute-done.13.refs_4_) | copy-start | bytes 589828
  130.9 2.3 %copy-start.9 = (bf16[128,768]{1,0:T(8,128)(2,1)}, bf16[128,768]{1,0:T(8,128)(2,1)S(1)}, u32[]{:S(2)}) copy-start(bf16[128,768]{1,0:T(8,128)(2,1)S(1)} %collective-permute-done.14.refs_5_) | copy-start | bytes 589828
  130.9 2.3 %copy-start.10 = (bf16[128,768]{1,0:T(8,128)(2,1)}, bf16[128,768]{1,0:T(8,128)(2,1)S(1)}, u32[]{:S(2)}) copy-start(bf16[128,768]{1,0:T(8,128)(2,1)S(1)} %collective-permute-done.15.refs_6_) | copy-start | bytes 589828
  133.2 0.7 copy-start.11

commit v4 on v3

--- a/solution.py
+++ b/solution.py
@@ -12,9 +12,10 @@
 SLOT = 1024
 TILE = 256
 REACH = 512
-CHUNKS = (2, 2)
+CHUNKS = (3, 1)
 SUM_ROWS = 16
 DP = ("z", "x")
+HEAD = ("y", "c")
 GROUPS = ((0, 256, 512, 768),)
 EPSILON = 1e-06
 NEG_FILL = -1e30
@@ -78,14 +79,11 @@
     ]
     for group in loads:
         start_all(group)
-    stores = []
     if len(outs) == 1:
         for g, group in enumerate(loads):
             wait_all(group)
             for s in range(g * span, (g + 1) * span):
-                copy = pltpu.make_async_copy(stage.at[s], outs[0].at[owners[s]], out_sems.at[s])
-                copy.start()
-                stores.append(copy)
+                pltpu.make_async_copy(stage.at[s], outs[0].at[owners[s]], out_sems.at[0]).start()
     else:
         for s in range(seqs):
             holder[owners[s]] = s
@@ -95,10 +93,9 @@
             x = lax.rem(lax.axis_index("x") + k, len(outs))
             for z in range(out.shape[0]):
                 s = holder[z * len(outs) + x]
-                copy = pltpu.make_async_copy(stage.at[s], out.at[z], out_sems.at[k * out.shape[0] + z])
-                copy.start()
-                stores.append(copy)
-    wait_all(stores)
+                pltpu.make_async_copy(stage.at[s], out.at[z], out_sems.at[k]).start()
+    for k, out in enumerate(outs):
+        pltpu.make_async_copy(out, out, out_sems.at[k]).wait()
 
 
 def regroup(*refs):
@@ -116,8 +113,7 @@
 
 
 def my_place():
-    head = lax.axis_index("head")
-    return head // 2, lax.rem(head, 2)
+    return lax.axis_index("y"), lax.axis_index("c")
 
 
 def attend(heads, first, last, *refs):
@@ -135,7 +131,7 @@
     else:
         carry_out = refs[:6]
         del refs[:6]
-    kv, own, send, kn, knt, vt, dk, dv, q_acc, in_sems, carry_sems, out_sem = refs
+    kv, own, send, kn, knt, vt, dk, dv, q_acc, *prior, in_sems, carry_sems, out_sem = refs
     kept = (kn, knt, vt, dk, dv, q_acc)
 
     def column(n):
@@ -150,7 +146,8 @@
         pltpu.make_async_copy(own_hbm.at[:, :, column(n)], own.at[n], in_sems.at[n + 2])
         for n in (m for h in range(heads) for m in (h, heads + h))
     ]
-    start_all(kv_in + own_in)
+    if first:
+        start_all(kv_in + own_in)
 
     def own_wait(n):
         return pltpu.make_async_copy(own.at[n], own.at[n], in_sems.at[n + 2])
@@ -158,9 +155,9 @@
     if not first:
         carry = [
             pltpu.make_async_copy(a, b, carry_sems.at[n])
-            for n, (a, b) in enumerate(zip(carry_in, kept))
+            for n, (a, b) in enumerate(zip(carry_in, (kn, knt, vt, *prior)))
         ]
-        start_all(carry)
+        start_all(carry[:1] + own_in[:2] + kv_in[1:] + carry[1:3] + own_in[2:] + kv_in[:1] + carry[3:])
 
     eye = identity(WIDTH)
     eye_tile = identity(TILE)
@@ -180,10 +177,10 @@
         start = start + jnp.where(doc_row > d, count, 0)
     gain = jnp.broadcast_to(q_gain[...], (TILE, WIDTH)).T
     y, c = my_place()
+    dk[...] = jnp.zeros_like(dk)
+    dv[...] = jnp.zeros_like(dv)
+    q_acc[...] = jnp.zeros_like(q_acc)
     if first:
-        dk[...] = jnp.zeros_like(dk)
-        dv[...] = jnp.zeros_like(dv)
-        q_acc[...] = jnp.zeros_like(q_acc)
         wait_all(kv_in)
         for at in range(0, SLOT, TILE):
             part = pl.ds(at, TILE)
@@ -192,7 +189,7 @@
             knt[:, part] = dot_t(eye, normed).astype(BF)
             vt[:, part] = dot_t(eye, rows(kv, 1, at, TILE)).astype(BF)
     else:
-        wait_all(kv_in + carry)
+        wait_all(kv_in[1:] + carry[:3])
     u_rel = lax.broadcasted_iota(jnp.int32, (TILE, TILE), 0)
     t_rel = lax.broadcasted_iota(jnp.int32, (1, TILE), 1)
 
@@ -270,6 +267,10 @@
                     send[t // TILE, n, :, cols] = block[n * WIDTH : (n + 1) * WIDTH]
 
     def finish():
+        if not first:
+            wait_all(kv_in[:1] + carry[3:])
+            for ref, before in zip((dk, dv, q_acc), prior):
+                ref[...] += before[...]
         k_sum = jnp.zeros((1, WIDTH), F32)
         for at in range(0, SLOT, WIDTH):
             part = pl.ds(at, WIDTH)
@@ -377,12 +378,12 @@
         pltpu.VMEM((2, SLOT // per_src, per_src, WIDTH), BF),
         pltpu.VMEM((2 * heads, SLOT // per_src, per_src, WIDTH), BF),
         pltpu.VMEM((4, 2, WIDTH, width), BF),
-        *(pltpu.VMEM(*a) for a in kept),
+        *(pltpu.VMEM(*a) for a in (kept if first else kept + kept[3:])),
         pltpu.SemaphoreType.DMA((2 + 2 * heads,)),
         pltpu.SemaphoreType.DMA((len(kept),)),
         pltpu.SemaphoreType.DMA((8,)),
     ]
-    outs += [shape((kv.shape[0], SUM_ROWS, WIDTH), F32)] if last else [shape(*a) for a in kept]
+    outs += [shape((16, SUM_ROWS, WIDTH), F32)] if last else [shape(*a) for a in kept]
     result = call(
         functools.partial(attend, heads, first, last),
         args,
@@ -415,7 +416,7 @@
             pltpu.VMEM((seqs, per_src, width), BF),
             pltpu.SMEM((seqs,), jnp.int32),
             pltpu.SemaphoreType.DMA((4, len(pieces))),
-            pltpu.SemaphoreType.DMA((seqs,)),
+            pltpu.SemaphoreType.DMA((count,)),
         ],
         "pack",
     )
@@ -442,7 +443,7 @@
 def per_device(query, key, value, grad, q_gain, k_gain, lengths, owners, doc_ids):
     seqs, _, features = query.shape
     heads = features // WIDTH
-    head_devs = lax.axis_size("head")
+    head_devs = lax.axis_size(HEAD)
     small = (owners, lengths, doc_ids, q_gain.reshape(1, WIDTH), k_gain.reshape(1, WIDTH))
     chunks, at = [], 0
     for count in CHUNKS:
@@ -460,12 +461,15 @@
         if not last:
             owned[n], chunk = lax.optimization_barrier((owned[n], chunks[n + 1]))
             owned.append(lax.all_to_all(chunk, "z", 0, 0, tiled=True).reshape(seqs, *query.shape[1:2], -1))
+        out, carry = attend_chunk(count, n == 0, last, *small, owned[0], owned[n], carry)
         if n > 0:
-            owned[n], received[-1] = lax.optimization_barrier((owned[n], received[-1]))
-        out, carry = attend_chunk(count, n == 0, last, *small, owned[0], owned[n], carry)
-        received.append([out[0]] + [lax.ppermute(out[r], "head", across(r)) for r in range(1, 8)])
-    sums, received[-1][1:4] = lax.optimization_barrier((total(carry[0], DP), received[-1][1:4]))
-    sums = total(jnp.broadcast_to(sums, (head_devs, *sums.shape)), "head")
+            out, received[-1] = lax.optimization_barrier((out, received[-1]))
+        got = [out[0]] * 8
+        for r in (4, 5, 2, 3, 6, 7, 1):
+            got[r] = lax.ppermute(out[r], HEAD, across(r))
+        received.append(got)
+    sums, received[-1][1:2] = lax.optimization_barrier((total(carry[0], ("z", "c")), received[-1][1:2]))
+    sums = total(jnp.broadcast_to(sums, carry[0].shape), ("x", "y"))
     wide, narrow = shape((1, WIDTH, heads * head_devs * WIDTH)), shape((1, WIDTH, head_devs * WIDTH))
     outs, at = [], 0
     for n, (count, got) in enumerate(zip(CHUNKS, received)):
@@ -493,10 +497,9 @@
 
 
 def solution(mesh):
-    dp, head = mesh.devices.shape
-    grid = Mesh(mesh.devices.reshape(dp // 4, 4, head), (*DP, "head"))
-    spread = P(None, DP, "head")
-    packed = P(DP, "head", None)
+    grid = Mesh(mesh.devices.reshape(8, 4, 4, 2), (*DP, *HEAD))
+    spread = P(None, DP, HEAD)
+    packed = P(DP, HEAD, None)
     return jax.shard_map(
         per_device,
         mesh=grid,

time: 138 us -> 132 us (0.957)
  starting transfers between devices: 58.2 us -> 53.2 us
    all_to_all x1, waiting for transfers between devices: 6.34 us -> 25.3 us  [per_device(): owned = [lax.all_to_all(chunks[0], DP, 0, 0, tiled=True)]]
    ppermute x14, waiting for transfers between devices: 13.1 us -> 0.79 us  [per_device(): got[r] = lax.ppermute(out[r], HEAD, across(r))]
    ppermute x3, waiting for transfers between devices: 20.5 us -> 13 us  [packed_chunk(): lax.ppermute(parts[k], 'x', shift[k])]
    all_to_all x2, starting transfers between devices: 14.7 us -> 11.1 us  [total(): return jnp.sum(lax.all_to_all(spread, axis, 0, 0, tiled=True), axis=0)]
    all_to_all x2, waiting for transfers between devices: 0.43 us -> 1.93 us  [total(): return jnp.sum(lax.all_to_all(spread, axis, 0, 0, tiled=True), axis=0)]
  transfers between devices with their start and end apart: 21 -> 21, of which waited for: 12 -> 8; matrix products, arithmetic and copies ran while one was open for 1% -> 1% of each run, Pallas kernels for 14% -> 22%
where the time goes in v4:
time: 132 us; the launch traced here: 131 us
  starting transfers between devices  53.2 us (40%)
  waiting for transfers between devices  41.1 us (31%)
  Pallas kernels  32.6 us (25%)
  local copies, waits for them, and re-layouts  2.81 us (2%)
    pallas_call x7, Pallas kernels, call(): pl.pallas_call(kernel, out_shape=outs, in_specs=in_specs, out_specs=out_s...  32.6 us
    all_to_all x1, waiting for transfers between devices, per_device(): owned = [lax.all_to_all(chunks[0], DP, 0, 0, tiled=True)]  25.3 us
    ppermute x14, starting transfers between devices, per_device(): got[r] = lax.ppermute(out[r], HEAD, across(r))  21.9 us
    ppermute x3, waiting for transfers between devices, packed_chunk(): lax.ppermute(parts[k], 'x', shift[k])  13 us
    all_to_all x1, starting transfers between devices, per_device(): owned = [lax.all_to_all(chunks[0], DP, 0, 0, tiled=True)]  11.9 us
    all_to_all x2, starting transfers between devices, total(): return jnp.sum(lax.all_to_all(spread, axis, 0, 0, tiled=True), axis=0)  11.1 us
    ppermute x3, starting transfers between devices, packed_chunk(): lax.ppermute(parts[k], 'x', shift[k])  4.88 us
    all_to_all x1, starting transfers between devices, per_device(): lax.all_to_all(chunk, 'z', 0, 0, tiled=True)  3.49 us
  transfers between devices with their start and end apart: 21, of which 8 were waited for; matrix products, arithmetic and copies ran while one was open for 1% of the time, Pallas kernels for 22%

profile of v4, /device:TPU:1, one launch (start us, length us, event | category | flops | bytes accessed | tf_op | source)
XLA Modules:
  0.0 131.3 jit_solution(2131746312331751527)
XLA Ops:
  0.6 3.2 %pack.2 = bf16[32,32,1024]{2,1,0:T(8,128)(2,1)} custom-call(s32[32]{0:T(128)} %refs_0_.7, bf16[32,32,512]{2,1,0:T(8,128)(2,1)} %refs_0_.5, bf16[32,32,512]{2,1,0:T(8,128)(2,1)} %refs_1_.5, bf16[32,32,128]{2,1,0:T(8,128)(2,1)} %refs_2_.3, bf16[32,32,128]{2,1,0:T(8,128)(2,1)} %refs_3_.1), custom_call_target="tpu_custom_call" | custom-call | bytes 4718720 | tf_op jit(solution)/shard_map/pack/pallas_call | solution.py:345
  3.9 11.9 %all-to-all-start = ((bf16[32,32,1024]{2,1,0:T(8,128)(2,1)}), bf16[32,32,1024]{2,1,0:T(8,128)(2,1)S(1)}, u32[]{:S(2)}, u32[]{:S(2)}) async-start(bf16[32,32,1024]{2,1,0:T(8,128)(2,1)} %pack.2), calls=%async_computation | async-start | bytes 4194304 | tf_op jit(solution)/shard_map/all_to_all | solution.py:457
  15.8 2.6 %pack.3 = (bf16[8,32,256]{2,1,0:T(8,128)(2,1)}, bf16[8,32,256]{2,1,0:T(8,128)(2,1)}, bf16[8,32,256]{2,1,0:T(8,128)(2,1)}, bf16[8,32,256]{2,1,0:T(8,128)(2,1)}) custom-call(s32[32]{0:T(128)} %refs_0_.7, bf16[32,32,512]{2,1,0:T(8,128)(2,1)} %refs_0_.5, bf16[32,32,512]{2,1,0:T(8,128)(2,1)} %refs_1_.5), custom_call_target="tpu_custom_call" | custom-call | bytes 2621568 | tf_op jit(solution)/shard_map/pack/pallas_call | solution.py:345
  18.4 1.3 collective-permute-start
  19.7 2.4 %collective-permute-start.1 = (bf16[8,32,256]{2,1,0:T(8,128)(2,1)}, bf16[8,32,256]{2,1,0:T(8,128)(2,1)S(1)}, u32[]{:S(2)}, u32[]{:S(2)}) collective-permute-start(bf16[8,32,256]{2,1,0:T(8,128)(2,1)} %get-tuple-element.63), channel_id=1, source_target_pairs={{0,16},{8,24},{16,0},{24,8},{1,17},{9,25},{17,1},{25,9},{2,18},{10... | collective-permute-start | bytes 393224 | tf_op jit(solution)/shard_map/ppermute | solution.py:426
  22.1 1.2 collective-permute-start.2
  23.3 2.8 %collective-permute-done.refs_1_ = bf16[8,32,256]{2,1,0:T(8,128)(2,1)S(1)} collective-permute-done((bf16[8,32,256]{2,1,0:T(8,128)(2,1)}, bf16[8,32,256]{2,1,0:T(8,128)(2,1)S(1)}, u32[]{:S(2)}, u32[]{:S(2)}) %collective-permute-start) | collective-permute-done | bytes 131104 | tf_op jit(solution)/shard_map/ppermute | solution.py:426
  26.1 3.6 %collective-permute-done.1.refs_2_ = bf16[8,32,256]{2,1,0:T(8,128)(2,1)S(1)} collective-permute-done((bf16[8,32,256]{2,1,0:T(8,128)(2,1)}, bf16[8,32,256]{2,1,0:T(8,128)(2,1)S(1)}, u32[]{:S(2)}, u32[]{:S(2)}) %collective-permute-start.1) | collective-permute-done | bytes 131104 | tf_op jit(solution)/shard_map/ppermute | solution.py:426
  29.7 6.6 %collective-permute-done.2.refs_3_ = bf16[8,32,256]{2,1,0:T(8,128)(2,1)S(1)} collective-permute-done((bf16[8,32,256]{2,1,0:T(8,128)(2,1)}, bf16[8,32,256]{2,1,0:T(8,128)(2,1)S(1)}, u32[]{:S(2)}, u32[]{:S(2)}) %collective-permute-start.2) | collective-permute-done | bytes 131104 | tf_op jit(solution)/shard_map/ppermute | solution.py:426
  36.3 0.0 copy-done.16
  36.3 0.0 copy-done.17
  36.3 0.6 copy-done.18
  37.0 1.9 %regroup.1 = bf16[8,4,32,256]{3,2,1,0:T(8,128)(2,1)} custom-call(bf16[8,32,256]{2,1,0:T(8,128)(2,1)} %get-tuple-element.61.refs_0_, bf16[8,32,256]{2,1,0:T(8,128)(2,1)} %copy-done.16, bf16[8,32,256]{2,1,0:T(8,128)(2,1)} %copy-done.17, bf16[8,32,256]{2,1,0:T(8,128)(2,1)} %copy-done.18), custom_call_target="tpu_custom_call" | custom-call | bytes 1048576 | tf_op jit(solution)/shard_map/regroup/pallas_call | solution.py:345
  38.9 25.3 %all-to-all-done.refs_5_ = bf16[32,32,1024]{2,1,0:T(8,128)(2,1)S(1)} async-done(((bf16[32,32,1024]{2,1,0:T(8,128)(2,1)}), bf16[32,32,1024]{2,1,0:T(8,128)(2,1)S(1)}, u32[]{:S(2)}, u32[]{:S(2)}) %all-to-all-start) | async-done | bytes 2097184 | tf_op jit(solution)/shard_map/all_to_all | solution.py:457
  64.2 3.5 %all-to-all-start.1 = ((bf16[8,4,32,256]{3,2,1,0:T(8,128)(2,1)}), bf16[8,4,32,256]{3,2,1,0:T(8,128)(2,1)S(1)}, u32[]{:S(2)}, u32[]{:S(2)}) async-start(bf16[8,4,32,256]{3,2,1,0:T(8,128)(2,1)} %regroup.1), calls=%async_computation.1 | async-start | bytes 1048576 | tf_op jit(solution)/shard_map/all_to_all | solution.py:463
  67.8 0.0 copy-done
  67.8 12.3 %attend.2 = (bf16[128,768]{1,0:T(8,128)(2,1)}, bf16[128,768]{1,0:T(8,128)(2,1)}, bf16[128,768]{1,0:T(8,128)(2,1)}, bf16[128,768]{1,0:T(8,128)(2,1)}, bf16[128,76...) custom-call(s32[32]{0:T(128)} %refs_0_.7, ...), custom_call_target="tpu_custom_call" | custom-call | flops 2717908992 | bytes 5768448 | tf_op jit(solution)/shard_map/attend/pallas_call | solution.py:345
  80.1 3.2 %collective-permute-start.3 = (bf16[128,768]{1,0:T(8,128)(2,1)}, bf16[128,768]{1,0:T(8,128)(2,1)S(1)}, u32[]{:S(2)}, u32[]{:S(2)}) collective-permute-start(bf16[128,768]{1,0:T(8,128)(2,1)} %get-tuple-element.82), channel_id=1, source_target_pairs={{0,1},{1,0},{2,3},{3,2},{4,5},{5,4},{6,7},{7,6},{8,9},{9,8},{10,11... | collective-permute-start | bytes 589832 | tf_op jit(solution)/shard_map/ppermute | solution.py:469
  83.3 1.3 collective-permute-start.4
  84.6 1.5 %collective-permute-start.5 = (bf16[128,768]{1,0:T(8,128)(2,1)}, bf16[128,768]{1,0:T(8,128)(2,1)S(1)}, u32[]{:S(2)}, u32[]{:S(2)}) collective-permute-start(bf16[128,768]{1,0:T(8,128)(2,1)} %get-tuple-element.84), channel_id=1, source_target_pairs={{0,3},{1,2},{2,5},{3,4},{4,7},{5,6},{6,1},{7,0},{8,11},{9,10},{10,... | collective-permute-start | bytes 589832 | tf_op jit(solution)/shard_map/ppermute | solution.py:469
  86.1 1.3 collective-permute-start.6
  87.4 2.0 %collective-permute-start.7 = (bf16[128,768]{1,0:T(8,128)(2,1)}, bf16[128,768]{1,0:T(8,128)(2,1)S(1)}, u32[]{:S(2)}, u32[]{:S(2)}) collective-permute-start(bf16[128,768]{1,0:T(8,128)(2,1)} %get-tuple-element.86), channel_id=1, source_target_pairs={{0,5},{1,4},{2,7},{3,6},{4,1},{5,0},{6,3},{7,2},{8,13},{9,12},{10,... | collective-permute-start | bytes 589832 | tf_op jit(solution)/shard_map/ppermute | solution.py:469
  89.5 0.0 collective-permute-done.3.refs_1_
  89.5 1.4 %collective-permute-start.8 = (bf16[128,768]{1,0:T(8,128)(2,1)}, bf16[128,768]{1,0:T(8,128)(2,1)S(1)}, u32[]{:S(2)}, u32[]{:S(2)}) collective-permute-start(bf16[128,768]{1,0:T(8,128)(2,1)} %get-tuple-element.87), channel_id=1, source_target_pairs={{0,6},{1,7},{2,0},{3,1},{4,2},{5,3},{6,4},{7,5},{8,14},{9,15},{10,... | collective-permute-start | bytes 589832 | tf_op jit(solution)/shard_map/ppermute | solution.py:469
  90.8 0.4 collective-permute-done.4.refs_2_
  91.3 2.6 %collective-permute-start.9 = (bf16[128,768]{1,0:T(8,128)(2,1)}, bf16[128,768]{1,0:T(8,128)(2,1)S(1)}, u32[]{:S(2)}, u32[]{:S(2)}) collective-permute-start(bf16[128,768]{1,0:T(8,128)(2,1)} %get-tuple-element.88), channel_id=1, source_target_pairs={{0,7},{1,6},{2,1},{3,0},{4,3},{5,2},{6,5},{7,4},{8,15},{9,14},{10,... | collective-permute-start | bytes 589832 | tf_op jit(solution)/shard_map/ppermute | solution.py:469
  93.9 0.0 all-to-all-done.1
  93.9 0.8 copy-done.1
  94.7 7.7 %attend.3 = (bf16[128,512]{1,0:T(8,128)(2,1)}, bf16[128,512]{1,0:T(8,128)(2,1)}, bf16[128,512]{1,0:T(8,128)(2,1)}, bf16[128,512]{1,0:T(8,128)(2,1)}, bf16[128,51...) custom-call(s32[32]{0:T(128)} %refs_0_.7, ...), custom_call_target="tpu_custom_call" | custom-call | flops 905969664 | bytes 5899520 | tf_op jit(solution)/shard_map/attend/pallas_call | solution.py:345
  102.5 7.3 %all-to-all-start.2 = ((f32[16,16,128]{2,1,0:T(8,128)}), f32[16,16,128]{2,1,0:T(8,128)S(1)}, u32[]{:S(2)}, u32[]{:S(2)}) async-start(f32[16,16,128]{2,1,0:T(8,128)} %get-tuple-element.90), calls=%async_computation.2 | async-start | bytes 262144 | tf_op jit(solution)/shard_map/all_to_all | solution.py:440
  109.8 0.0 collective-permute-done.5.refs_3_
  109.8 0.0 copy-start.4
  109.8 0.0 collective-permute-done.6.refs_4_
  109.8 0.0 copy-start.5
  109.8 0.0 collective-permute-done.7.refs_5_
  109.8 0.0 collective-permute-done.8.refs_6_
  109.9 0.0 copy-start.7
  109.9 0.0 collective-permute-done.9.refs_7_
  109.9 0.2 collective-permute-start.10
  110.1 0.0 collective-permute-start.11
  110.1 0.6 collective-permute-start.12
  110.7 3.8 %collective-permute-start.13 = (bf16[128,512]{1,0:T(8,128)(2,1)}, bf16[128,512]{1,0:T(8,128)(2,1)S(1)}, u32[]{:S(2)}, u32[]{:S(2)}) collective-permute-start(bf16[128,512]{1,0:T(8,128)(2,1)} %get-tuple-element.95), channel_id=1, source_target_pairs={{0,4},{1,5},{2,6},{3,7},{4,0},{5,1},{6,2},{7,3},{8,12},{9,13},{10,... | collective-permute-start | bytes 393224 | tf_op jit(solution)/shard_map/ppermute | solution.py:469
  114.5 0.0 collective-permute-start.14
  114.5 0.0 collective-permute-done.10.refs_1_
  114.5 2.1 %collective-permute-start.15 = (bf16[128,512]{1,0:T(8,128)(2,1)}, bf16[128,512]{1,0:T(8,128)(2,1)S(1)}, u32[]{:S(2)}, u32[]{:S(2)}) collective-permute-start(bf16[128,512]{1,0:T(8,128)(2,1)} %get-tuple-element.97), channel_id=1, source_target_pairs={{0,6},{1,7},{2,0},{3,1},{4,2},{5,3},{6,4},{7,5},{8,14},{9,15},{10,... | collective-permute-start | bytes 393224 | tf_op jit(solution)/shard_map/ppermute | solution.py:469
  116.6 0.0 collective-permute-done.11.refs_2_
  116.6 1.8 %collective-permute-start.16 = (bf16[128,512]{1,0:T(8,128)(2,1)}, bf16[128,512]{1,0:T(8,128)(2,1)S(1)}, u32[]{:S(2)}, u32[]{:S(2)}) collective-permute-start(bf16[128,512]{1,0:T(8,128)(2,1)} %get-tuple-element.98), channel_id=1, source_target_pairs={{0,7},{1,6},{2,1},{3,0},{4,3},{5,2},{6,5},{7,4},{8,15},{9,14},{10,... | collective-permute-start | bytes 393224 | tf_op jit(solution)/shard_map/ppermute | solution.py:469
  118.4 0.6 all-to-all-done.2
  119.0 0.7 broadcast_in_dim.3
  119.6 3.8 %all-to-all-start.3 = ((f32[16,16,128]{2,1,0:T(8,128)}), f32[16,16,128]{2,1,0:T(8,128)S(1)}, u32[]{:S(2)}, u32[]{:S(2)}) async-start(f32[16,16,128]{2,1,0:T(8,128)} %broadcast_in_dim.3), calls=%async_computation.3 | async-start | bytes 262144 | tf_op jit(solution)/shard_map/all_to_all | solution.py:440
  123.5 2.5 %place.2 = (bf16[1,128,4096]{2,1,0:T(8,128)(2,1)}, bf16[1,128,4096]{2,1,0:T(8,128)(2,1)}, bf16[1,128,1024]{2,1,0:T(8,128)(2,1)}, bf16[1,128,1024]{2,1,0:T(8,128)(2,1)}) custom-call(bf16[128,768]{1,0:T(8,128)(2,1)} %get-tuple-element.99.refs_0_, bf16[128,768]{1,0:T(8,128)(2,1)} %copy-done.2, bf16[128,768]{1,0:T(8,128)(2,1)} %copy-done.3, ...), custom_call_target="tpu_custom_call" | custom-call | bytes 4194304 | tf_op jit(solution)/shard_map/place/pallas_call | solution.py:345
  126.1 0.0 collective-permute-done.12.refs_3_
  126.1 0.0 collective-permute-done.13.refs_4_
  126.1 0.0 collective-permute-done.14.refs_5_
  126.1 0.0 collective-permute-done.15.refs_6_
  126.1 0.3 collective-permute-done.16.refs_7_
  126.5 0.3 copy-done.11
  126.7 0.1 copy-done.12
  126.8 0.0 copy-done.13
  126.8 0.0 copy-done.14
  126.9 0.2 copy-done.15
  127.1 2.3 %place.3 = (bf16[1,128,4096]{2,1,0:T(8,128)(2,1)}, bf16[1,128,4096]{2,1,0:T(8,128)(2,1)}, bf16[1,128,1024]{2,1,0:T(8,128)(2,1)}, bf16[1,128,1024]{2,1,0:T(8,128)(2,1)}) custom-call(bf16[128,512]{1,0:T(8,128)(2,1)} %get-tuple-element.89.refs_0_, ...), custom_call_target="tpu_custom_call", output_to_operand_aliasing={{0}: (8, {}), {1}: (9, {}), {2}: (10, {}), {3}: (11, {})} | custom-call | bytes 6291456 | tf_op jit(solution)/shard_map/place/pallas_call | solution.py:345
  129.4 1.3 %all-to-all-done.3 = f32[16,16,128]{2,1,0:T(8,128)S(1)} async-done(((f32[16,16,128]{2,1,0:T(8,128)}), f32[16,16,128]{2,1,0:T(8,128)S(1)}, u32[]{:S(2)}, u32[]{:S(2)}) %all-to-all-start.3) | async-done | bytes 131104 | tf_op jit(solution)/shard_map/all_to_all | solution.py:440
  130.8 0.5 fusion
  (27 shorter events, 0.1 us)
Async XLA Ops:
  3.9 60.4 %all-to-all-start = ((bf16[32,32,1024]{2,1,0:T(8,128)(2,1)}), bf16[32,32,1024]{2,1,0:T(8,128)(2,1)S(1)}, u32[]{:S(2)}, u32[]{:S(2)}) async-start(bf16[32,32,1024]{2,1,0:T(8,128)(2,1)} %pack.2), calls=%async_computation | async-start | bytes 4194304 | tf_op jit(solution)/shard_map/all_to_all | solution.py:457
  18.4 7.7 %collective-permute-start = (bf16[8,32,256]{2,1,0:T(8,128)(2,1)}, bf16[8,32,256]{2,1,0:T(8,128)(2,1)S(1)}, u32[]{:S(2)}, u32[]{:S(2)}) collective-permute-start(bf16[8,32,256]{2,1,0:T(8,128)(2,1)} %get-tuple-element.62), channel_id=1, source_target_pairs={{0,8},{8,16},{16,24},{24,0},{1,9},{9,17},{17,25},{25,1},{2,10},{10... | collective-permute-start | bytes 393224 | tf_op jit(solution)/shard_map/ppermute | solution.py:426
  19.7 10.0 %collective-permute-start.1 = (bf16[8,32,256]{2,1,0:T(8,128)(2,1)}, bf16[8,32,256]{2,1,0:T(8,128)(2,1)S(1)}, u32[]{:S(2)}, u32[]{:S(2)}) collective-permute-start(bf16[8,32,256]{2,1,0:T(8,128)(2,1)} %get-tuple-element.63), channel_id=1, source_target_pairs={{0,16},{8,24},{16,0},{24,8},{1,17},{9,25},{17,1},{25,9},{2,18},{10... | collective-permute-start | bytes 393224 | tf_op jit(solution)/shard_map/ppermute | solution.py:426
  22.1 14.2 %collective-permute-start.2 = (bf16[8,32,256]{2,1,0:T(8,128)(2,1)}, bf16[8,32,256]{2,1,0:T(8,128)(2,1)S(1)}, u32[]{:S(2)}, u32[]{:S(2)}) collective-permute-start(bf16[8,32,256]{2,1,0:T(8,128)(2,1)} %get-tuple-element.64), channel_id=1, source_target_pairs={{0,24},{8,0},{16,8},{24,16},{1,25},{9,1},{17,9},{25,17},{2,26},{10... | collective-permute-start | bytes 393224 | tf_op jit(solution)/shard_map/ppermute | solution.py:426
  26.1 10.3 %copy-start.16 = (bf16[8,32,256]{2,1,0:T(8,128)(2,1)}, bf16[8,32,256]{2,1,0:T(8,128)(2,1)S(1)}, u32[]{:S(2)}) copy-start(bf16[8,32,256]{2,1,0:T(8,128)(2,1)S(1)} %collective-permute-done.refs_1_) | copy-start | bytes 393220
  29.7 6.6 %copy-start.17 = (bf16[8,32,256]{2,1,0:T(8,128)(2,1)}, bf16[8,32,256]{2,1,0:T(8,128)(2,1)S(1)}, u32[]{:S(2)}) copy-start(bf16[8,32,256]{2,1,0:T(8,128)(2,1)S(1)} %collective-permute-done.1.refs_2_) | copy-start | bytes 393220
  36.3 0.7 copy-start.18
  64.2 3.5 %copy-start = (bf16[32,32,1024]{2,1,0:T(8,128)(2,1)}, bf16[32,32,1024]{2,1,0:T(8,128)(2,1)S(1)}, u32[]{:S(2)}) copy-start(bf16[32,32,1024]{2,1,0:T(8,128)(2,1)S(1)} %all-to-all-done.refs_5_) | copy-start | bytes 6291460
  64.2 29.7 %all-to-all-start.1 = ((bf16[8,4,32,256]{3,2,1,0:T(8,128)(2,1)}), bf16[8,4,32,256]{3,2,1,0:T(8,128)(2,1)S(1)}, u32[]{:S(2)}, u32[]{:S(2)}) async-start(bf16[8,4,32,256]{3,2,1,0:T(8,128)(2,1)} %regroup.1), calls=%async_computation.1 | async-start | bytes 1048576 | tf_op jit(solution)/shard_map/all_to_all | solution.py:463
  80.1 9.4 %collective-permute-start.3 = (bf16[128,768]{1,0:T(8,128)(2,1)}, bf16[128,768]{1,0:T(8,128)(2,1)S(1)}, u32[]{:S(2)}, u32[]{:S(2)}) collective-permute-start(bf16[128,768]{1,0:T(8,128)(2,1)} %get-tuple-element.82), channel_id=1, source_target_pairs={{0,1},{1,0},{2,3},{3,2},{4,5},{5,4},{6,7},{7,6},{8,9},{9,8},{10,11... | collective-permute-start | bytes 589832 | tf_op jit(solution)/shard_map/ppermute | solution.py:469
  83.3 8.0 %collective-permute-start.4 = (bf16[128,768]{1,0:T(8,128)(2,1)}, bf16[128,768]{1,0:T(8,128)(2,1)S(1)}, u32[]{:S(2)}, u32[]{:S(2)}) collective-permute-start(bf16[128,768]{1,0:T(8,128)(2,1)} %get-tuple-element.83), channel_id=1, source_target_pairs={{0,2},{1,3},{2,4},{3,5},{4,6},{5,7},{6,0},{7,1},{8,10},{9,11},{10,... | collective-permute-start | bytes 589832 | tf_op jit(solution)/shard_map/ppermute | solution.py:469
  84.6 25.2 %collective-permute-start.5 = (bf16[128,768]{1,0:T(8,128)(2,1)}, bf16[128,768]{1,0:T(8,128)(2,1)S(1)}, u32[]{:S(2)}, u32[]{:S(2)}) collective-permute-start(bf16[128,768]{1,0:T(8,128)(2,1)} %get-tuple-element.84), channel_id=1, source_target_pairs={{0,3},{1,2},{2,5},{3,4},{4,7},{5,6},{6,1},{7,0},{8,11},{9,10},{10,... | collective-permute-start | bytes 589832 | tf_op jit(solution)/shard_map/ppermute | solution.py:469
  86.1 23.7 %collective-permute-start.6 = (bf16[128,768]{1,0:T(8,128)(2,1)}, bf16[128,768]{1,0:T(8,128)(2,1)S(1)}, u32[]{:S(2)}, u32[]{:S(2)}) collective-permute-start(bf16[128,768]{1,0:T(8,128)(2,1)} %get-tuple-element.85), channel_id=1, source_target_pairs={{0,4},{1,5},{2,6},{3,7},{4,0},{5,1},{6,2},{7,3},{8,12},{9,13},{10,... | collective-permute-start | bytes 589832 | tf_op jit(solution)/shard_map/ppermute | solution.py:469
  87.4 22.4 %collective-permute-start.7 = (bf16[128,768]{1,0:T(8,128)(2,1)}, bf16[128,768]{1,0:T(8,128)(2,1)S(1)}, u32[]{:S(2)}, u32[]{:S(2)}) collective-permute-start(bf16[128,768]{1,0:T(8,128)(2,1)} %get-tuple-element.86), channel_id=1, source_target_pairs={{0,5},{1,4},{2,7},{3,6},{4,1},{5,0},{6,3},{7,2},{8,13},{9,12},{10,... | collective-permute-start | bytes 589832 | tf_op jit(solution)/shard_map/ppermute | solution.py:469
  89.5 34.0 %copy-start.2 = (bf16[128,768]{1,0:T(8,128)(2,1)}, bf16[128,768]{1,0:T(8,128)(2,1)S(1)}, u32[]{:S(2)}) copy-start(bf16[128,768]{1,0:T(8,128)(2,1)S(1)} %collective-permute-done.3.refs_1_) | copy-start | bytes 589828
  89.5 20.4 %collective-permute-start.8 = (bf16[128,768]{1,0:T(8,128)(2,1)}, bf16[128,768]{1,0:T(8,128)(2,1)S(1)}, u32[]{:S(2)}, u32[]{:S(2)}) collective-permute-start(bf16[128,768]{1,0:T(8,128)(2,1)} %get-tuple-element.87), channel_id=1, source_target_pairs={{0,6},{1,7},{2,0},{3,1},{4,2},{5,3},{6,4},{7,5},{8,14},{9,15},{10,... | collective-permute-start | bytes 589832 | tf_op jit(solution)/shard_map/ppermute | solution.py:469
  91.3 32.2 %copy-start.3 = (bf16[128,768]{1,0:T(8,128)(2,1)}, bf16[128,768]{1,0:T(8,128)(2,1)S(1)}, u32[]{:S(2)}) copy-start(bf16[128,768]{1,0:T(8,128)(2,1)S(1)} %collective-permute-done.4.refs_2_) | copy-start | bytes 589828
  91.3 18.6 %collective-permute-start.9 = (bf16[128,768]{1,0:T(8,128)(2,1)}, bf16[128,768]{1,0:T(8,128)(2,1)S(1)}, u32[]{:S(2)}, u32[]{:S(2)}) collective-permute-start(bf16[128,768]{1,0:T(8,128)(2,1)} %get-tuple-element.88), channel_id=1, source_target_pairs={{0,7},{1,6},{2,1},{3,0},{4,3},{5,2},{6,5},{7,4},{8,15},{9,14},{10,... | collective-permute-start | bytes 589832 | tf_op jit(solution)/shard_map/ppermute | solution.py:469
  93.9 0.8 copy-start.1
  102.5 16.5 %all-to-all-start.2 = ((f32[16,16,128]{2,1,0:T(8,128)}), f32[16,16,128]{2,1,0:T(8,128)S(1)}, u32[]{:S(2)}, u32[]{:S(2)}) async-start(f32[16,16,128]{2,1,0:T(8,128)} %get-tuple-element.90), calls=%async_computation.2 | async-start | bytes 262144 | tf_op jit(solution)/shard_map/all_to_all | solution.py:440
  109.8 13.7 %copy-start.4 = (bf16[128,768]{1,0:T(8,128)(2,1)}, bf16[128,768]{1,0:T(8,128)(2,1)S(1)}, u32[]{:S(2)}) copy-start(bf16[128,768]{1,0:T(8,128)(2,1)S(1)} %collective-permute-done.5.refs_3_) | copy-start | bytes 589828
  109.8 13.7 %copy-start.5 = (bf16[128,768]{1,0:T(8,128)(2,1)}, bf16[128,768]{1,0:T(8,128)(2,1)S(1)}, u32[]{:S(2)}) copy-start(bf16[128,768]{1,0:T(8,128)(2,1)S(1)} %collective-permute-done.6.refs_4_) | copy-start | bytes 589828
  109.8 13.7 %copy-start.6 = (bf16[128,768]{1,0:T(8,128)(2,1)}, bf16[128,768]{1,0:T(8,128)(2,1)S(1)}, u32[]{:S(2)}) copy-start(bf16[128,768]{1,0:T(8,128)(2,1)S(1)} %collective-permute-done.7.refs_5_) | copy-start | bytes 589828
  109.9 13.7 %copy-start.7 = (bf16[128,768]{1,0:T(8,128)(2,1)}, bf16[128,768]{1,0:T(8,128)(2,1)S(1)}, u32[]{:S(2)}) copy-start(bf16[128,768]{1,0:T(8,128)(2,1)S(1)} %collective-permute-done.8.refs_6_) | copy-start | bytes 589828
  109.9 13.7 %copy-start.8 = (bf16[128,768]{1,0:T(8,128)(2,1)}, bf16[128,768]{1,0:T(8,128)(2,1)S(1)}, u32[]{:S(2)}) copy-start(bf16[128,768]{1,0:T(8,128)(2,1)S(1)} %collective-permute-done.9.refs_7_) | copy-start | bytes 589828
  109.9 4.6 %collective-permute-start.10 = (bf16[128,512]{1,0:T(8,128)(2,1)}, bf16[128,512]{1,0:T(8,128)(2,1)S(1)}, u32[]{:S(2)}, u32[]{:S(2)}) collective-permute-start(bf16[128,512]{1,0:T(8,128)(2,1)} %get-tuple-element.91), channel_id=1, source_target_pairs={{0,1},{1,0},{2,3},{3,2},{4,5},{5,4},{6,7},{7,6},{8,9},{9,8},{10,11... | collective-permute-start | bytes 393224 | tf_op jit(solution)/shard_map/ppermute | solution.py:469
  110.1 6.5 %collective-permute-start.11 = (bf16[128,512]{1,0:T(8,128)(2,1)}, bf16[128,512]{1,0:T(8,128)(2,1)S(1)}, u32[]{:S(2)}, u32[]{:S(2)}) collective-permute-start(bf16[128,512]{1,0:T(8,128)(2,1)} %get-tuple-element.93), channel_id=1, source_target_pairs={{0,2},{1,3},{2,4},{3,5},{4,6},{5,7},{6,0},{7,1},{8,10},{9,11},{10,... | collective-permute-start | bytes 393224 | tf_op jit(solution)/shard_map/ppermute | solution.py:469
  110.1 16.0 %collective-permute-start.12 = (bf16[128,512]{1,0:T(8,128)(2,1)}, bf16[128,512]{1,0:T(8,128)(2,1)S(1)}, u32[]{:S(2)}, u32[]{:S(2)}) collective-permute-start(bf16[128,512]{1,0:T(8,128)(2,1)} %get-tuple-element.94), channel_id=1, source_target_pairs={{0,3},{1,2},{2,5},{3,4},{4,7},{5,6},{6,1},{7,0},{8,11},{9,10},{10,... | collective-permute-start | bytes 393224 | tf_op jit(solution)/shard_map/ppermute | solution.py:469
  110.7 15.4 %collective-permute-start.13 = (bf16[128,512]{1,0:T(8,128)(2,1)}, bf16[128,512]{1,0:T(8,128)(2,1)S(1)}, u32[]{:S(2)}, u32[]{:S(2)}) collective-permute-start(bf16[128,512]{1,0:T(8,128)(2,1)} %get-tuple-element.95), channel_id=1, source_target_pairs={{0,4},{1,5},{2,6},{3,7},{4,0},{5,1},{6,2},{7,3},{8,12},{9,13},{10,... | collective-permute-start | bytes 393224 | tf_op jit(solution)/shard_map/ppermute | solution.py:469
  114.5 11.6 %collective-permute-start.14 = (bf16[128,512]{1,0:T(8,128)(2,1)}, bf16[128,512]{1,0:T(8,128)(2,1)S(1)}, u32[]{:S(2)}, u32[]{:S(2)}) collective-permute-start(bf16[128,512]{1,0:T(8,128)(2,1)} %get-tuple-element.96), channel_id=1, source_target_pairs={{0,5},{1,4},{2,7},{3,6},{4,1},{5,0},{6,3},{7,2},{8,13},{9,12},{10,... | collective-permute-start | bytes 393224 | tf_op jit(solution)/shard_map/ppermute | solution.py:469
  114.5 11.9 %copy-start.9 = (bf16[128,512]{1,0:T(8,128)(2,1)}, bf16[128,512]{1,0:T(8,128)(2,1)S(1)}, u32[]{:S(2)}) copy-start(bf16[128,512]{1,0:T(8,128)(2,1)S(1)} %collective-permute-done.10.refs_1_) | copy-start | bytes 393220
  114.5 11.6 %collective-permute-start.15 = (bf16[128,512]{1,0:T(8,128)(2,1)}, bf16[128,512]{1,0:T(8,128)(2,1)S(1)}, u32[]{:S(2)}, u32[]{:S(2)}) collective-permute-start(bf16[128,512]{1,0:T(8,128)(2,1)} %get-tuple-element.97), channel_id=1, source_target_pairs={{0,6},{1,7},{2,0},{3,1},{4,2},{5,3},{6,4},{7,5},{8,14},{9,15},{10,... | collective-permute-start | bytes 393224 | tf_op jit(solution)/shard_map/ppermute | solution.py:469
  116.6 9.9 %copy-start.10 = (bf16[128,512]{1,0:T(8,128)(2,1)}, bf16[128,512]{1,0:T(8,128)(2,1)S(1)}, u32[]{:S(2)}) copy-start(bf16[128,512]{1,0:T(8,128)(2,1)S(1)} %collective-permute-done.11.refs_2_) | copy-start | bytes 393220
  116.6 9.9 %collective-permute-start.16 = (bf16[128,512]{1,0:T(8,128)(2,1)}, bf16[128,512]{1,0:T(8,128)(2,1)S(1)}, u32[]{:S(2)}, u32[]{:S(2)}) collective-permute-start(bf16[128,512]{1,0:T(8,128)(2,1)} %get-tuple-element.98), channel_id=1, source_target_pairs={{0,7},{1,6},{2,1},{3,0},{4,3},{5,2},{6,5},{7,4},{8,15},{9,14},{10,... | collective-permute-start | bytes 393224 | tf_op jit(solution)/shard_map/ppermute | solution.py:469
  119.6 11.1 %all-to-all-start.3 = ((f32[16,16,128]{2,1,0:T(8,128)}), f32[16,16,128]{2,1,0:T(8,128)S(1)}, u32[]{:S(2)}, u32[]{:S(2)}) async-start(f32[16,16,128]{2,1,0:T(8,128)} %broadcast_in_dim.3), calls=%async_computation.3 | async-start | bytes 262144 | tf_op jit(solution)/shard_map/all_to_all | solution.py:440
  126.1 0.7 copy-start.11
  126.1 0.7 copy-start.12
  126.1 0.7 copy-start.13
  126.1 0.7 copy-start.14
  126.5 0.7 copy-start.15

commit v5 on v4

--- a/solution.py
+++ b/solution.py
@@ -181,7 +181,7 @@
     dv[...] = jnp.zeros_like(dv)
     q_acc[...] = jnp.zeros_like(q_acc)
     if first:
-        wait_all(kv_in)
+        wait_all(kv_in + own_in)
         for at in range(0, SLOT, TILE):
             part = pl.ds(at, TILE)
             normed = (rms(rows(kv, 0, at, TILE))[0] * k_gain[...]).astype(BF)
@@ -189,7 +189,7 @@
             knt[:, part] = dot_t(eye, normed).astype(BF)
             vt[:, part] = dot_t(eye, rows(kv, 1, at, TILE)).astype(BF)
     else:
-        wait_all(kv_in[1:] + carry[:3])
+        wait_all(kv_in[1:] + carry[:3] + own_in)
     u_rel = lax.broadcasted_iota(jnp.int32, (TILE, TILE), 0)
     t_rel = lax.broadcasted_iota(jnp.int32, (1, TILE), 1)
 
@@ -203,7 +203,6 @@
         ]
 
     def one_head(h):
-        wait_all([own_wait(h), own_wait(heads + h)])
         for group in GROUPS:
             together(h, group)
         start_all(copies_out(h) + copies_out(heads + h))
@@ -288,10 +287,8 @@
         both = jnp.where(row == 0, q_row, jnp.where(row == 1, k_sum, 0.0))
         sums[...] = jnp.broadcast_to(both, sums.shape)
 
-    if heads == 1:
-        one_head(0)
-    else:
-        pl.loop(0, heads)(one_head)
+    for h in range(heads):
+        one_head(h)
     if last:
         finish()
     else:
@@ -463,12 +460,12 @@
             owned.append(lax.all_to_all(chunk, "z", 0, 0, tiled=True).reshape(seqs, *query.shape[1:2], -1))
         out, carry = attend_chunk(count, n == 0, last, *small, owned[0], owned[n], carry)
         if n > 0:
-            out, received[-1] = lax.optimization_barrier((out, received[-1]))
+            out, received[-1][2:] = lax.optimization_barrier((out, received[-1][2:]))
         got = [out[0]] * 8
         for r in (4, 5, 2, 3, 6, 7, 1):
             got[r] = lax.ppermute(out[r], HEAD, across(r))
         received.append(got)
-    sums, received[-1][1:2] = lax.optimization_barrier((total(carry[0], ("z", "c")), received[-1][1:2]))
+    sums = total(carry[0], ("z", "c"))
     sums = total(jnp.broadcast_to(sums, carry[0].shape), ("x", "y"))
     wide, narrow = shape((1, WIDTH, heads * head_devs * WIDTH)), shape((1, WIDTH, head_devs * WIDTH))
     outs, at = [], 0

time: 132 us -> 132 us (level)
  transfers between devices with their start and end apart: 21 -> 21, of which waited for: 8 -> 7; matrix products, arithmetic and copies ran while one was open for 1% -> 1% of each run, Pallas kernels for 22% -> 22%
where the time goes in v5:
time: 132 us; the launch traced here: 131 us
  starting transfers between devices  54 us (41%)
  waiting for transfers between devices  40.7 us (31%)
  Pallas kernels  32.1 us (24%)
  local copies, waits for them, and re-layouts  2.9 us (2%)
    pallas_call x7, Pallas kernels, call(): pl.pallas_call(kernel, out_shape=outs, in_specs=in_specs, out_specs=out_s...  32.1 us
    all_to_all x1, waiting for transfers between devices, per_device(): owned = [lax.all_to_all(chunks[0], DP, 0, 0, tiled=True)]  25.3 us
    ppermute x14, starting transfers between devices, per_device(): got[r] = lax.ppermute(out[r], HEAD, across(r))  22.3 us
    ppermute x3, waiting for transfers between devices, packed_chunk(): lax.ppermute(parts[k], 'x', shift[k])  13 us
    all_to_all x1, starting transfers between devices, per_device(): owned = [lax.all_to_all(chunks[0], DP, 0, 0, tiled=True)]  11.9 us
    all_to_all x2, starting transfers between devices, total(): return jnp.sum(lax.all_to_all(spread, axis, 0, 0, tiled=True), axis=0)  11.4 us
    ppermute x3, starting transfers between devices, packed_chunk(): lax.ppermute(parts[k], 'x', shift[k])  4.88 us
    all_to_all x1, starting transfers between devices, per_device(): lax.all_to_all(chunk, 'z', 0, 0, tiled=True)  3.49 us
  transfers between devices with their start and end apart: 21, of which 7 were waited for; matrix products, arithmetic and copies ran while one was open for 1% of the time, Pallas kernels for 22%

profile of v5, /device:TPU:1, one launch (start us, length us, event | category | flops | bytes accessed | tf_op | source)
XLA Modules:
  0.0 131.2 jit_solution(3278025079577433216)
XLA Ops:
  0.6 3.2 %pack.2 = bf16[32,32,1024]{2,1,0:T(8,128)(2,1)} custom-call(s32[32]{0:T(128)} %refs_0_.7, bf16[32,32,512]{2,1,0:T(8,128)(2,1)} %refs_0_.5, bf16[32,32,512]{2,1,0:T(8,128)(2,1)} %refs_1_.5, bf16[32,32,128]{2,1,0:T(8,128)(2,1)} %refs_2_.3, bf16[32,32,128]{2,1,0:T(8,128)(2,1)} %refs_3_.1), custom_call_target="tpu_custom_call" | custom-call | bytes 4718720 | tf_op jit(solution)/shard_map/pack/pallas_call | solution.py:342
  3.9 11.9 %all-to-all-start = ((bf16[32,32,1024]{2,1,0:T(8,128)(2,1)}), bf16[32,32,1024]{2,1,0:T(8,128)(2,1)S(1)}, u32[]{:S(2)}, u32[]{:S(2)}) async-start(bf16[32,32,1024]{2,1,0:T(8,128)(2,1)} %pack.2), calls=%async_computation | async-start | bytes 4194304 | tf_op jit(solution)/shard_map/all_to_all | solution.py:454
  15.7 2.6 %pack.3 = (bf16[8,32,256]{2,1,0:T(8,128)(2,1)}, bf16[8,32,256]{2,1,0:T(8,128)(2,1)}, bf16[8,32,256]{2,1,0:T(8,128)(2,1)}, bf16[8,32,256]{2,1,0:T(8,128)(2,1)}) custom-call(s32[32]{0:T(128)} %refs_0_.7, bf16[32,32,512]{2,1,0:T(8,128)(2,1)} %refs_0_.5, bf16[32,32,512]{2,1,0:T(8,128)(2,1)} %refs_1_.5), custom_call_target="tpu_custom_call" | custom-call | bytes 2621568 | tf_op jit(solution)/shard_map/pack/pallas_call | solution.py:342
  18.4 1.3 collective-permute-start
  19.7 2.4 %collective-permute-start.1 = (bf16[8,32,256]{2,1,0:T(8,128)(2,1)}, bf16[8,32,256]{2,1,0:T(8,128)(2,1)S(1)}, u32[]{:S(2)}, u32[]{:S(2)}) collective-permute-start(bf16[8,32,256]{2,1,0:T(8,128)(2,1)} %get-tuple-element.59), channel_id=1, source_target_pairs={{0,16},{8,24},{16,0},{24,8},{1,17},{9,25},{17,1},{25,9},{2,18},{10... | collective-permute-start | bytes 393224 | tf_op jit(solution)/shard_map/ppermute | solution.py:423
  22.1 1.2 collective-permute-start.2
  23.2 2.8 %collective-permute-done.refs_1_ = bf16[8,32,256]{2,1,0:T(8,128)(2,1)S(1)} collective-permute-done((bf16[8,32,256]{2,1,0:T(8,128)(2,1)}, bf16[8,32,256]{2,1,0:T(8,128)(2,1)S(1)}, u32[]{:S(2)}, u32[]{:S(2)}) %collective-permute-start) | collective-permute-done | bytes 131104 | tf_op jit(solution)/shard_map/ppermute | solution.py:423
  26.0 3.6 %collective-permute-done.1.refs_2_ = bf16[8,32,256]{2,1,0:T(8,128)(2,1)S(1)} collective-permute-done((bf16[8,32,256]{2,1,0:T(8,128)(2,1)}, bf16[8,32,256]{2,1,0:T(8,128)(2,1)S(1)}, u32[]{:S(2)}, u32[]{:S(2)}) %collective-permute-start.1) | collective-permute-done | bytes 131104 | tf_op jit(solution)/shard_map/ppermute | solution.py:423
  29.7 6.6 %collective-permute-done.2.refs_3_ = bf16[8,32,256]{2,1,0:T(8,128)(2,1)S(1)} collective-permute-done((bf16[8,32,256]{2,1,0:T(8,128)(2,1)}, bf16[8,32,256]{2,1,0:T(8,128)(2,1)S(1)}, u32[]{:S(2)}, u32[]{:S(2)}) %collective-permute-start.2) | collective-permute-done | bytes 131104 | tf_op jit(solution)/shard_map/ppermute | solution.py:423
  36.3 0.0 copy-done.16
  36.3 0.0 copy-done.17
  36.3 0.6 copy-done.18
  36.9 1.9 %regroup.1 = bf16[8,4,32,256]{3,2,1,0:T(8,128)(2,1)} custom-call(bf16[8,32,256]{2,1,0:T(8,128)(2,1)} %get-tuple-element.57.refs_0_, bf16[8,32,256]{2,1,0:T(8,128)(2,1)} %copy-done.16, bf16[8,32,256]{2,1,0:T(8,128)(2,1)} %copy-done.17, bf16[8,32,256]{2,1,0:T(8,128)(2,1)} %copy-done.18), custom_call_target="tpu_custom_call" | custom-call | bytes 1048576 | tf_op jit(solution)/shard_map/regroup/pallas_call | solution.py:342
  38.9 25.3 %all-to-all-done.refs_5_ = bf16[32,32,1024]{2,1,0:T(8,128)(2,1)S(1)} async-done(((bf16[32,32,1024]{2,1,0:T(8,128)(2,1)}), bf16[32,32,1024]{2,1,0:T(8,128)(2,1)S(1)}, u32[]{:S(2)}, u32[]{:S(2)}) %all-to-all-start) | async-done | bytes 2097184 | tf_op jit(solution)/shard_map/all_to_all | solution.py:454
  64.2 3.5 %all-to-all-start.1 = ((bf16[8,4,32,256]{3,2,1,0:T(8,128)(2,1)}), bf16[8,4,32,256]{3,2,1,0:T(8,128)(2,1)S(1)}, u32[]{:S(2)}, u32[]{:S(2)}) async-start(bf16[8,4,32,256]{3,2,1,0:T(8,128)(2,1)} %regroup.1), calls=%async_computation.1 | async-start | bytes 1048576 | tf_op jit(solution)/shard_map/all_to_all | solution.py:460
  67.7 0.0 copy-done
  67.7 11.8 %attend.2 = (bf16[128,768]{1,0:T(8,128)(2,1)}, bf16[128,768]{1,0:T(8,128)(2,1)}, bf16[128,768]{1,0:T(8,128)(2,1)}, bf16[128,768]{1,0:T(8,128)(2,1)}, bf16[128,76...) custom-call(s32[32]{0:T(128)} %refs_0_.7, ...), custom_call_target="tpu_custom_call" | custom-call | flops 2717908992 | bytes 5768448 | tf_op jit(solution)/shard_map/attend/pallas_call | solution.py:342
  79.5 1.6 %collective-permute-start.3 = (bf16[128,768]{1,0:T(8,128)(2,1)}, bf16[128,768]{1,0:T(8,128)(2,1)S(1)}, u32[]{:S(2)}, u32[]{:S(2)}) collective-permute-start(bf16[128,768]{1,0:T(8,128)(2,1)} %get-tuple-element.77), channel_id=1, source_target_pairs={{0,2},{1,3},{2,4},{3,5},{4,6},{5,7},{6,0},{7,1},{8,10},{9,11},{10,... | collective-permute-start | bytes 589832 | tf_op jit(solution)/shard_map/ppermute | solution.py:466
  81.1 4.6 %collective-permute-start.4 = (bf16[128,768]{1,0:T(8,128)(2,1)}, bf16[128,768]{1,0:T(8,128)(2,1)S(1)}, u32[]{:S(2)}, u32[]{:S(2)}) collective-permute-start(bf16[128,768]{1,0:T(8,128)(2,1)} %get-tuple-element.78), channel_id=1, source_target_pairs={{0,3},{1,2},{2,5},{3,4},{4,7},{5,6},{6,1},{7,0},{8,11},{9,10},{10,... | collective-permute-start | bytes 589832 | tf_op jit(solution)/shard_map/ppermute | solution.py:466
  85.7 1.3 collective-permute-start.5
  86.9 0.7 collective-permute-start.6
  87.6 1.4 %collective-permute-start.7 = (bf16[128,768]{1,0:T(8,128)(2,1)}, bf16[128,768]{1,0:T(8,128)(2,1)S(1)}, u32[]{:S(2)}, u32[]{:S(2)}) collective-permute-start(bf16[128,768]{1,0:T(8,128)(2,1)} %get-tuple-element.81), channel_id=1, source_target_pairs={{0,6},{1,7},{2,0},{3,1},{4,2},{5,3},{6,4},{7,5},{8,14},{9,15},{10,... | collective-permute-start | bytes 589832 | tf_op jit(solution)/shard_map/ppermute | solution.py:466
  89.1 0.0 collective-permute-done.3.refs_2_
  89.1 4.3 %collective-permute-start.8 = (bf16[128,768]{1,0:T(8,128)(2,1)}, bf16[128,768]{1,0:T(8,128)(2,1)S(1)}, u32[]{:S(2)}, u32[]{:S(2)}) collective-permute-start(bf16[128,768]{1,0:T(8,128)(2,1)} %get-tuple-element.82), channel_id=1, source_target_pairs={{0,7},{1,6},{2,1},{3,0},{4,3},{5,2},{6,5},{7,4},{8,15},{9,14},{10,... | collective-permute-start | bytes 589832 | tf_op jit(solution)/shard_map/ppermute | solution.py:466
  93.4 0.0 all-to-all-done.1
  93.4 0.8 copy-done.1
  94.2 7.8 %attend.3 = (bf16[128,512]{1,0:T(8,128)(2,1)}, bf16[128,512]{1,0:T(8,128)(2,1)}, bf16[128,512]{1,0:T(8,128)(2,1)}, bf16[128,512]{1,0:T(8,128)(2,1)}, bf16[128,51...) custom-call(s32[32]{0:T(128)} %refs_0_.7, ...), custom_call_target="tpu_custom_call" | custom-call | flops 905969664 | bytes 5899520 | tf_op jit(solution)/shard_map/attend/pallas_call | solution.py:342
  102.0 7.4 %all-to-all-start.2 = ((f32[16,16,128]{2,1,0:T(8,128)}), f32[16,16,128]{2,1,0:T(8,128)S(1)}, u32[]{:S(2)}, u32[]{:S(2)}) async-start(f32[16,16,128]{2,1,0:T(8,128)} %get-tuple-element.107), calls=%async_computation.2 | async-start | bytes 262144 | tf_op jit(solution)/shard_map/all_to_all | solution.py:437
  109.4 0.0 collective-permute-done.4.refs_3_
  109.4 0.0 copy-start.3
  109.4 0.2 collective-permute-start.16
  109.6 0.0 collective-permute-done.5.refs_4_
  109.6 0.0 collective-permute-done.6.refs_5_
  109.7 0.0 collective-permute-done.7.refs_6_
  109.7 0.0 copy-start.6
  109.7 0.0 collective-permute-done.8.refs_7_
  109.7 0.5 collective-permute-start.9
  110.2 0.0 collective-permute-start.10
  110.2 0.0 collective-permute-start.11
  110.2 4.1 %collective-permute-start.12 = (bf16[128,512]{1,0:T(8,128)(2,1)}, bf16[128,512]{1,0:T(8,128)(2,1)S(1)}, u32[]{:S(2)}, u32[]{:S(2)}) collective-permute-start(bf16[128,512]{1,0:T(8,128)(2,1)} %get-tuple-element.87), channel_id=1, source_target_pairs={{0,4},{1,5},{2,6},{3,7},{4,0},{5,1},{6,2},{7,3},{8,12},{9,13},{10,... | collective-permute-start | bytes 393224 | tf_op jit(solution)/shard_map/ppermute | solution.py:466
  114.3 0.0 collective-permute-done.16.refs_1_
  114.3 0.1 collective-permute-start.13
  114.5 0.0 collective-permute-done.9.refs_1_
  114.5 2.0 %collective-permute-start.14 = (bf16[128,512]{1,0:T(8,128)(2,1)}, bf16[128,512]{1,0:T(8,128)(2,1)S(1)}, u32[]{:S(2)}, u32[]{:S(2)}) collective-permute-start(bf16[128,512]{1,0:T(8,128)(2,1)} %get-tuple-element.89), channel_id=1, source_target_pairs={{0,6},{1,7},{2,0},{3,1},{4,2},{5,3},{6,4},{7,5},{8,14},{9,15},{10,... | collective-permute-start | bytes 393224 | tf_op jit(solution)/shard_map/ppermute | solution.py:466
  116.5 0.2 collective-permute-done.10.refs_2_
  116.7 1.5 %collective-permute-start.15 = (bf16[128,512]{1,0:T(8,128)(2,1)}, bf16[128,512]{1,0:T(8,128)(2,1)S(1)}, u32[]{:S(2)}, u32[]{:S(2)}) collective-permute-start(bf16[128,512]{1,0:T(8,128)(2,1)} %get-tuple-element.90), channel_id=1, source_target_pairs={{0,7},{1,6},{2,1},{3,0},{4,3},{5,2},{6,5},{7,4},{8,15},{9,14},{10,... | collective-permute-start | bytes 393224 | tf_op jit(solution)/shard_map/ppermute | solution.py:466
  118.2 0.4 all-to-all-done.2
  118.6 0.7 broadcast_in_dim.3
  119.3 4.0 %all-to-all-start.3 = ((f32[16,16,128]{2,1,0:T(8,128)}), f32[16,16,128]{2,1,0:T(8,128)S(1)}, u32[]{:S(2)}, u32[]{:S(2)}) async-start(f32[16,16,128]{2,1,0:T(8,128)} %broadcast_in_dim.3), calls=%async_computation.3 | async-start | bytes 262144 | tf_op jit(solution)/shard_map/all_to_all | solution.py:437
  123.4 2.5 %place.2 = (bf16[1,128,4096]{2,1,0:T(8,128)(2,1)}, bf16[1,128,4096]{2,1,0:T(8,128)(2,1)}, bf16[1,128,1024]{2,1,0:T(8,128)(2,1)}, bf16[1,128,1024]{2,1,0:T(8,128)(2,1)}) custom-call(bf16[128,768]{1,0:T(8,128)(2,1)} %get-tuple-element.91.refs_0_, bf16[128,768]{1,0:T(8,128)(2,1)} %copy-done.8, bf16[128,768]{1,0:T(8,128)(2,1)} %copy-done.2, ...), custom_call_target="tpu_custom_call" | custom-call | bytes 4194304 | tf_op jit(solution)/shard_map/place/pallas_call | solution.py:342
  125.9 0.0 collective-permute-done.11.refs_3_
  125.9 0.0 copy-start.11
  125.9 0.0 collective-permute-done.12.refs_4_
  125.9 0.0 collective-permute-done.13.refs_5_
  126.0 0.0 collective-permute-done.14.refs_6_
  126.0 0.0 collective-permute-done.15.refs_7_
  126.0 0.5 copy-done.11
  126.5 0.1 copy-done.12
  126.6 0.1 copy-done.13
  126.7 0.0 copy-done.14
  126.7 0.1 copy-done.15
  126.7 2.3 %place.3 = (bf16[1,128,4096]{2,1,0:T(8,128)(2,1)}, bf16[1,128,4096]{2,1,0:T(8,128)(2,1)}, bf16[1,128,1024]{2,1,0:T(8,128)(2,1)}, bf16[1,128,1024]{2,1,0:T(8,128)(2,1)}) custom-call(bf16[128,512]{1,0:T(8,128)(2,1)} %get-tuple-element.83.refs_0_, ...), custom_call_target="tpu_custom_call", output_to_operand_aliasing={{0}: (8, {}), {1}: (9, {}), {2}: (10, {}), {3}: (11, {})} | custom-call | bytes 6291456 | tf_op jit(solution)/shard_map/place/pallas_call | solution.py:342
  129.0 1.7 %all-to-all-done.3 = f32[16,16,128]{2,1,0:T(8,128)S(1)} async-done(((f32[16,16,128]{2,1,0:T(8,128)}), f32[16,16,128]{2,1,0:T(8,128)S(1)}, u32[]{:S(2)}, u32[]{:S(2)}) %all-to-all-start.3) | async-done | bytes 131104 | tf_op jit(solution)/shard_map/all_to_all | solution.py:437
  130.7 0.5 fusion
  (29 shorter events, 0.1 us)
Async XLA Ops:
  3.9 60.4 %all-to-all-start = ((bf16[32,32,1024]{2,1,0:T(8,128)(2,1)}), bf16[32,32,1024]{2,1,0:T(8,128)(2,1)S(1)}, u32[]{:S(2)}, u32[]{:S(2)}) async-start(bf16[32,32,1024]{2,1,0:T(8,128)(2,1)} %pack.2), calls=%async_computation | async-start | bytes 4194304 | tf_op jit(solution)/shard_map/all_to_all | solution.py:454
  18.4 7.7 %collective-permute-start = (bf16[8,32,256]{2,1,0:T(8,128)(2,1)}, bf16[8,32,256]{2,1,0:T(8,128)(2,1)S(1)}, u32[]{:S(2)}, u32[]{:S(2)}) collective-permute-start(bf16[8,32,256]{2,1,0:T(8,128)(2,1)} %get-tuple-element.58), channel_id=1, source_target_pairs={{0,8},{8,16},{16,24},{24,0},{1,9},{9,17},{17,25},{25,1},{2,10},{10... | collective-permute-start | bytes 393224 | tf_op jit(solution)/shard_map/ppermute | solution.py:423
  19.7 10.0 %collective-permute-start.1 = (bf16[8,32,256]{2,1,0:T(8,128)(2,1)}, bf16[8,32,256]{2,1,0:T(8,128)(2,1)S(1)}, u32[]{:S(2)}, u32[]{:S(2)}) collective-permute-start(bf16[8,32,256]{2,1,0:T(8,128)(2,1)} %get-tuple-element.59), channel_id=1, source_target_pairs={{0,16},{8,24},{16,0},{24,8},{1,17},{9,25},{17,1},{25,9},{2,18},{10... | collective-permute-start | bytes 393224 | tf_op jit(solution)/shard_map/ppermute | solution.py:423
  22.1 14.2 %collective-permute-start.2 = (bf16[8,32,256]{2,1,0:T(8,128)(2,1)}, bf16[8,32,256]{2,1,0:T(8,128)(2,1)S(1)}, u32[]{:S(2)}, u32[]{:S(2)}) collective-permute-start(bf16[8,32,256]{2,1,0:T(8,128)(2,1)} %get-tuple-element.60), channel_id=1, source_target_pairs={{0,24},{8,0},{16,8},{24,16},{1,25},{9,1},{17,9},{25,17},{2,26},{10... | collective-permute-start | bytes 393224 | tf_op jit(solution)/shard_map/ppermute | solution.py:423
  26.0 10.3 %copy-start.16 = (bf16[8,32,256]{2,1,0:T(8,128)(2,1)}, bf16[8,32,256]{2,1,0:T(8,128)(2,1)S(1)}, u32[]{:S(2)}) copy-start(bf16[8,32,256]{2,1,0:T(8,128)(2,1)S(1)} %collective-permute-done.refs_1_) | copy-start | bytes 393220
  29.7 6.6 %copy-start.17 = (bf16[8,32,256]{2,1,0:T(8,128)(2,1)}, bf16[8,32,256]{2,1,0:T(8,128)(2,1)S(1)}, u32[]{:S(2)}) copy-start(bf16[8,32,256]{2,1,0:T(8,128)(2,1)S(1)} %collective-permute-done.1.refs_2_) | copy-start | bytes 393220
  36.3 0.7 copy-start.18
  64.2 3.5 %copy-start = (bf16[32,32,1024]{2,1,0:T(8,128)(2,1)}, bf16[32,32,1024]{2,1,0:T(8,128)(2,1)S(1)}, u32[]{:S(2)}) copy-start(bf16[32,32,1024]{2,1,0:T(8,128)(2,1)S(1)} %all-to-all-done.refs_5_) | copy-start | bytes 6291460
  64.2 29.2 %all-to-all-start.1 = ((bf16[8,4,32,256]{3,2,1,0:T(8,128)(2,1)}), bf16[8,4,32,256]{3,2,1,0:T(8,128)(2,1)S(1)}, u32[]{:S(2)}, u32[]{:S(2)}) async-start(bf16[8,4,32,256]{3,2,1,0:T(8,128)(2,1)} %regroup.1), calls=%async_computation.1 | async-start | bytes 1048576 | tf_op jit(solution)/shard_map/all_to_all | solution.py:460
  79.5 9.6 %collective-permute-start.3 = (bf16[128,768]{1,0:T(8,128)(2,1)}, bf16[128,768]{1,0:T(8,128)(2,1)S(1)}, u32[]{:S(2)}, u32[]{:S(2)}) collective-permute-start(bf16[128,768]{1,0:T(8,128)(2,1)} %get-tuple-element.77), channel_id=1, source_target_pairs={{0,2},{1,3},{2,4},{3,5},{4,6},{5,7},{6,0},{7,1},{8,10},{9,11},{10,... | collective-permute-start | bytes 589832 | tf_op jit(solution)/shard_map/ppermute | solution.py:466
  81.1 28.4 %collective-permute-start.4 = (bf16[128,768]{1,0:T(8,128)(2,1)}, bf16[128,768]{1,0:T(8,128)(2,1)S(1)}, u32[]{:S(2)}, u32[]{:S(2)}) collective-permute-start(bf16[128,768]{1,0:T(8,128)(2,1)} %get-tuple-element.78), channel_id=1, source_target_pairs={{0,3},{1,2},{2,5},{3,4},{4,7},{5,6},{6,1},{7,0},{8,11},{9,10},{10,... | collective-permute-start | bytes 589832 | tf_op jit(solution)/shard_map/ppermute | solution.py:466
  85.7 24.0 %collective-permute-start.5 = (bf16[128,768]{1,0:T(8,128)(2,1)}, bf16[128,768]{1,0:T(8,128)(2,1)S(1)}, u32[]{:S(2)}, u32[]{:S(2)}) collective-permute-start(bf16[128,768]{1,0:T(8,128)(2,1)} %get-tuple-element.79), channel_id=1, source_target_pairs={{0,4},{1,5},{2,6},{3,7},{4,0},{5,1},{6,2},{7,3},{8,12},{9,13},{10,... | collective-permute-start | bytes 589832 | tf_op jit(solution)/shard_map/ppermute | solution.py:466
  86.9 22.7 %collective-permute-start.6 = (bf16[128,768]{1,0:T(8,128)(2,1)}, bf16[128,768]{1,0:T(8,128)(2,1)S(1)}, u32[]{:S(2)}, u32[]{:S(2)}) collective-permute-start(bf16[128,768]{1,0:T(8,128)(2,1)} %get-tuple-element.80), channel_id=1, source_target_pairs={{0,5},{1,4},{2,7},{3,6},{4,1},{5,0},{6,3},{7,2},{8,13},{9,12},{10,... | collective-permute-start | bytes 589832 | tf_op jit(solution)/shard_map/ppermute | solution.py:466
  87.6 22.0 %collective-permute-start.7 = (bf16[128,768]{1,0:T(8,128)(2,1)}, bf16[128,768]{1,0:T(8,128)(2,1)S(1)}, u32[]{:S(2)}, u32[]{:S(2)}) collective-permute-start(bf16[128,768]{1,0:T(8,128)(2,1)} %get-tuple-element.81), channel_id=1, source_target_pairs={{0,6},{1,7},{2,0},{3,1},{4,2},{5,3},{6,4},{7,5},{8,14},{9,15},{10,... | collective-permute-start | bytes 589832 | tf_op jit(solution)/shard_map/ppermute | solution.py:466
  89.1 34.2 %copy-start.2 = (bf16[128,768]{1,0:T(8,128)(2,1)}, bf16[128,768]{1,0:T(8,128)(2,1)S(1)}, u32[]{:S(2)}) copy-start(bf16[128,768]{1,0:T(8,128)(2,1)S(1)} %collective-permute-done.3.refs_2_) | copy-start | bytes 589828
  89.1 20.6 %collective-permute-start.8 = (bf16[128,768]{1,0:T(8,128)(2,1)}, bf16[128,768]{1,0:T(8,128)(2,1)S(1)}, u32[]{:S(2)}, u32[]{:S(2)}) collective-permute-start(bf16[128,768]{1,0:T(8,128)(2,1)} %get-tuple-element.82), channel_id=1, source_target_pairs={{0,7},{1,6},{2,1},{3,0},{4,3},{5,2},{6,5},{7,4},{8,15},{9,14},{10,... | collective-permute-start | bytes 589832 | tf_op jit(solution)/shard_map/ppermute | solution.py:466
  93.4 0.8 copy-start.1
  94.2 15.2 %copy-start.19 = (bf16[128,768]{1,0:T(8,128)(2,1)S(1)}, bf16[128,768]{1,0:T(8,128)(2,1)}, u32[]{:S(2)}) copy-start(bf16[128,768]{1,0:T(8,128)(2,1)} %get-tuple-element.92) | copy-start | bytes 589828
  102.0 16.6 %all-to-all-start.2 = ((f32[16,16,128]{2,1,0:T(8,128)}), f32[16,16,128]{2,1,0:T(8,128)S(1)}, u32[]{:S(2)}, u32[]{:S(2)}) async-start(f32[16,16,128]{2,1,0:T(8,128)} %get-tuple-element.107), calls=%async_computation.2 | async-start | bytes 262144 | tf_op jit(solution)/shard_map/all_to_all | solution.py:437
  109.4 13.9 %copy-start.3 = (bf16[128,768]{1,0:T(8,128)(2,1)}, bf16[128,768]{1,0:T(8,128)(2,1)S(1)}, u32[]{:S(2)}) copy-start(bf16[128,768]{1,0:T(8,128)(2,1)S(1)} %collective-permute-done.4.refs_3_) | copy-start | bytes 589828
  109.4 4.9 %collective-permute-start.16 = (bf16[128,768]{1,0:T(8,128)(2,1)S(1)}, bf16[128,768]{1,0:T(8,128)(2,1)S(1)}, u32[]{:S(2)}, u32[]{:S(2)}) collective-permute-start(bf16[128,768]{1,0:T(8,128)(2,1)S(1)} %copy-done.19), channel_id=1, source_target_pairs={{0,1},{1,0},{2,3},{3,2},{4,5},{5,4},{6,7},{7,6},{8,9},{9,8},{10,11... | collective-permute-start | bytes 589832 | tf_op jit(solution)/shard_map/ppermute | solution.py:466
  109.6 13.7 %copy-start.4 = (bf16[128,768]{1,0:T(8,128)(2,1)}, bf16[128,768]{1,0:T(8,128)(2,1)S(1)}, u32[]{:S(2)}) copy-start(bf16[128,768]{1,0:T(8,128)(2,1)S(1)} %collective-permute-done.5.refs_4_) | copy-start | bytes 589828
  109.6 13.7 %copy-start.5 = (bf16[128,768]{1,0:T(8,128)(2,1)}, bf16[128,768]{1,0:T(8,128)(2,1)S(1)}, u32[]{:S(2)}) copy-start(bf16[128,768]{1,0:T(8,128)(2,1)S(1)} %collective-permute-done.6.refs_5_) | copy-start | bytes 589828
  109.7 13.7 %copy-start.6 = (bf16[128,768]{1,0:T(8,128)(2,1)}, bf16[128,768]{1,0:T(8,128)(2,1)S(1)}, u32[]{:S(2)}) copy-start(bf16[128,768]{1,0:T(8,128)(2,1)S(1)} %collective-permute-done.7.refs_6_) | copy-start | bytes 589828
  109.7 13.7 %copy-start.7 = (bf16[128,768]{1,0:T(8,128)(2,1)}, bf16[128,768]{1,0:T(8,128)(2,1)S(1)}, u32[]{:S(2)}) copy-start(bf16[128,768]{1,0:T(8,128)(2,1)S(1)} %collective-permute-done.8.refs_7_) | copy-start | bytes 589828
  109.7 4.8 %collective-permute-start.9 = (bf16[128,512]{1,0:T(8,128)(2,1)}, bf16[128,512]{1,0:T(8,128)(2,1)S(1)}, u32[]{:S(2)}, u32[]{:S(2)}) collective-permute-start(bf16[128,512]{1,0:T(8,128)(2,1)} %get-tuple-element.84), channel_id=1, source_target_pairs={{0,1},{1,0},{2,3},{3,2},{4,5},{5,4},{6,7},{7,6},{8,9},{9,8},{10,11... | collective-permute-start | bytes 393224 | tf_op jit(solution)/shard_map/ppermute | solution.py:466
  110.2 6.5 %collective-permute-start.10 = (bf16[128,512]{1,0:T(8,128)(2,1)}, bf16[128,512]{1,0:T(8,128)(2,1)S(1)}, u32[]{:S(2)}, u32[]{:S(2)}) collective-permute-start(bf16[128,512]{1,0:T(8,128)(2,1)} %get-tuple-element.85), channel_id=1, source_target_pairs={{0,2},{1,3},{2,4},{3,5},{4,6},{5,7},{6,0},{7,1},{8,10},{9,11},{10,... | collective-permute-start | bytes 393224 | tf_op jit(solution)/shard_map/ppermute | solution.py:466
  110.2 15.7 %collective-permute-start.11 = (bf16[128,512]{1,0:T(8,128)(2,1)}, bf16[128,512]{1,0:T(8,128)(2,1)S(1)}, u32[]{:S(2)}, u32[]{:S(2)}) collective-permute-start(bf16[128,512]{1,0:T(8,128)(2,1)} %get-tuple-element.86), channel_id=1, source_target_pairs={{0,3},{1,2},{2,5},{3,4},{4,7},{5,6},{6,1},{7,0},{8,11},{9,10},{10,... | collective-permute-start | bytes 393224 | tf_op jit(solution)/shard_map/ppermute | solution.py:466
  110.2 15.7 %collective-permute-start.12 = (bf16[128,512]{1,0:T(8,128)(2,1)}, bf16[128,512]{1,0:T(8,128)(2,1)S(1)}, u32[]{:S(2)}, u32[]{:S(2)}) collective-permute-start(bf16[128,512]{1,0:T(8,128)(2,1)} %get-tuple-element.87), channel_id=1, source_target_pairs={{0,4},{1,5},{2,6},{3,7},{4,0},{5,1},{6,2},{7,3},{8,12},{9,13},{10,... | collective-permute-start | bytes 393224 | tf_op jit(solution)/shard_map/ppermute | solution.py:466
  114.3 9.0 %copy-start.8 = (bf16[128,768]{1,0:T(8,128)(2,1)}, bf16[128,768]{1,0:T(8,128)(2,1)S(1)}, u32[]{:S(2)}) copy-start(bf16[128,768]{1,0:T(8,128)(2,1)S(1)} %collective-permute-done.16.refs_1_) | copy-start | bytes 589828
  114.3 11.6 %collective-permute-start.13 = (bf16[128,512]{1,0:T(8,128)(2,1)}, bf16[128,512]{1,0:T(8,128)(2,1)S(1)}, u32[]{:S(2)}, u32[]{:S(2)}) collective-permute-start(bf16[128,512]{1,0:T(8,128)(2,1)} %get-tuple-element.88), channel_id=1, source_target_pairs={{0,5},{1,4},{2,7},{3,6},{4,1},{5,0},{6,3},{7,2},{8,13},{9,12},{10,... | collective-permute-start | bytes 393224 | tf_op jit(solution)/shard_map/ppermute | solution.py:466
  114.5 11.5 %copy-start.9 = (bf16[128,512]{1,0:T(8,128)(2,1)}, bf16[128,512]{1,0:T(8,128)(2,1)S(1)}, u32[]{:S(2)}) copy-start(bf16[128,512]{1,0:T(8,128)(2,1)S(1)} %collective-permute-done.9.refs_1_) | copy-start | bytes 393220
  114.5 11.5 %collective-permute-start.14 = (bf16[128,512]{1,0:T(8,128)(2,1)}, bf16[128,512]{1,0:T(8,128)(2,1)S(1)}, u32[]{:S(2)}, u32[]{:S(2)}) collective-permute-start(bf16[128,512]{1,0:T(8,128)(2,1)} %get-tuple-element.89), channel_id=1, source_target_pairs={{0,6},{1,7},{2,0},{3,1},{4,2},{5,3},{6,4},{7,5},{8,14},{9,15},{10,... | collective-permute-start | bytes 393224 | tf_op jit(solution)/shard_map/ppermute | solution.py:466
  116.7 9.3 %copy-start.10 = (bf16[128,512]{1,0:T(8,128)(2,1)}, bf16[128,512]{1,0:T(8,128)(2,1)S(1)}, u32[]{:S(2)}) copy-start(bf16[128,512]{1,0:T(8,128)(2,1)S(1)} %collective-permute-done.10.refs_2_) | copy-start | bytes 393220
  116.7 9.3 %collective-permute-start.15 = (bf16[128,512]{1,0:T(8,128)(2,1)}, bf16[128,512]{1,0:T(8,128)(2,1)S(1)}, u32[]{:S(2)}, u32[]{:S(2)}) collective-permute-start(bf16[128,512]{1,0:T(8,128)(2,1)} %get-tuple-element.90), channel_id=1, source_target_pairs={{0,7},{1,6},{2,1},{3,0},{4,3},{5,2},{6,5},{7,4},{8,15},{9,14},{10,... | collective-permute-start | bytes 393224 | tf_op jit(solution)/shard_map/ppermute | solution.py:466
  119.3 11.4 %all-to-all-start.3 = ((f32[16,16,128]{2,1,0:T(8,128)}), f32[16,16,128]{2,1,0:T(8,128)S(1)}, u32[]{:S(2)}, u32[]{:S(2)}) async-start(f32[16,16,128]{2,1,0:T(8,128)} %broadcast_in_dim.3), calls=%async_computation.3 | async-start | bytes 262144 | tf_op jit(solution)/shard_map/all_to_all | solution.py:437
  125.9 0.6 copy-start.11
  125.9 0.7 copy-start.12
  125.9 0.7 copy-start.13
  126.0 0.7 copy-start.14
  126.0 0.8 copy-start.15
